TPU v7x, 512 devices: a whole 4x4x16 slice. The times are simulated.
512 devices in a mesh: seq: 32 (over y, z_hi, core), chan: 16 (over x, z_lo).
Axes of the slice: x: 4, y: 4, z: 16 (z_hi: 4, z_lo: 4; z = z_hi * 4 + z_lo), core: 2. Of those that a mesh axis runs over, the one named last changes fastest.
Arguments:
- tokens: int32 [8192], P('seq'), may hold values from 0 to 4
- complement: int32 [5], replicated, may hold values from 0 to 4, each once
- embed: bfloat16 [5, 2048], replicated, may hold values from -6 to 6
- w_x: bfloat16 [2048, 4096], P(None, 'chan'), may hold values from -0.125 to 0.125
- w_z: bfloat16 [2048, 4096], P(None, 'chan'), may hold values from -0.125 to 0.125
- w_bc: bfloat16 [2048, 256], P('chan'), may hold values from -0.125 to 0.125
- w_dt: bfloat16 [2048, 64], P(None, 'chan'), may hold values from -0.125 to 0.125
- dt_bias: float32 [64], P('chan'), may hold values from -1 to 1
- decay_rate: float32 [64], P('chan'), may hold values from 2.4414062e-06 to 0.05
- d_skip: float32 [64], P('chan'), may hold values from 0.5 to 1.5
- conv_x: bfloat16 [4, 4096], P(None, 'chan'), may hold values from -3 to 3
- conv_bc: bfloat16 [4, 256], replicated, may hold values from -3 to 3
- norm_gain: float32 [4096], P('chan'), may hold values from 0.1 to 1.9
- w_out: bfloat16 [4096, 2048], P('chan'), may hold values from -0.09375 to 0.09375
Outputs:
- mixed_out: bfloat16 [8192, 2048], P(('seq', 'chan'))
Inputs may be any that keep to these rules, and one draw needn't show every extreme that they name: `complement`: a permutation of the 5 token ids.
All inputs are finite; a program needn't handle non-finite values.
Results may differ from a plain program's by a relative error of at most 0.0073.
Values may be sent and summed in bfloat16 or wider, within the bound.
No kernel may reach another device: no remote copies, remote signals or barrier semaphores. Data moves between devices by JAX's collectives and lax.ppermute only.
A program may use at most 64 MiB of HBM per device.

v0:
```python
import jax
import jax.numpy as jnp
from jax import lax
from jax.sharding import PartitionSpec as P

HEADS = 64
HEAD_DIM = 64
STATE = 128
CONV = 4


EPSILON = 1e-05


def from_behind(value, axis, steps):
    count = lax.axis_size(axis)
    initial, last = (max(0, -steps), min(count, count - steps))
    return lax.ppermute(value, axis, [(source, source + steps) for source in range(initial, last)])


def carried_in(value, axis, join, neutral):
    count, mine = (lax.axis_size(axis), lax.axis_index(axis))
    pieces = jax.tree.map(lambda part: lax.all_gather(part, axis), value)
    total = jax.tree.map(
        lambda part, zero: jnp.full_like(part, 0) + jnp.asarray(zero, part.dtype), value, neutral
    )

    def lap(position, total):
        longer = join(total, jax.tree.map(lambda part: part[position], pieces))
        return jax.tree.map(lambda new, old: jnp.where(position < mine, new, old), longer, total)

    return lax.fori_loop(0, count - 1, lap, total)


def partner(value, axis, distance):
    mask = 2**distance
    pairs = [(source, source ^ mask) for source in range(lax.axis_size(axis))]
    return lax.ppermute(value, axis, pairs)


def embed_rows(ids, embed):
    onehot = (ids[:, None] == lax.iota(jnp.int32, embed.shape[0])[None, :]).astype(jnp.bfloat16)
    return jnp.dot(onehot, embed, preferred_element_type=jnp.float32).astype(jnp.bfloat16)


def complement_ids(ids, complement):
    hits = ids[:, None] == lax.iota(jnp.int32, complement.shape[0])[None, :]
    return jnp.sum(jnp.where(hits, complement[None, :], 0), axis=1)


def conv_silu(raw, rim, weight):
    count = raw.shape[0]
    padded = lax.optimization_barrier(jnp.concatenate([rim, raw], 0)).astype(jnp.float32)
    total = jnp.zeros((count, raw.shape[1]), jnp.float32)
    for offset in range(weight.shape[0]):
        total = total + padded[offset : offset + count] * weight[offset].astype(jnp.float32)
    return jax.nn.silu(total)


def local_scan(mixed, dt_raw, dt_bias, decay_rate, d_skip):
    count = mixed.shape[0]
    heads = decay_rate.shape[0]
    inner = heads * HEAD_DIM
    values = mixed[:, :inner].reshape(count, heads, HEAD_DIM)
    b_in = mixed[:, inner : inner + STATE]
    c_out = mixed[:, inner + STATE :]
    step = jax.nn.softplus(dt_raw + dt_bias[None, :])
    cumul = jnp.cumsum(-step * decay_rate[None, :], axis=0)
    cumt = cumul.T
    causal = (lax.iota(jnp.int32, count)[:, None] >= lax.iota(jnp.int32, count)[None, :])[
        None, :, :
    ]
    scores = jnp.dot(c_out, b_in.T, precision=lax.Precision.HIGHEST)
    spread = jnp.where(causal, cumt[:, :, None] - cumt[:, None, :], 0.0)
    weights = jnp.where(causal, jnp.exp(spread), 0.0) * scores[None, :, :] * step.T[:, None, :]
    within = jnp.einsum("hts,shp->thp", weights, values, precision=lax.Precision.HIGHEST)
    within = within + values * d_skip[None, :, None]
    last = cumul[-1]
    weighted = values * (jnp.exp(last[None, :] - cumul) * step)[:, :, None]
    summary = jnp.einsum("sn,shp->hnp", b_in, weighted, precision=lax.Precision.HIGHEST)
    return (within, cumul, c_out, jnp.exp(last), summary)


def finish(within, cumul, c_out, carried):
    inter = (
        jnp.einsum("tn,hnp->thp", c_out, carried, precision=lax.Precision.HIGHEST)
        * jnp.exp(cumul)[:, :, None]
    )
    return (within + inter).reshape(within.shape[0], -1)


def combine(earlier, later):
    return (earlier[0] * later[0], later[0][..., None, None] * earlier[1] + later[1])


def per_device(
    tokens,
    complement,
    embed,
    w_x,
    w_z,
    w_bc,
    w_dt,
    dt_bias,
    decay_rate,
    d_skip,
    conv_x,
    conv_bc,
    norm_gain,
    w_out,
):
    rows = tokens.shape[0]
    heads = decay_rate.shape[0]
    every_id = lax.all_gather(tokens, "seq", axis=0, tiled=True)
    mirrored = (lax.axis_size("seq") - 1 - lax.axis_index("seq")) * rows
    other = lax.dynamic_slice_in_dim(every_id, mirrored, rows, 0)
    back_ids = jnp.flip(complement_ids(other, complement), 0)
    both = jnp.concatenate([embed_rows(tokens, embed), embed_rows(back_ids, embed)], 0)
    x_raw = jnp.dot(both, w_x, preferred_element_type=jnp.float32).astype(jnp.bfloat16)
    z_gate = jnp.dot(both, w_z, preferred_element_type=jnp.float32).astype(jnp.bfloat16)
    dt_raw = jnp.dot(both, w_dt, preferred_element_type=jnp.float32)
    bc_sum = jnp.dot(
        both, lax.all_gather(w_bc, "chan", axis=0, tiled=True), preferred_element_type=jnp.float32
    )
    bc_raw = bc_sum.astype(jnp.bfloat16)
    conv_weight = jnp.concatenate([conv_x, conv_bc], 1)
    raw = jnp.concatenate([x_raw, bc_raw], 1)
    raw_fwd = raw[:rows]
    raw_back = raw[rows:]
    edge = CONV - 1
    rim_fwd, rim_back = from_behind((raw_fwd[rows - edge :], raw_back[rows - edge :]), "seq", 1)
    part_fwd = local_scan(
        conv_silu(raw_fwd, rim_fwd, conv_weight), dt_raw[:rows], dt_bias, decay_rate, d_skip
    )
    part_back = local_scan(
        conv_silu(raw_back, rim_back, conv_weight), dt_raw[rows:], dt_bias, decay_rate, d_skip
    )
    decays = jnp.stack([part_fwd[3], part_back[3]], 0)
    summaries = jnp.stack([part_fwd[4], part_back[4]], 0)
    neutral = (
        jnp.ones((2, heads), jnp.float32),
        jnp.zeros((2, heads, STATE, HEAD_DIM), jnp.float32),
    )
    carried = carried_in((decays, summaries), "seq", combine, neutral)[1]
    carry_fwd = carried[0]
    carry_back = carried[1]
    scanned = jnp.concatenate(
        [
            finish(part_fwd[0], part_fwd[1], part_fwd[2], carry_fwd),
            finish(part_back[0], part_back[1], part_back[2], carry_back),
        ],
        0,
    )
    gated = scanned * jax.nn.silu(lax.optimization_barrier(z_gate).astype(jnp.float32))
    squares = jnp.sum(gated * gated, axis=1).reshape(2, rows)
    totals = lax.psum(squares, "chan").reshape(2 * rows)
    scale = lax.rsqrt(totals / (HEADS * HEAD_DIM) + EPSILON)
    normed = (gated * scale[:, None] * norm_gain[None, :]).astype(jnp.bfloat16)
    back_rows = jnp.flip(normed[rows:], 0)
    for bit in range(lax.axis_size("seq").bit_length() - 1):
        back_rows = partner(back_rows, "seq", bit)
    combined = (normed[:rows].astype(jnp.float32) + back_rows.astype(jnp.float32)).astype(
        jnp.bfloat16
    )
    return lax.psum_scatter(
        jnp.dot(combined, w_out, preferred_element_type=jnp.float32),
        "chan",
        scatter_dimension=0,
        tiled=True,
    ).astype(jnp.bfloat16)


def solution(mesh):
    placed = (
        P("seq"),
        P(),
        P(),
        P(None, "chan"),
        P(None, "chan"),
        P("chan", None),
        P(None, "chan"),
        P("chan"),
        P("chan"),
        P("chan"),
        P(None, "chan"),
        P(),
        P("chan"),
        P("chan", None),
    )
    return jax.shard_map(
        per_device, mesh=mesh, in_specs=placed, out_specs=P(("seq", "chan"), None), check_vma=False
    )
```

profile of v0, /device:TPU:8, one launch (start us, length us, event | category | flops | bytes accessed | tf_op | source)
XLA Modules:
  0.0 503.5 jit_solution(12107104748296624150)
XLA Ops:
  7.3 55.3 %all-gather.2 = s32[32,1,256]{2,1,0:T(1,128)S(1)} all-gather(s32[1,1,256]{2,1,0:T(1,128)} %bitcast.136), channel_id=1, replica_groups=mesh['seq'=32,'chan'=16] {'seq'}, dimensions={0}, use_global_device_ids=true | all-gather | bytes 33792 | tf_op jit(solution)/shard_map/all_gather | solution.py:114
  70.6 2.0 convolution_convert_fusion.4
  72.6 28.8 %all-gather.7.cloned.1.call-done = bf16[2048,256]{1,0:T(8,128)(2,1)} async-done(((bf16[128,256]{1,0:T(8,128)(2,1)}), bf16[2048,256]{1,0:T(8,128)(2,1)}) %all-gather.7.cloned.1.call-update) | async-done | bytes 1048592 | tf_op jit(solution)/shard_map/all_gather | solution.py:123
  101.4 2.0 convolution_convert_fusion.3
  103.5 1.9 collective-permute-start
  105.5 7.3 %collective-permute-start.1 = (bf16[3,512]{0,1:T(8,128)(2,1)S(1)}, bf16[3,512]{0,1:T(8,128)(2,1)S(1)}, u32[]{:S(2)}, u32[]{:S(2)}) collective-permute-start(bf16[3,512]{0,1:T(8,128)(2,1)S(1)} %get-tuple-element.151), channel_id=1, source_target_pairs={{0,16},{16,32},{32,48},{48,64},{64,80},{80,96},{96,112},{112,128},... | collective-permute-start | bytes 9224 | tf_op jit(solution)/shard_map/ppermute | solution.py:18
  112.8 6.2 %collective-permute-done = bf16[3,512]{0,1:T(8,128)(2,1)S(1)} collective-permute-done((bf16[3,512]{0,1:T(8,128)(2,1)S(1)}, bf16[3,512]{0,1:T(8,128)(2,1)S(1)}, u32[]{:S(2)}, u32[]{:S(2)}) %collective-permute-start) | collective-permute-done | bytes 3104 | tf_op jit(solution)/shard_map/ppermute | solution.py:18
  123.9 3.3 convolution_convert_fusion.2
  127.3 51.0 %all-gather.3 = f32[32,2,4]{2,1,0:T(2,128)S(1)} all-gather(f32[1,2,4]{2,1,0:T(2,128)S(1)} %bitcast.139), channel_id=2, replica_groups=mesh['seq'=32,'chan'=16] {'seq'}, dimensions={0}, use_global_device_ids=true | all-gather | bytes 1056 | tf_op jit(solution)/shard_map/all_gather | solution.py:23
  180.7 77.5 %all-gather.9.cloned.1.call-done = f32[64,4,128,64]{2,3,1,0:T(8,128)} async-done(((f32[2,4,128,64]{2,3,1,0:T(8,128)}), f32[64,4,128,64]{2,3,1,0:T(8,128)}) %all-gather.9.cloned.1.call-update) | async-done | bytes 8388624 | tf_op jit(solution)/shard_map/all_gather | solution.py:23
  258.1 42.1 %while.14 = (s32[]{:T(128)}, f32[2,4,128,64]{3,2,1,0:T(8,128)S(1)}, s32[]{:T(128)}, f32[32,2,4]{2,1,0:T(2,128)S(1)}, f32[32,2,4,128,64]{3,4,2,1,0:T(8,128)}, /*index=5*/s32[]{:T(128)}, s32[]{:T(128)}) while((s32[]{:T(128)}, f32[2,4,128,64]{3,2,1,0:T(8,128)S(1)}, s32[]{:T(128)}, f32[32,2,4]{2,1,0:T(2,128)S(1)}, ...), condition=%wide.region_6.7_spmd.clone, body=%wide.region_5.6_spmd.clone.sunk | while | flops 262148 | bytes 1835217 | solution.py:32
  300.9 2.5 fusion.4
  305.7 38.0 %psum.7 = f32[2,256]{1,0:T(2,128)S(1)} all-reduce(f32[2,256]{1,0:T(2,128)S(1)} %reshape.127), channel_id=1, replica_groups=mesh['seq'=32,'chan'=16] {'chan'}, use_global_device_ids=true, to_apply=%region_8.9 | all-reduce | flops 512 | bytes 4096 | tf_op jit(solution)/shard_map/psum | solution.py:156
  344.1 1.9 collective-permute-start.2
  347.3 4.9 collective-permute-start.3
  352.2 11.8 %collective-permute-done.3 = bf16[256,256]{1,0:T(8,128)(2,1)S(1)} collective-permute-done((bf16[256,256]{1,0:T(8,128)(2,1)S(1)}, bf16[256,256]{1,0:T(8,128)(2,1)S(1)}, u32[]{:S(2)}, u32[]{:S(2)}) %collective-permute-start.3) | collective-permute-done | bytes 131104 | tf_op jit(solution)/shard_map/ppermute | solution.py:38
  364.0 7.0 %collective-permute-start.4 = (bf16[256,256]{1,0:T(8,128)(2,1)S(1)}, bf16[256,256]{1,0:T(8,128)(2,1)S(1)}, u32[]{:S(2)}, u32[]{:S(2)}) collective-permute-start(bf16[256,256]{1,0:T(8,128)(2,1)S(1)} %collective-permute-done.3), channel_id=1, source_target_pairs={{0,64},{16,80},{32,96},{48,112},{64,0},{80,16},{96,32},{112,48},{1... | collective-permute-start | bytes 393224 | tf_op jit(solution)/shard_map/ppermute | solution.py:38
  371.1 13.8 %collective-permute-done.4 = bf16[256,256]{1,0:T(8,128)(2,1)S(1)} collective-permute-done((bf16[256,256]{1,0:T(8,128)(2,1)S(1)}, bf16[256,256]{1,0:T(8,128)(2,1)S(1)}, u32[]{:S(2)}, u32[]{:S(2)}) %collective-permute-start.4) | collective-permute-done | bytes 131104 | tf_op jit(solution)/shard_map/ppermute | solution.py:38
  384.9 2.2 collective-permute-start.5
  387.1 5.1 %collective-permute-done.5 = bf16[256,256]{1,0:T(8,128)(2,1)S(1)} collective-permute-done((bf16[256,256]{1,0:T(8,128)(2,1)S(1)}, bf16[256,256]{1,0:T(8,128)(2,1)S(1)}, u32[]{:S(2)}, u32[]{:S(2)}) %collective-permute-start.5) | collective-permute-done | bytes 131104 | tf_op jit(solution)/shard_map/ppermute | solution.py:38
  392.2 4.0 collective-permute-start.6
  396.2 4.4 collective-permute-done.6
  400.6 1.8 fusion.46
  402.4 93.0 %reduce-scatter.2.cloned.1.call-done = f32[16,2048]{1,0:T(8,128)} async-done(((f32[256,2048]{1,0:T(8,128)}), f32[16,2048]{1,0:T(8,128)}) %reduce-scatter.2.cloned.1.call-update) | async-done | bytes 131088 | tf_op jit(solution)/shard_map/reduce_scatter | solution.py:165
  (225 shorter events, 62.9 us)
Async XLA Ops:
  6.5 394.0 %copy-start = (bf16[256,2048]{1,0:T(8,128)(2,1)S(1)}, bf16[256,2048]{1,0:T(8,128)(2,1)}, u32[]{:S(2)}) copy-start(bf16[256,2048]{1,0:T(8,128)(2,1)} %param.29) | copy-start | bytes 3145732
  6.5 59.6 %copy-start.13 = (bf16[2048,4]{0,1:T(4,128)(2,1)S(1)}, bf16[2048,4]{0,1:T(4,128)(2,1)}, u32[]{:S(2)}) copy-start(bf16[2048,4]{0,1:T(4,128)(2,1)} %param.22) | copy-start | bytes 49156
  6.5 94.9 %all-gather.7.cloned.1.call-start = ((), (), s32[]{:S(2)}) async-start(), calls=%async_computation.1 | async-start | bytes 1114112 | tf_op jit(solution)/shard_map/all_gather | solution.py:123
  7.3 250.9 %all-gather.9.cloned.1.call-start = ((), (), s32[]{:S(2)}) async-start(), calls=%async_computation.3 | async-start | bytes 8650752 | tf_op jit(solution)/shard_map/all_gather | solution.py:23
  64.8 36.6 %copy-start.1 = (bf16[256,2048]{1,0:T(8,128)(2,1)}, bf16[256,2048]{1,0:T(8,128)(2,1)S(1)}, u32[]{:S(2)}) copy-start(bf16[256,2048]{1,0:T(8,128)(2,1)S(1)} %convolution_convert_fusion.1) | copy-start | bytes 3145732
  64.8 2.0 copy-start.8
  64.8 2.0 copy-start.12
  66.1 35.3 %copy-start.2 = (bf16[256,2048]{1,0:T(8,128)(2,1)}, bf16[256,2048]{1,0:T(8,128)(2,1)S(1)}, u32[]{:S(2)}) copy-start(bf16[256,2048]{1,0:T(8,128)(2,1)S(1)} %convolution_convert_fusion) | copy-start | bytes 3145732
  66.1 4.0 copy-start.9
  66.2 4.0 copy-start.10
  103.5 15.5 %collective-permute-start = (bf16[3,512]{0,1:T(8,128)(2,1)S(1)}, bf16[3,512]{0,1:T(8,128)(2,1)S(1)}, u32[]{:S(2)}, u32[]{:S(2)}) collective-permute-start(bf16[3,512]{0,1:T(8,128)(2,1)S(1)} %get-tuple-element.150), channel_id=1, source_target_pairs={{0,16},{16,32},{32,48},{48,64},{64,80},{80,96},{96,112},{112,128},... | collective-permute-start | bytes 9224 | tf_op jit(solution)/shard_map/ppermute | solution.py:18
  105.5 14.9 %collective-permute-start.1 = (bf16[3,512]{0,1:T(8,128)(2,1)S(1)}, bf16[3,512]{0,1:T(8,128)(2,1)S(1)}, u32[]{:S(2)}, u32[]{:S(2)}) collective-permute-start(bf16[3,512]{0,1:T(8,128)(2,1)S(1)} %get-tuple-element.151), channel_id=1, source_target_pairs={{0,16},{16,32},{32,48},{48,64},{64,80},{80,96},{96,112},{112,128},... | collective-permute-start | bytes 9224 | tf_op jit(solution)/shard_map/ppermute | solution.py:18
  121.9 1.2 copy-start.5
  123.8 371.6 %reduce-scatter.2.cloned.1.call-start = ((), (), s32[]{:S(2)}) async-start(), calls=%async_computation.2 | async-start | bytes 2228224 | tf_op jit(solution)/shard_map/reduce_scatter | solution.py:165
  258.1 42.7 %copy-start.14 = (f32[4]{0:T(128)S(1)}, f32[4]{0:T(128)}, u32[]{:S(2)}) copy-start(f32[4]{0:T(128)} %param.25) | copy-start | bytes 52
  300.5 3.4 copy-start.4
  300.5 3.4 copy-start.7
  303.4 2.1 copy-start.6
  303.9 39.8 %copy-start.11 = (f32[256]{0:T(256)S(1)}, f32[256]{0:T(256)}, u32[]{:S(2)}) copy-start(f32[256]{0:T(256)} %param.28) | copy-start | bytes 3076
  344.1 3.2 collective-permute-start.2
  347.3 16.7 %collective-permute-start.3 = (bf16[256,256]{1,0:T(8,128)(2,1)S(1)}, bf16[256,256]{1,0:T(8,128)(2,1)S(1)}, u32[]{:S(2)}, u32[]{:S(2)}) collective-permute-start(bf16[256,256]{1,0:T(8,128)(2,1)S(1)} %collective-permute-done.2), channel_id=1, source_target_pairs={{0,32},{16,48},{32,0},{48,16},{64,96},{80,112},{96,64},{112,80},{1... | collective-permute-start | bytes 393224 | tf_op jit(solution)/shard_map/ppermute | solution.py:38
  364.0 20.9 %collective-permute-start.4 = (bf16[256,256]{1,0:T(8,128)(2,1)S(1)}, bf16[256,256]{1,0:T(8,128)(2,1)S(1)}, u32[]{:S(2)}, u32[]{:S(2)}) collective-permute-start(bf16[256,256]{1,0:T(8,128)(2,1)S(1)} %collective-permute-done.3), channel_id=1, source_target_pairs={{0,64},{16,80},{32,96},{48,112},{64,0},{80,16},{96,32},{112,48},{1... | collective-permute-start | bytes 393224 | tf_op jit(solution)/shard_map/ppermute | solution.py:38
  384.9 7.3 %collective-permute-start.5 = (bf16[256,256]{1,0:T(8,128)(2,1)S(1)}, bf16[256,256]{1,0:T(8,128)(2,1)S(1)}, u32[]{:S(2)}, u32[]{:S(2)}) collective-permute-start(bf16[256,256]{1,0:T(8,128)(2,1)S(1)} %collective-permute-done.4), channel_id=1, source_target_pairs={{0,128},{16,144},{32,160},{48,176},{64,192},{80,208},{96,224},{112... | collective-permute-start | bytes 393224 | tf_op jit(solution)/shard_map/ppermute | solution.py:38
  392.2 8.4 %collective-permute-start.6 = (bf16[256,256]{1,0:T(8,128)(2,1)S(1)}, bf16[256,256]{1,0:T(8,128)(2,1)S(1)}, u32[]{:S(2)}, u32[]{:S(2)}) collective-permute-start(bf16[256,256]{1,0:T(8,128)(2,1)S(1)} %collective-permute-done.5), channel_id=1, source_target_pairs={{0,256},{16,272},{32,288},{48,304},{64,320},{80,336},{96,352},{112... | collective-permute-start | bytes 393224 | tf_op jit(solution)/shard_map/ppermute | solution.py:38
  (1 other events, 0.8 us)
Sparse Core Ops, SparseCore 0:
  9.4 91.9 all-gather.6
  123.9 134.1 all-gather.8
  402.5 92.8 reduce-scatter.1
where the time goes:
time: 505 us; the launch traced here: 503 us
  waiting for transfers between devices  244 us (48%)
  blocking collectives  144 us (29%)
  local copies, waits for them, and re-layouts  39.1 us (8%)
  starting transfers between devices  29.3 us (6%)
  matrix products  19.9 us (4%)
  between operations  13.6 us (3%)
  other arithmetic  12.1 us (2%)
    reduce_scatter x1, waiting for transfers between devices, per_device(): lax.psum_scatter(jnp.dot(combined, w_out, preferred_element_type=jnp.floa...  93 us
    all_gather x1, waiting for transfers between devices, carried_in(): pieces = jax.tree.map(lambda part: lax.all_gather(part, axis), value)  77.5 us
    all_gather x1, blocking collectives, per_device(): every_id = lax.all_gather(tokens, 'seq', axis=0, tiled=True)  55.3 us
    all_gather x1, blocking collectives, carried_in(): pieces = jax.tree.map(lambda part: lax.all_gather(part, axis), value)  51 us
    psum x1, blocking collectives, per_device(): totals = lax.psum(squares, 'chan').reshape(2 * rows)  38 us
    ppermute x5, waiting for transfers between devices, partner(): return lax.ppermute(value, axis, pairs)  36.4 us
    dynamic_slice x62, local copies, waits for them, and re-layouts, lap(): longer = join(total, jax.tree.map(lambda part: part[position], pieces))  36.4 us
    all_gather x1, waiting for transfers between devices, per_device(): lax.all_gather(w_bc, 'chan', axis=0, tiled=True)  28.8 us
  transfers between devices with their start and end apart: 10, of which 10 were waited for; matrix products, arithmetic and copies ran while one was open for 3% of the time, Pallas kernels for 0%

commit v1 on v0

v1 whole, which is shorter than its diff:
```python
import jax
import jax.numpy as jnp
import numpy as np
from jax import lax
from jax.experimental import pallas as pl
from jax.experimental.pallas import tpu as pltpu
from jax.sharding import PartitionSpec as P

HEADS = 64
HEAD_DIM = 64
STATE = 128
CONV = 4
VOCAB = 5
ROWS = 256
OWN_HEADS = 4
OWN = OWN_HEADS * HEAD_DIM
SEQ = 32
CHAN = 16
CHIPS = SEQ // 2
LENGTH = SEQ * ROWS
LINES = LENGTH // 128
EPSILON = 1e-05
NONE = VOCAB
VMEM = pltpu.VMEM
SMEM = pltpu.SMEM
F32 = jnp.float32
BF16 = jnp.bfloat16


def gram_table():
    table = np.zeros((64, 1024), np.float32)
    for older in range(31):
        for newer in range(30):
            pair = lambda code: (5, 5) if code == 30 else (code // 5, code % 5)
            for tap, symbol in enumerate(pair(older) + pair(newer)):
                if symbol < VOCAB:
                    table[tap * 8 + symbol, older * 32 + newer] = 1
                    table[32 + tap * 8 + symbol, older * 32 + newer] = 1
    return table


def spread_table():
    row, column = (np.arange(128)[:, None], np.arange(OWN)[None, :])
    return (row // 32 == column // HEAD_DIM).astype(np.float32)


def place():
    return lax.axis_index("seq"), lax.axis_index("chan")


def iota(shape, axis):
    return lax.broadcasted_iota(jnp.int32, shape, axis)


def fiota(shape, axis):
    return iota(shape, axis).astype(F32)


def dot(a, b, contract):
    return lax.dot_general(a, b, ((contract[:1], contract[1:]), ((), ())), preferred_element_type=F32)


def silu(x):
    return x / (1.0 + jnp.exp(-x))


def tables_kernel(tokens, sibling, embed, w_x, w_z, w_bc, w_dt, dt_bias, decay, send, table, steps):
    seq, chan = place()
    emb = embed[...]
    x_tab = dot(emb, w_x[...], (1, 0)).astype(BF16).astype(F32)
    z_tab = dot(emb, w_z[...], (1, 0)).astype(BF16).astype(F32)
    table[...] = jnp.zeros(table.shape, F32)
    table[0:VOCAB, 0:OWN] = x_tab
    table[0:VOCAB, OWN:] = silu(z_tab)
    dt_tab = dot(emb, w_dt[...], (1, 0))
    lane = iota((VOCAB, OWN_HEADS), 1)
    bias = jnp.zeros((VOCAB, OWN_HEADS), F32)
    rate = jnp.zeros((VOCAB, OWN_HEADS), F32)
    for head in range(OWN_HEADS):
        bias = jnp.where(lane == head, dt_bias[head], bias)
        rate = jnp.where(lane == head, decay[head], rate)
    raw = dt_tab + bias
    step = jnp.maximum(raw, 0.0) + jnp.log1p(jnp.exp(-jnp.abs(raw)))
    steps[...] = jnp.zeros(steps.shape, F32)
    steps[0:VOCAB, 0:OWN_HEADS] = step
    steps[8 : 8 + VOCAB, 0:OWN_HEADS] = step * rate
    part = embed[:, pl.ds(pl.multiple_of(chan * 128, 128), 128)]
    bc = dot(part, w_bc[...], (1, 0))
    mine = tokens[...].astype(F32)
    other = sibling[...].astype(F32)
    first = lax.rem(seq, 2) == 0
    send[0, 0:VOCAB, :] = bc[:, :STATE]
    send[0, 5:7, :] = jnp.where(first, mine, other)
    send[0, 7:8, :] = jnp.zeros((1, 128), F32)
    send[0, 8 : 8 + VOCAB, :] = bc[:, STATE:]
    send[0, 13:15, :] = jnp.where(first, other, mine)
    send[0, 15:16, :] = jnp.zeros((1, 128), F32)
    block = send[0]
    for peer in range(1, CHIPS):
        send[peer] = block


def before(x, steps):
    lane, line = (iota(x.shape, 1), iota(x.shape, 0))
    turned = pltpu.roll(x, steps, 1)
    over = jnp.where(line == 0, float(NONE), pltpu.roll(turned, 1, 0))
    return jnp.where(lane < steps, over, turned)


def after(x, steps):
    lane, line = (iota(x.shape, 1), iota(x.shape, 0))
    turned = pltpu.roll(x, 128 - steps, 1)
    over = jnp.where(line == LINES - 1, float(NONE), pltpu.roll(turned, LINES - 1, 0))
    return jnp.where(lane >= 128 - steps, over, turned)


def hot(symbols, count):
    return jnp.where(fiota((count, symbols.shape[1]), 0) == symbols, 1.0, 0.0)


def taps_table(taps, table):
    return jnp.concatenate([taps[k : k + 1, :] * table for k in range(CONV)], 0)


def halves(x):
    high = x.astype(BF16)
    low = (x - high.astype(F32)).astype(BF16)
    return jnp.concatenate([high.astype(F32), low.astype(F32)], 0).astype(BF16)


def scan_kernel(
    received, complement, table, steps, step_at, conv_x, conv_bc, d_skip, gain, grams, grams_t, spread,
    out, send, tok_ref, fwd_ref, back_ref,
):
    seq, _ = place()
    for chip in range(CHIPS):
        tok_ref[4 * chip : 4 * chip + 2, :] = received[chip, 5:7, :]
        tok_ref[4 * chip + 2 : 4 * chip + 4, :] = received[chip, 13:15, :]
    bc_sum = received[0]
    for chip in range(1, CHIPS):
        bc_sum = bc_sum + received[chip]
    bc_sum = jnp.where(lax.rem(iota((16, 128), 0), 8) < VOCAB, bc_sum, 0.0)
    bc_sum = bc_sum.astype(BF16).astype(F32)
    bc_tab = jnp.concatenate([bc_sum[0:8], bc_sum[8:16]], 1)
    conv_tab = jnp.concatenate(
        [
            taps_table(conv_x[...].astype(F32), table[:, :OWN]),
            taps_table(conv_bc[...].astype(F32), bc_tab),
            jnp.concatenate([jnp.zeros((24, OWN), F32), table[:, OWN:]], 0),
        ],
        1,
    )
    conv_tab = halves(conv_tab)

    tok = tok_ref[...]
    flipped = jnp.zeros(tok.shape, F32)
    for symbol in range(VOCAB):
        flipped = jnp.where(tok == float(symbol), complement[symbol].astype(F32), flipped)
    fwd = [before(tok, 3), before(tok, 2), before(tok, 1), tok]
    back = [after(flipped, 3), after(flipped, 2), after(flipped, 1), flipped]
    for k in range(CONV):
        fwd_ref[k] = fwd[k]
        back_ref[k] = back[k]

    line = iota((LINES, 128), 0)
    start, end = (2 * seq, 2 * seq + 2)
    ahead = line < start
    inside = jnp.logical_or(ahead, line >= end)
    gram = [jnp.where(ahead, f, b) for f, b in zip(fwd, back)]
    older = gram[0] * 5.0 + gram[1] + jnp.where(ahead, 0.0, 32.0)
    newer = gram[2] * 5.0 + gram[3]
    newest = [jnp.logical_and(gram[3] == float(symbol), inside) for symbol in range(VOCAB)]
    marks = jnp.concatenate([jnp.where(hit, 1.0, 0.0) for hit in newest], 0).astype(BF16)
    row, column = (iota((128, 128), 0), iota((128, 128), 1))
    within = jnp.concatenate(
        [
            jnp.where(row > column, 1.0, 0.0),
            jnp.where(row < column, 1.0, 0.0),
            jnp.ones((128, 128), F32),
        ],
        1,
    ).astype(BF16)
    counts = dot(marks, within, (1, 0))
    parts = [counts[LINES * symbol : LINES * (symbol + 1)] for symbol in range(VOCAB)]
    totals = jnp.concatenate([part[:, 256:384] for part in parts], 1).astype(BF16)
    to, of = (iota((LINES, LINES), 0), iota((LINES, LINES), 1))
    between = jnp.logical_or(
        jnp.logical_and(to < of, of < start), jnp.logical_and(of >= end, of < to)
    )
    lines_between = dot(jnp.where(between, 1.0, 0.0).astype(BF16), totals, (1, 0))
    passed = [
        jnp.where(ahead, part[:, 0:128], part[:, 128:256]) + lines_between[:, 128 * k : 128 * k + 128]
        for k, part in enumerate(parts)
    ]
    weights = []
    for head in range(OWN_HEADS):
        lost = jnp.zeros((LINES, 128), F32)
        own_step = jnp.zeros((LINES, 128), F32)
        for symbol in range(VOCAB):
            lost = lost + step_at[8 + symbol, head] * passed[symbol]
            own_step = jnp.where(newest[symbol], step_at[symbol, head], own_step)
        weights.append(own_step * jnp.exp(-lost))

    sums = jnp.zeros((64, 128), F32)
    for first in range(0, LINES, 2):
        left, right = ([], [])
        for at in (first, first + 1):
            left.append(hot(older[at : at + 1], 64))
            hits = fiota((32, 128), 0) == newer[at : at + 1]
            right.append(
                jnp.concatenate([jnp.where(hits, w[at : at + 1], 0.0) for w in weights], 0)
            )
        sums = sums + dot(
            jnp.concatenate(left, 1).astype(BF16), jnp.concatenate(right, 1).astype(BF16), (1, 1)
        )

    gram_values = silu(dot(grams_t[...], conv_tab[:, :OWN], (1, 0)))
    gram_b = silu(dot(conv_tab[:, OWN : OWN + STATE], grams[...], (0, 0))).astype(BF16)
    same = jnp.where(lax.rem(iota((32, 128), 1), 32) == iota((32, 128), 0), 1.0, 0.0)
    states = []
    for strand in range(2):
        placed = jnp.concatenate(
            [sums[32 * strand + code : 32 * strand + code + 1] * same for code in range(32)], 0
        )
        wide = dot(placed.astype(BF16), spread[...], (1, 0))
        states.append(dot(gram_b, (wide * gram_values).astype(BF16), (1, 0)))

    hots = []
    for ref in (fwd_ref, back_ref):
        for k in range(2):
            hots.append(
                jnp.concatenate([hot(ref[tap, pl.ds(start + k, 1), :], 8) for tap in range(CONV)], 0)
            )
    hots = jnp.concatenate(hots, 1)
    mixed = dot(jnp.concatenate([hots, hots], 0).astype(BF16), conv_tab, (0, 0))
    gate = mixed[:, OWN + 2 * STATE :]
    mixed = silu(mixed[:, : OWN + 2 * STATE])
    head_of = iota((1, OWN), 1) // HEAD_DIM
    skip = jnp.zeros((1, OWN), F32)
    for head in range(OWN_HEADS):
        skip = jnp.where(head_of == head, d_skip[head], skip)
    row, column = (iota((ROWS, ROWS), 0), iota((ROWS, ROWS), 1))
    squares = []
    for strand in range(2):
        rows = slice(ROWS * strand, ROWS * (strand + 1))
        values = mixed[rows, :OWN]
        b_in = mixed[rows, OWN : OWN + STATE].astype(BF16)
        c_out = mixed[rows, OWN + STATE :]
        causal = row >= column if strand == 0 else row <= column
        order = row <= column if strand == 0 else row >= column
        symbols = hots[24:32, rows]
        seen = dot(symbols.astype(BF16), jnp.where(order, 1.0, 0.0).astype(BF16), (1, 0))
        cumul, step = ([], [])
        for head in range(OWN_HEADS):
            total = jnp.zeros((1, ROWS), F32)
            own_step = jnp.zeros((1, ROWS), F32)
            for symbol in range(VOCAB):
                total = total - step_at[8 + symbol, head] * seen[symbol : symbol + 1]
                own_step = own_step + step_at[symbol, head] * symbols[symbol : symbol + 1]
            cumul.append(total)
            step.append(own_step)
        across = jnp.transpose(
            jnp.concatenate(cumul + [jnp.zeros((128 - OWN_HEADS, ROWS), F32)], 0)
        )
        scores = dot(c_out.astype(BF16), b_in, (1, 1))
        left, right, tail_left, tail_right = ([], [], [], [])
        for head in range(OWN_HEADS):
            column_of = across[:, head : head + 1]
            decayed = jnp.exp(jnp.where(causal, column_of - cumul[head], -1e30))
            left.append((decayed * (scores * step[head])).astype(BF16))
            right.append(jnp.where(head_of == head, values, 0.0).astype(BF16))
            tail_left.append((c_out * jnp.exp(column_of)).astype(BF16))
            tail_right.append(jnp.where(head_of == head, states[strand], 0.0).astype(BF16))
        ssd = dot(
            jnp.concatenate(left + tail_left, 1), jnp.concatenate(right + tail_right, 0), (1, 0)
        )
        gated = (ssd + values * skip) * gate[rows]
        out[rows, :] = gated * gain[...]
        squared = gated * gated
        squares.append(
            jnp.sum(jnp.transpose(squared[:, :128] + squared[:, 128:]), axis=0, keepdims=True)
        )
    mine = jnp.concatenate(
        [square[:, 128 * k : 128 * k + 128] for square in squares for k in range(2)], 0
    )
    for peer in range(CHAN):
        send[peer] = mine


def project_kernel(squares, gated, w_out, out):
    total = squares[0]
    for peer in range(1, CHAN):
        total = total + squares[peer]
    scale = lax.rsqrt(total / (HEADS * HEAD_DIM) + EPSILON)
    normed = []
    for part in range(4):
        down = jnp.transpose(jnp.broadcast_to(scale[part : part + 1], (128, 128)))
        block = gated[128 * part : 128 * part + 128, :]
        normed.append((block * jnp.concatenate([down, down], 1)).astype(BF16).astype(F32))
    combined = jnp.concatenate([normed[0] + normed[2], normed[1] + normed[3]], 0).astype(BF16)
    mixed = dot(combined, w_out[...], (1, 0))
    out[...] = mixed.astype(BF16).reshape(out.shape)


def call(kernel, outs, kinds, scratch=()):
    return pl.pallas_call(
        kernel,
        out_shape=outs,
        in_specs=[pl.BlockSpec(memory_space=kind) for kind in kinds],
        out_specs=jax.tree.map(lambda _: pl.BlockSpec(memory_space=VMEM), outs),
        scratch_shapes=scratch,
        compiler_params=pltpu.CompilerParams(vmem_limit_bytes=48 * 2**20),
    )


def make_tables(*args):
    return call(
        tables_kernel,
        (
            jax.ShapeDtypeStruct((CHIPS, 16, 128), F32),
            jax.ShapeDtypeStruct((8, 2 * OWN), F32),
            jax.ShapeDtypeStruct((16, 128), F32),
        ),
        [VMEM] * 7 + [SMEM] * 2,
    )(*args)


def make_scan(received, complement, table, steps, conv_x, conv_bc, d_skip, norm_gain):
    grams = gram_table()
    return call(
        scan_kernel,
        (
            jax.ShapeDtypeStruct((2 * ROWS, OWN), F32),
            jax.ShapeDtypeStruct((CHAN, 4, 128), F32),
        ),
        [VMEM, SMEM, VMEM, VMEM, SMEM, VMEM, VMEM, SMEM, VMEM, VMEM, VMEM, VMEM],
        [
            pltpu.VMEM((LINES, 128), F32),
            pltpu.VMEM((CONV, LINES, 128), F32),
            pltpu.VMEM((CONV, LINES, 128), F32),
        ],
    )(
        received, complement, table, steps, steps, conv_x, conv_bc, d_skip, norm_gain.reshape(1, OWN),
        jnp.asarray(grams, BF16), jnp.asarray(grams.T, BF16), jnp.asarray(spread_table(), BF16),
    )


def make_project(squares, gated, w_out):
    return call(
        project_kernel, jax.ShapeDtypeStruct((CHAN, ROWS // CHAN, w_out.shape[1]), BF16), [VMEM] * 3
    )(squares, gated, w_out)


def per_device(
    tokens, complement, embed, w_x, w_z, w_bc, w_dt, dt_bias, decay_rate, d_skip, conv_x, conv_bc,
    norm_gain, w_out,
):
    own = tokens.reshape(2, 128)
    sibling = lax.ppermute(own, "seq", [(source, source ^ 1) for source in range(SEQ)])
    send, table, steps = make_tables(
        own, sibling, embed, w_x, w_z, w_bc, w_dt, dt_bias, decay_rate
    )
    groups = [
        [(2 * chip + core) * CHAN + (chip + shift) % CHAN for chip in range(CHIPS)]
        for core in range(2)
        for shift in range(CHAN)
    ]
    received = lax.all_to_all(
        send, ("seq", "chan"), 0, 0, tiled=True, axis_index_groups=groups
    )
    gated, squares = make_scan(
        received, complement, table, steps, conv_x, conv_bc, d_skip, norm_gain
    )
    squares = lax.all_to_all(squares, "chan", 0, 0, tiled=True)
    partial = make_project(squares, gated, w_out)
    pieces = lax.all_to_all(partial, "chan", 0, 0, tiled=True)
    return jnp.sum(pieces.astype(F32), axis=0).astype(BF16)


def solution(mesh):
    placed = (
        P("seq"),
        P(),
        P(),
        P(None, "chan"),
        P(None, "chan"),
        P("chan", None),
        P(None, "chan"),
        P("chan"),
        P("chan"),
        P("chan"),
        P(None, "chan"),
        P(),
        P("chan"),
        P("chan", None),
    )
    return jax.shard_map(
        per_device, mesh=mesh, in_specs=placed, out_specs=P(("seq", "chan"), None), check_vma=False
    )
```

time: 505 us -> 91.3 us (0.18)
  the two profiles are of different devices: /device:TPU:8 before, /device:TPU:1 now
where the time goes in v1:
time: 91.3 us; the launch traced here: 90.9 us
  blocking collectives  69.8 us (76%)
  starting transfers between devices  8.92 us (10%)
  Pallas kernels  6.41 us (7%)
  local copies, waits for them, and re-layouts  4.86 us (5%)
    all_to_all x1, blocking collectives, per_device(): pieces = lax.all_to_all(partial, 'chan', 0, 0, tiled=True)  29.3 us
    all_to_all x1, blocking collectives, per_device(): lax.all_to_all(send, ('seq', 'chan'), 0, 0, tiled=True, axis_index_groups...  28.2 us
    all_to_all x1, blocking collectives, per_device(): squares = lax.all_to_all(squares, 'chan', 0, 0, tiled=True)  12.4 us
    ppermute x1, starting transfers between devices, per_device(): lax.ppermute(own, 'seq', [(source, source ^ 1) for source in range(SEQ)])  8.92 us
    unnamed x33, local copies, waits for them, and re-layouts  4.86 us
    pallas_call x1, Pallas kernels, make_scan(): call(scan_kernel, (jax.ShapeDtypeStruct((2 * ROWS, OWN), F32), jax.ShapeD...  4.86 us
  transfers between devices with their start and end apart: 1, of which 0 were waited for; matrix products, arithmetic and copies ran while one was open for 1% of the time, Pallas kernels for 0%

profile of v1, /device:TPU:1, one launch (start us, length us, event | category | flops | bytes accessed | tf_op | source)
XLA Modules:
  0.0 90.9 jit_solution(15631796595029524471)
XLA Ops:
  0.0 0.7 copy-done.10
  0.7 8.9 %collective-permute-start = (s32[2,128]{1,0:T(2,128)S(1)}, s32[2,128]{1,0:T(2,128)S(1)}, u32[]{:S(2)}, u32[]{:S(2)}) collective-permute-start(s32[2,128]{1,0:T(2,128)S(1)} %bitcast.2), channel_id=1, source_target_pairs={{0,16},{16,0},{32,48},{48,32},{64,80},{80,64},{96,112},{112,96},{1... | collective-permute-start | bytes 3080 | tf_op jit(solution)/shard_map/ppermute | solution.py:359
  9.6 1.0 %copy.18.w_dt = bf16[2048,4]{1,0:T(8,128)(2,1)S(1)} copy(bf16[2048,4]{0,1:T(4,128)(2,1)} %param.23) | data formatting | bytes 32768 | tf_op args[6]
  10.6 0.0 collective-permute-done.sibling
  10.7 0.0 copy-done.5
  10.7 0.0 copy-done.7
  10.7 0.0 copy-done.14
  10.7 0.0 copy-done.15
  10.7 0.0 copy-start
  10.7 1.2 %copy-done = bf16[2048,256]{1,0:T(8,128)(2,1)S(1)} copy-done((bf16[2048,256]{1,0:T(8,128)(2,1)S(1)}, bf16[2048,256]{1,0:T(8,128)(2,1)}, u32[]{:S(2)}) %copy-start) | copy-done | bytes 1048600
  11.9 1.2 %copy-done.1 = bf16[2048,256]{1,0:T(8,128)(2,1)S(1)} copy-done((bf16[2048,256]{1,0:T(8,128)(2,1)S(1)}, bf16[2048,256]{1,0:T(8,128)(2,1)}, u32[]{:S(2)}) %copy-start.1) | copy-done | bytes 1048600
  13.2 1.0 %shard_map.163 = (f32[16,16,128]{2,1,0:T(8,128)S(1)}, f32[8,512]{1,0:T(8,128)S(1)}, f32[16,128]{1,0:T(8,128)S(1)}) custom-call(s32[2,128]{1,0:T(2,128)S(1)} %bitcast.3, s32[2,128]{1,0:T(2,128)S(1)} %collective-permute-done.sibling, bf16[5,2048]{1,0:T(8,128)(2,1)S(1)} %copy-done.7, bf16[2048,256]{1,0:T(8,128)(2,1)S(1)} %copy-done, ...), custom_call_target="tpu_custom_call" | custom-call | tf_op jit(solution)/shard_map/pallas_call | solution.py:317
  14.2 0.0 copy-start.3
  14.2 0.0 copy-start.13
  14.2 28.2 %all_to_all.15.received = f32[16,16,128]{2,1,0:T(8,128)S(1)} all-to-all(f32[16,16,128]{2,1,0:T(8,128)S(1)} %get-tuple-element.10), channel_id=1, replica_groups={{0,33,66,99,132,165,198,231,264,297,330,363,396,429,462,495},{1,34,67,1..., dimensions={0} | all-to-all | bytes 262144 | tf_op jit(solution)/shard_map/all_to_all | solution.py:368
  42.4 0.0 copy-done.4
  42.4 0.6 copy-done.9
  43.1 0.0 copy-done.8
  43.1 0.0 copy-done.11
  43.1 4.9 %shard_map.164 = (f32[512,256]{1,0:T(8,128)S(1)}, f32[16,4,128]{2,1,0:T(4,128)S(1)}) custom-call(f32[16,16,128]{2,1,0:T(8,128)S(1)} %all_to_all.15.received, s32[5]{0:T(128)S(1)} %copy-done.12, f32[8,512]{1,0:T(8,128)S(1)} %get-tuple-element.11.table, f32[16,128]{1,0:T(8,128)S(1)} %get-tuple-element.12.steps.step_at, ...), custom_call_target="tpu_custom_call" | custom-call | tf_op jit(solution)/shard_map/pallas_call | solution.py:330
  48.0 12.4 %all_to_all.16.squares = f32[16,4,128]{2,1,0:T(4,128)S(1)} all-to-all(f32[16,4,128]{2,1,0:T(4,128)S(1)} %get-tuple-element.13), channel_id=1, replica_groups=mesh['seq'=32,'chan'=16] {'chan'}, dimensions={0} | all-to-all | bytes 65536 | tf_op jit(solution)/shard_map/all_to_all | solution.py:374
  60.3 0.5 shard_map.165
  60.9 29.3 %all_to_all.17 = bf16[16,16,2048]{2,1,0:T(8,128)(2,1)S(1)} all-to-all(bf16[16,16,2048]{2,1,0:T(8,128)(2,1)S(1)} %shard_map.165), channel_id=1, replica_groups=mesh['seq'=32,'chan'=16] {'chan'}, dimensions={0} | all-to-all | bytes 2097152 | tf_op jit(solution)/shard_map/all_to_all | solution.py:376
  90.1 0.8 reduce_sum.12
  (18 shorter events, 0.0 us)
Async XLA Ops:
  0.0 0.7 copy-start.10
  0.7 10.0 %copy-start.5 = (bf16[128,256]{1,0:T(8,128)(2,1)S(1)}, bf16[128,256]{1,0:T(8,128)(2,1)}, u32[]{:S(2)}) copy-start(bf16[128,256]{1,0:T(8,128)(2,1)} %w_bc.1) | copy-start | bytes 196612
  0.7 10.0 %copy-start.7 = (bf16[5,2048]{1,0:T(8,128)(2,1)S(1)}, bf16[5,2048]{1,0:T(8,128)(2,1)}, u32[]{:S(2)}) copy-start(bf16[5,2048]{1,0:T(8,128)(2,1)} %embed.1) | copy-start | bytes 61444
  0.7 10.0 %copy-start.14 = (f32[4]{0:T(128)S(1)}, f32[4]{0:T(128)}, u32[]{:S(2)}) copy-start(f32[4]{0:T(128)} %dt_bias.1) | copy-start | bytes 52
  0.7 10.0 %copy-start.15 = (f32[4]{0:T(128)S(1)}, f32[4]{0:T(128)}, u32[]{:S(2)}) copy-start(f32[4]{0:T(128)} %decay.1) | copy-start | bytes 52
  0.7 10.0 %collective-permute-start = (s32[2,128]{1,0:T(2,128)S(1)}, s32[2,128]{1,0:T(2,128)S(1)}, u32[]{:S(2)}, u32[]{:S(2)}) collective-permute-start(s32[2,128]{1,0:T(2,128)S(1)} %bitcast.2), channel_id=1, source_target_pairs={{0,16},{16,0},{32,48},{48,32},{64,80},{80,64},{96,112},{112,96},{1... | collective-permute-start | bytes 3080 | tf_op jit(solution)/shard_map/ppermute | solution.py:359
  10.7 1.2 %copy-start = (bf16[2048,256]{1,0:T(8,128)(2,1)S(1)}, bf16[2048,256]{1,0:T(8,128)(2,1)}, u32[]{:S(2)}) copy-start(bf16[2048,256]{1,0:T(8,128)(2,1)} %w_x.1) | copy-start | bytes 3145732
  11.9 1.2 %copy-start.1 = (bf16[2048,256]{1,0:T(8,128)(2,1)S(1)}, bf16[2048,256]{1,0:T(8,128)(2,1)}, u32[]{:S(2)}) copy-start(bf16[2048,256]{1,0:T(8,128)(2,1)} %w_z.1) | copy-start | bytes 3145732
  13.2 29.2 %copy-start.4 = (bf16[64,1024]{1,0:T(8,128)(2,1)S(1)}, bf16[64,1024]{1,0:T(8,128)(2,1)}, u32[]{:S(2)}) copy-start(bf16[64,1024]{1,0:T(8,128)(2,1)} %constant.9.clone.grams) | copy-start | bytes 393220
  13.2 29.3 %copy-start.6 = (bf16[128,256]{1,0:T(8,128)(2,1)S(1)}, bf16[128,256]{1,0:T(8,128)(2,1)}, u32[]{:S(2)}) copy-start(bf16[128,256]{1,0:T(8,128)(2,1)} %constant.11.clone.spread) | copy-start | bytes 196612
  13.2 47.2 %copy-start.2 = (bf16[256,2048]{1,0:T(8,128)(2,1)S(1)}, bf16[256,2048]{1,0:T(8,128)(2,1)}, u32[]{:S(2)}) copy-start(bf16[256,2048]{1,0:T(8,128)(2,1)} %w_out.1) | copy-start | bytes 3145732
  14.2 28.2 %copy-start.3 = (bf16[1024,64]{1,0:T(8,128)(2,1)S(1)}, bf16[1024,64]{1,0:T(8,128)(2,1)}, u32[]{:S(2)}) copy-start(bf16[1024,64]{1,0:T(8,128)(2,1)} %constant.10.clone.grams_t) | copy-start | bytes 393220
  14.2 28.2 %copy-start.13 = (f32[4]{0:T(128)S(1)}, f32[4]{0:T(128)}, u32[]{:S(2)}) copy-start(f32[4]{0:T(128)} %d_skip.1) | copy-start | bytes 52
  42.4 0.7 copy-start.9
  42.4 0.7 copy-start.8
  42.4 0.7 copy-start.11
  42.4 0.7 copy-start.12

commit v2 on v1

--- a/solution.py
+++ b/solution.py
@@ -19,6 +19,9 @@
 CHIPS = SEQ // 2
 LENGTH = SEQ * ROWS
 LINES = LENGTH // 128
+SIDE = 4
+PART = ROWS // SIDE
+PIECE = PART // SIDE
 EPSILON = 1e-05
 NONE = VOCAB
 VMEM = pltpu.VMEM
@@ -64,26 +67,8 @@
     return x / (1.0 + jnp.exp(-x))
 
 
-def tables_kernel(tokens, sibling, embed, w_x, w_z, w_bc, w_dt, dt_bias, decay, send, table, steps):
+def send_kernel(tokens, sibling, embed, w_bc, send):
     seq, chan = place()
-    emb = embed[...]
-    x_tab = dot(emb, w_x[...], (1, 0)).astype(BF16).astype(F32)
-    z_tab = dot(emb, w_z[...], (1, 0)).astype(BF16).astype(F32)
-    table[...] = jnp.zeros(table.shape, F32)
-    table[0:VOCAB, 0:OWN] = x_tab
-    table[0:VOCAB, OWN:] = silu(z_tab)
-    dt_tab = dot(emb, w_dt[...], (1, 0))
-    lane = iota((VOCAB, OWN_HEADS), 1)
-    bias = jnp.zeros((VOCAB, OWN_HEADS), F32)
-    rate = jnp.zeros((VOCAB, OWN_HEADS), F32)
-    for head in range(OWN_HEADS):
-        bias = jnp.where(lane == head, dt_bias[head], bias)
-        rate = jnp.where(lane == head, decay[head], rate)
-    raw = dt_tab + bias
-    step = jnp.maximum(raw, 0.0) + jnp.log1p(jnp.exp(-jnp.abs(raw)))
-    steps[...] = jnp.zeros(steps.shape, F32)
-    steps[0:VOCAB, 0:OWN_HEADS] = step
-    steps[8 : 8 + VOCAB, 0:OWN_HEADS] = step * rate
     part = embed[:, pl.ds(pl.multiple_of(chan * 128, 128), 128)]
     bc = dot(part, w_bc[...], (1, 0))
     mine = tokens[...].astype(F32)
@@ -100,6 +85,30 @@
         send[peer] = block
 
 
+def tables_kernel(embed, w_x, w_z, w_dt, dt_bias, decay, conv_x, grams_t, table, gram_values, steps):
+    emb = embed[...]
+    x_tab = dot(emb, w_x[...], (1, 0)).astype(BF16).astype(F32)
+    z_tab = dot(emb, w_z[...], (1, 0)).astype(BF16).astype(F32)
+    pad = jnp.zeros((8 - VOCAB, OWN), F32)
+    x_taps = halves(taps_table(conv_x[...].astype(F32), jnp.concatenate([x_tab, pad], 0)))
+    gate = jnp.concatenate([jnp.zeros((24, OWN), F32), silu(z_tab), pad], 0)
+    table[:, :OWN] = x_taps
+    table[:, OWN:] = halves(gate)
+    gram_values[...] = silu(dot(grams_t[...], x_taps, (1, 0)))
+    dt_tab = dot(emb, w_dt[...], (1, 0))
+    lane = iota((VOCAB, OWN_HEADS), 1)
+    bias = jnp.zeros((VOCAB, OWN_HEADS), F32)
+    rate = jnp.zeros((VOCAB, OWN_HEADS), F32)
+    for head in range(OWN_HEADS):
+        bias = jnp.where(lane == head, dt_bias[head], bias)
+        rate = jnp.where(lane == head, decay[head], rate)
+    raw = dt_tab + bias
+    step = jnp.maximum(raw, 0.0) + jnp.log1p(jnp.exp(-jnp.abs(raw)))
+    steps[...] = jnp.zeros(steps.shape, F32)
+    steps[0:VOCAB, 0:OWN_HEADS] = step
+    steps[8 : 8 + VOCAB, 0:OWN_HEADS] = step * rate
+
+
 def before(x, steps):
     lane, line = (iota(x.shape, 1), iota(x.shape, 0))
     turned = pltpu.roll(x, steps, 1)
@@ -129,7 +138,7 @@
 
 
 def scan_kernel(
-    received, complement, table, steps, step_at, conv_x, conv_bc, d_skip, gain, grams, grams_t, spread,
+    received, complement, table, gram_values, step_at, conv_bc, d_skip, gain, grams, spread,
     out, send, tok_ref, fwd_ref, back_ref,
 ):
     seq, _ = place()
@@ -142,15 +151,8 @@
     bc_sum = jnp.where(lax.rem(iota((16, 128), 0), 8) < VOCAB, bc_sum, 0.0)
     bc_sum = bc_sum.astype(BF16).astype(F32)
     bc_tab = jnp.concatenate([bc_sum[0:8], bc_sum[8:16]], 1)
-    conv_tab = jnp.concatenate(
-        [
-            taps_table(conv_x[...].astype(F32), table[:, :OWN]),
-            taps_table(conv_bc[...].astype(F32), bc_tab),
-            jnp.concatenate([jnp.zeros((24, OWN), F32), table[:, OWN:]], 0),
-        ],
-        1,
-    )
-    conv_tab = halves(conv_tab)
+    bc_taps = halves(taps_table(conv_bc[...].astype(F32), bc_tab))
+    conv_tab = jnp.concatenate([table[:, :OWN], bc_taps, table[:, OWN:]], 1)
 
     tok = tok_ref[...]
     flipped = jnp.zeros(tok.shape, F32)
@@ -214,8 +216,7 @@
             jnp.concatenate(left, 1).astype(BF16), jnp.concatenate(right, 1).astype(BF16), (1, 1)
         )
 
-    gram_values = silu(dot(grams_t[...], conv_tab[:, :OWN], (1, 0)))
-    gram_b = silu(dot(conv_tab[:, OWN : OWN + STATE], grams[...], (0, 0))).astype(BF16)
+    gram_b = silu(dot(bc_taps[:, :STATE], grams[...], (0, 0))).astype(BF16)
     same = jnp.where(lax.rem(iota((32, 128), 1), 32) == iota((32, 128), 0), 1.0, 0.0)
     states = []
     for strand in range(2):
@@ -223,7 +224,7 @@
             [sums[32 * strand + code : 32 * strand + code + 1] * same for code in range(32)], 0
         )
         wide = dot(placed.astype(BF16), spread[...], (1, 0))
-        states.append(dot(gram_b, (wide * gram_values).astype(BF16), (1, 0)))
+        states.append(dot(gram_b, (wide * gram_values[...]).astype(BF16), (1, 0)))
 
     hots = []
     for ref in (fwd_ref, back_ref):
@@ -302,6 +303,13 @@
     out[...] = mixed.astype(BF16).reshape(out.shape)
 
 
+def sum_kernel(received, out):
+    total = received[0].astype(F32)
+    for peer in range(1, SIDE):
+        total = total + received[peer].astype(F32)
+    out[...] = total.astype(BF16).reshape(out.shape)
+
+
 def call(kernel, outs, kinds, scratch=()):
     return pl.pallas_call(
         kernel,
@@ -313,42 +321,76 @@
     )
 
 
+def make_send(*args):
+    return call(send_kernel, jax.ShapeDtypeStruct((CHIPS, 16, 128), F32), [VMEM] * 4)(*args)
+
+
 def make_tables(*args):
     return call(
         tables_kernel,
         (
-            jax.ShapeDtypeStruct((CHIPS, 16, 128), F32),
-            jax.ShapeDtypeStruct((8, 2 * OWN), F32),
+            jax.ShapeDtypeStruct((64, 2 * OWN), BF16),
+            jax.ShapeDtypeStruct((1024, OWN), F32),
             jax.ShapeDtypeStruct((16, 128), F32),
         ),
-        [VMEM] * 7 + [SMEM] * 2,
-    )(*args)
-
-
-def make_scan(received, complement, table, steps, conv_x, conv_bc, d_skip, norm_gain):
-    grams = gram_table()
+        [VMEM] * 4 + [SMEM] * 2 + [VMEM] * 2,
+    )(*args, jnp.asarray(gram_table().T, BF16))
+
+
+def make_scan(received, complement, table, gram_values, steps, conv_bc, d_skip, norm_gain):
     return call(
         scan_kernel,
-        (
-            jax.ShapeDtypeStruct((2 * ROWS, OWN), F32),
-            jax.ShapeDtypeStruct((CHAN, 4, 128), F32),
-        ),
-        [VMEM, SMEM, VMEM, VMEM, SMEM, VMEM, VMEM, SMEM, VMEM, VMEM, VMEM, VMEM],
+        (jax.ShapeDtypeStruct((2 * ROWS, OWN), F32), jax.ShapeDtypeStruct((CHAN, 4, 128), F32)),
+        [VMEM, SMEM, VMEM, VMEM, SMEM, VMEM, SMEM, VMEM, VMEM, VMEM],
         [
             pltpu.VMEM((LINES, 128), F32),
             pltpu.VMEM((CONV, LINES, 128), F32),
             pltpu.VMEM((CONV, LINES, 128), F32),
         ],
     )(
-        received, complement, table, steps, steps, conv_x, conv_bc, d_skip, norm_gain.reshape(1, OWN),
-        jnp.asarray(grams, BF16), jnp.asarray(grams.T, BF16), jnp.asarray(spread_table(), BF16),
+        received, complement, table, gram_values, steps, conv_bc, d_skip, norm_gain.reshape(1, OWN),
+        jnp.asarray(gram_table(), BF16), jnp.asarray(spread_table(), BF16),
     )
 
 
 def make_project(squares, gated, w_out):
     return call(
-        project_kernel, jax.ShapeDtypeStruct((CHAN, ROWS // CHAN, w_out.shape[1]), BF16), [VMEM] * 3
+        project_kernel, jax.ShapeDtypeStruct((SIDE, PART, w_out.shape[1]), BF16), [VMEM] * 3
     )(squares, gated, w_out)
+
+
+def make_sum(received, shape):
+    return call(sum_kernel, jax.ShapeDtypeStruct(shape, BF16), [VMEM])(received)
+
+
+def device(seq, chan):
+    return seq * CHAN + chan
+
+
+def mixed_groups():
+    side = range(SIDE)
+    return [
+        [
+            device(2 * (SIDE * y + high) + core, (y + right) % SIDE * SIDE + (high + up) % SIDE)
+            for y in side
+            for high in side
+        ]
+        for core in range(2)
+        for right in side
+        for up in side
+    ]
+
+
+def x_groups():
+    return [[x * SIDE + z for x in range(SIDE)] for z in range(SIDE)]
+
+
+def z_groups():
+    return [[x * SIDE + z for z in range(SIDE)] for x in range(SIDE)]
+
+
+def exchange(value, axes, groups=None):
+    return lax.all_to_all(value, axes, 0, 0, tiled=True, axis_index_groups=groups)
 
 
 def per_device(
@@ -357,24 +399,14 @@
 ):
     own = tokens.reshape(2, 128)
     sibling = lax.ppermute(own, "seq", [(source, source ^ 1) for source in range(SEQ)])
-    send, table, steps = make_tables(
-        own, sibling, embed, w_x, w_z, w_bc, w_dt, dt_bias, decay_rate
-    )
-    groups = [
-        [(2 * chip + core) * CHAN + (chip + shift) % CHAN for chip in range(CHIPS)]
-        for core in range(2)
-        for shift in range(CHAN)
-    ]
-    received = lax.all_to_all(
-        send, ("seq", "chan"), 0, 0, tiled=True, axis_index_groups=groups
-    )
+    received = exchange(make_send(own, sibling, embed, w_bc), ("seq", "chan"), mixed_groups())
+    table, gram_values, steps = make_tables(embed, w_x, w_z, w_dt, dt_bias, decay_rate, conv_x)
     gated, squares = make_scan(
-        received, complement, table, steps, conv_x, conv_bc, d_skip, norm_gain
-    )
-    squares = lax.all_to_all(squares, "chan", 0, 0, tiled=True)
-    partial = make_project(squares, gated, w_out)
-    pieces = lax.all_to_all(partial, "chan", 0, 0, tiled=True)
-    return jnp.sum(pieces.astype(F32), axis=0).astype(BF16)
+        received, complement, table, gram_values, steps, conv_bc, d_skip, norm_gain
+    )
+    partial = make_project(exchange(squares, "chan"), gated, w_out)
+    partial = make_sum(exchange(partial, "chan", x_groups()), (SIDE, PIECE, w_out.shape[1]))
+    return make_sum(exchange(partial, "chan", z_groups()), (PIECE, w_out.shape[1]))
 
 
 def solution(mesh):

time: 91.3 us -> 86.8 us (0.951)
  the two profiles are of different devices: /device:TPU:1 before, /device:TPU:2 now
where the time goes in v2:
time: 86.8 us; the launch traced here: 86.1 us
  blocking collectives  38.3 us (44%)
  starting transfers between devices  20.5 us (24%)
  waiting for transfers between devices  13.1 us (15%)
  Pallas kernels  8.34 us (10%)
  local copies, waits for them, and re-layouts  5.68 us (7%)
    all_to_all x3, blocking collectives, exchange(): lax.all_to_all(value, axes, 0, 0, tiled=True, axis_index_groups=groups)  38.3 us
    all_to_all x1, starting transfers between devices, exchange(): lax.all_to_all(value, axes, 0, 0, tiled=True, axis_index_groups=groups)  18.6 us
    all_to_all x1, waiting for transfers between devices, exchange(): lax.all_to_all(value, axes, 0, 0, tiled=True, axis_index_groups=groups)  12 us
    unnamed x37, local copies, waits for them, and re-layouts  5.68 us
    pallas_call x1, Pallas kernels, make_scan(): call(scan_kernel, (jax.ShapeDtypeStruct((2 * ROWS, OWN), F32), jax.ShapeD...  4.87 us
    ppermute x1, starting transfers between devices, per_device(): lax.ppermute(own, 'seq', [(source, source ^ 1) for source in range(SEQ)])  1.91 us
  transfers between devices with their start and end apart: 2, of which 2 were waited for; matrix products, arithmetic and copies ran while one was open for 0% of the time, Pallas kernels for 2%

profile of v2, /device:TPU:2, one launch (start us, length us, event | category | flops | bytes accessed | tf_op | source)
XLA Modules:
  0.0 86.1 jit_solution(3677008105283934558)
XLA Ops:
  0.0 0.7 copy-done.11
  0.7 1.9 %collective-permute-start = (s32[2,128]{1,0:T(2,128)S(1)}, s32[2,128]{1,0:T(2,128)S(1)}, u32[]{:S(2)}, u32[]{:S(2)}) collective-permute-start(s32[2,128]{1,0:T(2,128)S(1)} %bitcast.2), channel_id=1, source_target_pairs={{0,16},{16,0},{32,48},{48,32},{64,80},{80,64},{96,112},{112,96},{1... | collective-permute-start | bytes 3080 | tf_op jit(solution)/shard_map/ppermute | solution.py:401
  2.6 1.1 %collective-permute-done.sibling = s32[2,128]{1,0:T(2,128)S(1)} collective-permute-done((s32[2,128]{1,0:T(2,128)S(1)}, s32[2,128]{1,0:T(2,128)S(1)}, u32[]{:S(2)}, u32[]{:S(2)}) %collective-permute-start) | collective-permute-done | bytes 1056 | tf_op jit(solution)/shard_map/ppermute | solution.py:401
  3.7 0.8 copy-done.4
  4.5 0.8 copy-done.7
  5.3 0.8 shard_map.163
  6.1 18.6 %all-to-all-start = ((f32[16,16,128]{2,1,0:T(8,128)}), f32[16,16,128]{2,1,0:T(8,128)S(1)}, u32[]{:S(2)}, u32[]{:S(2)}) async-start(f32[16,16,128]{2,1,0:T(8,128)} %shard_map.163), calls=%async_computation | async-start | bytes 262144 | tf_op jit(solution)/shard_map/all_to_all | solution.py:393
  24.7 0.0 copy-start.3
  24.8 0.0 copy-start.9
  24.8 0.0 copy-start.13
  24.8 0.3 copy.18.w_dt
  25.1 0.6 copy-done.3
  25.7 1.2 %copy-done = bf16[2048,256]{1,0:T(8,128)(2,1)S(1)} copy-done((bf16[2048,256]{1,0:T(8,128)(2,1)S(1)}, bf16[2048,256]{1,0:T(8,128)(2,1)}, u32[]{:S(2)}) %copy-start) | copy-done | bytes 1048600
  26.9 1.2 %copy-done.1 = bf16[2048,256]{1,0:T(8,128)(2,1)S(1)} copy-done((bf16[2048,256]{1,0:T(8,128)(2,1)S(1)}, bf16[2048,256]{1,0:T(8,128)(2,1)}, u32[]{:S(2)}) %copy-start.1) | copy-done | bytes 1048600
  28.2 1.4 %shard_map.164 = (bf16[64,512]{1,0:T(8,128)(2,1)S(1)}, f32[1024,256]{1,0:T(8,128)S(1)}, f32[16,128]{1,0:T(8,128)S(1)}) custom-call(bf16[5,2048]{1,0:T(8,128)(2,1)S(1)} %copy-done.5, bf16[2048,256]{1,0:T(8,128)(2,1)S(1)} %copy-done, bf16[2048,256]{1,0:T(8,128)(2,1)S(1)} %copy-done.1, bf16[2048,4]{1,0:T(8,128)(2,1)S(1)} %copy.18.w_dt, f32[4]{0:T(128)S(1)} %copy-done.13, ...), custom_call_target="tpu_custom_call" | custom-call | tf_op jit(solution)/shard_map/pallas_call | solution.py:329
  29.6 0.0 copy-start.2
  29.6 12.0 %all-to-all-done.received = f32[16,16,128]{2,1,0:T(8,128)S(1)} async-done(((f32[16,16,128]{2,1,0:T(8,128)}), f32[16,16,128]{2,1,0:T(8,128)S(1)}, u32[]{:S(2)}, u32[]{:S(2)}) %all-to-all-start) | async-done | bytes 131104 | tf_op jit(solution)/shard_map/all_to_all | solution.py:393
  41.6 4.9 %shard_map.165 = (f32[512,256]{1,0:T(8,128)S(1)}, f32[16,4,128]{2,1,0:T(4,128)S(1)}) custom-call(f32[16,16,128]{2,1,0:T(8,128)S(1)} %all-to-all-done.received, s32[5]{0:T(128)S(1)} %copy-done.15, bf16[64,512]{1,0:T(8,128)(2,1)S(1)} %get-tuple-element.10.table, f32[1024,256]{1,0:T(8,128)S(1)} %get-tuple-element.11.gram_values, ...), custom_call_target="tpu_custom_call" | custom-call | tf_op jit(solution)/shard_map/pallas_call | solution.py:341
  46.4 13.1 %all_to_all.20.squares = f32[16,4,128]{2,1,0:T(4,128)S(1)} all-to-all(f32[16,4,128]{2,1,0:T(4,128)S(1)} %get-tuple-element.13), channel_id=1, replica_groups=mesh['seq'=32,'chan'=16] {'chan'}, dimensions={0} | all-to-all | bytes 65536 | tf_op jit(solution)/shard_map/all_to_all | solution.py:393
  59.6 0.5 shard_map.166
  60.1 15.7 %all_to_all.21.received = bf16[4,64,2048]{2,1,0:T(8,128)(2,1)S(1)} all-to-all(bf16[4,64,2048]{2,1,0:T(8,128)(2,1)S(1)} %shard_map.166), channel_id=1, replica_groups={{0,4,8,12},{1,5,9,13},{2,6,10,14},{3,7,11,15},{16,20,24,28},{17,21,25,2..., dimensions={0} | all-to-all | bytes 2097152 | tf_op jit(solution)/shard_map/all_to_all | solution.py:393
  75.8 0.1 shard_map.167
  75.9 9.5 %all_to_all.22.received = bf16[4,16,2048]{2,1,0:T(8,128)(2,1)S(1)} all-to-all(bf16[4,16,2048]{2,1,0:T(8,128)(2,1)S(1)} %shard_map.167), channel_id=1, replica_groups={{0,1,2,3},{4,5,6,7},{8,9,10,11},{12,13,14,15},{16,17,18,19},{20,21,22,2..., dimensions={0} | all-to-all | bytes 524288 | tf_op jit(solution)/shard_map/all_to_all | solution.py:393
  85.5 0.7 shard_map.168
  (26 shorter events, 0.1 us)
Async XLA Ops:
  0.0 0.7 copy-start.11
  0.7 3.0 %collective-permute-start = (s32[2,128]{1,0:T(2,128)S(1)}, s32[2,128]{1,0:T(2,128)S(1)}, u32[]{:S(2)}, u32[]{:S(2)}) collective-permute-start(s32[2,128]{1,0:T(2,128)S(1)} %bitcast.2), channel_id=1, source_target_pairs={{0,16},{16,0},{32,48},{48,32},{64,80},{80,64},{96,112},{112,96},{1... | collective-permute-start | bytes 3080 | tf_op jit(solution)/shard_map/ppermute | solution.py:401
  3.7 0.8 copy-start.4
  4.5 0.8 copy-start.7
  6.1 18.6 %copy-start.17 = (bf16[2048,4]{0,1:T(4,128)(2,1)S(1)}, bf16[2048,4]{0,1:T(4,128)(2,1)}, u32[]{:S(2)}) copy-start(bf16[2048,4]{0,1:T(4,128)(2,1)} %param.23) | copy-start | bytes 49156
  6.1 35.4 %all-to-all-start = ((f32[16,16,128]{2,1,0:T(8,128)}), f32[16,16,128]{2,1,0:T(8,128)S(1)}, u32[]{:S(2)}, u32[]{:S(2)}) async-start(f32[16,16,128]{2,1,0:T(8,128)} %shard_map.163), calls=%async_computation | async-start | bytes 262144 | tf_op jit(solution)/shard_map/all_to_all | solution.py:393
  24.7 1.0 %copy-start.3 = (bf16[1024,64]{1,0:T(8,128)(2,1)S(1)}, bf16[1024,64]{1,0:T(8,128)(2,1)}, u32[]{:S(2)}) copy-start(bf16[1024,64]{1,0:T(8,128)(2,1)} %constant.6.clone.grams_t) | copy-start | bytes 393220
  24.8 0.9 %copy-start.5 = (bf16[5,2048]{1,0:T(8,128)(2,1)S(1)}, bf16[5,2048]{1,0:T(8,128)(2,1)}, u32[]{:S(2)}) copy-start(bf16[5,2048]{1,0:T(8,128)(2,1)} %embed.3) | copy-start | bytes 61444
  24.8 0.9 %copy-start.9 = (bf16[4,256]{1,0:T(4,128)(2,1)S(1)}, bf16[4,256]{1,0:T(4,128)(2,1)}, u32[]{:S(2)}) copy-start(bf16[4,256]{1,0:T(4,128)(2,1)} %conv_x.1) | copy-start | bytes 6148
  24.8 0.9 %copy-start.13 = (f32[4]{0:T(128)S(1)}, f32[4]{0:T(128)}, u32[]{:S(2)}) copy-start(f32[4]{0:T(128)} %dt_bias.1) | copy-start | bytes 52
  24.8 0.9 %copy-start.14 = (f32[4]{0:T(128)S(1)}, f32[4]{0:T(128)}, u32[]{:S(2)}) copy-start(f32[4]{0:T(128)} %decay.1) | copy-start | bytes 52
  25.7 1.2 %copy-start = (bf16[2048,256]{1,0:T(8,128)(2,1)S(1)}, bf16[2048,256]{1,0:T(8,128)(2,1)}, u32[]{:S(2)}) copy-start(bf16[2048,256]{1,0:T(8,128)(2,1)} %w_x.1) | copy-start | bytes 3145732
  26.9 1.2 %copy-start.1 = (bf16[2048,256]{1,0:T(8,128)(2,1)S(1)}, bf16[2048,256]{1,0:T(8,128)(2,1)}, u32[]{:S(2)}) copy-start(bf16[2048,256]{1,0:T(8,128)(2,1)} %w_z.1) | copy-start | bytes 3145732
  28.2 13.4 %copy-start.6 = (bf16[64,1024]{1,0:T(8,128)(2,1)S(1)}, bf16[64,1024]{1,0:T(8,128)(2,1)}, u32[]{:S(2)}) copy-start(bf16[64,1024]{1,0:T(8,128)(2,1)} %constant.7.clone.grams) | copy-start | bytes 393220
  28.2 13.4 %copy-start.8 = (bf16[128,256]{1,0:T(8,128)(2,1)S(1)}, bf16[128,256]{1,0:T(8,128)(2,1)}, u32[]{:S(2)}) copy-start(bf16[128,256]{1,0:T(8,128)(2,1)} %constant.8.clone.spread) | copy-start | bytes 196612
  28.2 13.4 %copy-start.10 = (bf16[4,256]{1,0:T(4,128)(2,1)S(1)}, bf16[4,256]{1,0:T(4,128)(2,1)}, u32[]{:S(2)}) copy-start(bf16[4,256]{1,0:T(4,128)(2,1)} %conv_bc.1) | copy-start | bytes 6148
  28.2 13.4 %copy-start.12 = (f32[256]{0:T(256)S(1)}, f32[256]{0:T(256)}, u32[]{:S(2)}) copy-start(f32[256]{0:T(256)} %param.29) | copy-start | bytes 3076
  28.2 13.4 %copy-start.15 = (s32[5]{0:T(128)S(1)}, s32[5]{0:T(128)}, u32[]{:S(2)}) copy-start(s32[5]{0:T(128)} %complement.1) | copy-start | bytes 64
  28.2 13.4 %copy-start.16 = (f32[4]{0:T(128)S(1)}, f32[4]{0:T(128)}, u32[]{:S(2)}) copy-start(f32[4]{0:T(128)} %d_skip.1) | copy-start | bytes 52
  29.6 30.0 %copy-start.2 = (bf16[256,2048]{1,0:T(8,128)(2,1)S(1)}, bf16[256,2048]{1,0:T(8,128)(2,1)}, u32[]{:S(2)}) copy-start(bf16[256,2048]{1,0:T(8,128)(2,1)} %w_out.1) | copy-start | bytes 3145732

commit v3 on v2

v3 whole, which is shorter than its diff:
```python
import jax
import jax.numpy as jnp
import numpy as np
from jax import lax
from jax.experimental import pallas as pl
from jax.experimental.pallas import tpu as pltpu
from jax.sharding import PartitionSpec as P

HEADS = 64
HEAD_DIM = 64
STATE = 128
CONV = 4
VOCAB = 5
ROWS = 256
OWN_HEADS = 4
OWN = OWN_HEADS * HEAD_DIM
SEQ = 32
CHAN = 16
CHIPS = SEQ // 2
LENGTH = SEQ * ROWS
LINES = LENGTH // 128
SIDE = 4
PAIR_HEADS = 2 * OWN_HEADS
PAIR = 2 * OWN
GROUP = CHAN // 2
LINE = 128
PIECE = LINE // GROUP
EPSILON = 1e-05
NONE = VOCAB
VMEM = pltpu.VMEM
SMEM = pltpu.SMEM
F32 = jnp.float32
BF16 = jnp.bfloat16


def gram_table():
    table = np.zeros((64, 1024), np.float32)
    for older in range(31):
        for newer in range(30):
            pair = lambda code: (5, 5) if code == 30 else (code // 5, code % 5)
            for tap, symbol in enumerate(pair(older) + pair(newer)):
                if symbol < VOCAB:
                    table[tap * 8 + symbol, older * 32 + newer] = 1
                    table[32 + tap * 8 + symbol, older * 32 + newer] = 1
    return table


def place():
    return lax.axis_index("seq"), lax.axis_index("chan")


def iota(shape, axis):
    return lax.broadcasted_iota(jnp.int32, shape, axis)


def fiota(shape, axis):
    return iota(shape, axis).astype(F32)


def dot(a, b, contract):
    return lax.dot_general(a, b, ((contract[:1], contract[1:]), ((), ())), preferred_element_type=F32)


def silu(x):
    return x / (1.0 + jnp.exp(-x))


def send_kernel(tokens, sibling, embed, w_bc, send):
    seq, chan = place()
    part = embed[:, pl.ds(pl.multiple_of(chan * 128, 128), 128)]
    bc = dot(part, w_bc[...], (1, 0))
    mine = tokens[...].astype(F32)
    other = sibling[...].astype(F32)
    first = lax.rem(seq, 2) == 0
    send[0, 0:VOCAB, :] = bc[:, :STATE]
    send[0, 5:7, :] = jnp.where(first, mine, other)
    send[0, 7:8, :] = jnp.zeros((1, 128), F32)
    send[0, 8 : 8 + VOCAB, :] = bc[:, STATE:]
    send[0, 13:15, :] = jnp.where(first, other, mine)
    send[0, 15:16, :] = jnp.zeros((1, 128), F32)
    block = send[0]
    for peer in range(1, CHIPS):
        send[peer] = block


def tables_kernel(embed, w_x, w_z, w_dt, params, tables):
    emb = embed[...]
    x_tab = dot(emb, w_x[...], (1, 0)).astype(BF16).astype(F32)
    z_tab = dot(emb, w_z[...], (1, 0)).astype(BF16).astype(F32)
    tables[...] = jnp.zeros(tables.shape, F32)
    tables[0:VOCAB, :] = x_tab
    tables[8 : 8 + VOCAB, :] = silu(z_tab)
    tables[16:24, :] = params[...]
    raw = dot(emb, w_dt[...], (1, 1)) + params[6:7, 0:OWN_HEADS]
    step = jnp.maximum(raw, 0.0) + jnp.log1p(jnp.exp(-jnp.abs(raw)))
    tables[24 : 24 + VOCAB, 0:OWN_HEADS] = step
    tables[24 : 24 + VOCAB, LINE : LINE + OWN_HEADS] = step * params[7:8, 0:OWN_HEADS]


def prepare_kernel(mine, other, conv_bc, grams_in, complement, tables, rows, steps):
    for side, given in enumerate((mine, other)):
        at = slice(OWN * side, OWN * (side + 1))
        x_taps = halves(taps_table(given[16:20, :], given[0:8, :]))
        tables[:, at] = x_taps
        gates = jnp.concatenate([jnp.zeros((24, OWN), F32), given[8:16, :]], 0)
        tables[:, PAIR + OWN * side : PAIR + OWN * (side + 1)] = halves(gates)
        rows[0:8, at] = given[16:24, :]
    tables[:, 2 * PAIR :] = grams_in[...]
    rows[8:12, 0 : 2 * STATE] = conv_bc[...].astype(F32)
    rows[8:12, 2 * STATE :] = jnp.zeros((4, PAIR - 2 * STATE), F32)
    rows[12:16, :] = jnp.zeros((4, PAIR), F32)
    for part in range(2):
        at = slice(LINE * part, LINE * (part + 1))
        steps[8 * part : 8 * part + 8, :] = given_steps(mine, at) + pltpu.roll(given_steps(other, at), OWN_HEADS, 1)
    lane = iota((1, LINE), 1)
    flips = jnp.zeros((1, LINE), F32)
    for symbol in range(VOCAB):
        flips = jnp.where(lane == symbol, complement[symbol].astype(F32), flips)
    steps[15:16, :] = flips


def given_steps(given, at):
    return given[24:32, at]


def before(x, steps):
    lane, line = (iota(x.shape, 1), iota(x.shape, 0))
    turned = pltpu.roll(x, steps, 1)
    over = jnp.where(line == 0, float(NONE), pltpu.roll(turned, 1, 0))
    return jnp.where(lane < steps, over, turned)


def after(x, steps):
    lane, line = (iota(x.shape, 1), iota(x.shape, 0))
    turned = pltpu.roll(x, 128 - steps, 1)
    over = jnp.where(line == LINES - 1, float(NONE), pltpu.roll(turned, LINES - 1, 0))
    return jnp.where(lane >= 128 - steps, over, turned)


def hot(symbols, count):
    return jnp.where(fiota((count, symbols.shape[1]), 0) == symbols, 1.0, 0.0)


def taps_table(taps, table):
    return jnp.concatenate([taps[k : k + 1, :] * table for k in range(CONV)], 0)


def halves(x):
    high = x.astype(BF16)
    low = (x - high.astype(F32)).astype(BF16)
    return jnp.concatenate([high.astype(F32), low.astype(F32)], 0).astype(BF16)


def scan_kernel(
    received, tables, rows, step_at, out, send,
    tok_ref, fwd_ref, back_ref,
):
    seq, chan = place()
    own_line = 2 * seq + chan // GROUP
    for chip in range(CHIPS):
        tok_ref[4 * chip : 4 * chip + 2, :] = received[chip, 5:7, :]
        tok_ref[4 * chip + 2 : 4 * chip + 4, :] = received[chip, 13:15, :]
    bc_sum = received[0]
    for chip in range(1, CHIPS):
        bc_sum = bc_sum + received[chip]
    bc_sum = jnp.where(lax.rem(iota((16, 128), 0), 8) < VOCAB, bc_sum, 0.0)
    bc_sum = bc_sum.astype(BF16).astype(F32)
    bc_tab = jnp.concatenate([bc_sum[0:8], bc_sum[8:16]], 1)
    bc_taps = halves(taps_table(rows[8:12, 0 : 2 * STATE], bc_tab))
    conv_tab = jnp.concatenate([tables[:, :PAIR], bc_taps, tables[:, PAIR : 2 * PAIR]], 1)

    tok = tok_ref[...]
    flipped = jnp.zeros(tok.shape, F32)
    for symbol in range(VOCAB):
        flipped = jnp.where(tok == float(symbol), step_at[15, symbol], flipped)
    fwd = [before(tok, 3), before(tok, 2), before(tok, 1), tok]
    back = [after(flipped, 3), after(flipped, 2), after(flipped, 1), flipped]
    for k in range(CONV):
        fwd_ref[k] = fwd[k]
        back_ref[k] = back[k]

    line = iota((LINES, 128), 0)
    ahead = line < own_line
    inside = line != own_line
    gram = [jnp.where(ahead, f, b) for f, b in zip(fwd, back)]
    older = gram[0] * 5.0 + gram[1] + jnp.where(ahead, 0.0, 32.0)
    newer = gram[2] * 5.0 + gram[3]
    newest = [jnp.logical_and(gram[3] == float(symbol), inside) for symbol in range(VOCAB)]
    marks = jnp.concatenate([jnp.where(hit, 1.0, 0.0) for hit in newest], 0).astype(BF16)
    row, column = (iota((128, 128), 0), iota((128, 128), 1))
    within = jnp.concatenate(
        [
            jnp.where(row > column, 1.0, 0.0),
            jnp.where(row < column, 1.0, 0.0),
            jnp.ones((128, 128), F32),
        ],
        1,
    ).astype(BF16)
    counts = dot(marks, within, (1, 0))
    parts = [counts[LINES * symbol : LINES * (symbol + 1)] for symbol in range(VOCAB)]
    totals = jnp.concatenate([part[:, 256:384] for part in parts], 1).astype(BF16)
    to, of = (iota((LINES, LINES), 0), iota((LINES, LINES), 1))
    between = jnp.logical_or(
        jnp.logical_and(to < of, of < own_line), jnp.logical_and(of > own_line, of < to)
    )
    lines_between = dot(jnp.where(between, 1.0, 0.0).astype(BF16), totals, (1, 0))
    passed = [
        jnp.where(ahead, part[:, 0:128], part[:, 128:256]) + lines_between[:, 128 * k : 128 * k + 128]
        for k, part in enumerate(parts)
    ]
    weights = []
    for head in range(PAIR_HEADS):
        lost = jnp.zeros((LINES, 128), F32)
        own_step = jnp.zeros((LINES, 128), F32)
        for symbol in range(VOCAB):
            lost = lost + step_at[8 + symbol, head] * passed[symbol]
            own_step = jnp.where(newest[symbol], step_at[symbol, head], own_step)
        weights.append(own_step * jnp.exp(-lost))

    sums = jnp.zeros((64, 32 * PAIR_HEADS), F32)
    for first in range(0, LINES, 2):
        left, right = ([], [])
        for at in (first, first + 1):
            left.append(hot(older[at : at + 1], 64))
            hits = fiota((32, 128), 0) == newer[at : at + 1]
            right.append(
                jnp.concatenate([jnp.where(hits, w[at : at + 1], 0.0) for w in weights], 0)
            )
        sums = sums + dot(
            jnp.concatenate(left, 1).astype(BF16), jnp.concatenate(right, 1).astype(BF16), (1, 1)
        )

    gram_b = silu(dot(bc_taps[:, :STATE], tables[:, 2 * PAIR :], (0, 0))).astype(BF16)
    wide_code = (32, 32 * PAIR_HEADS)
    same = jnp.where(lax.rem(iota(wide_code, 1), 32) == iota(wide_code, 0), 1.0, 0.0)
    gram_values = silu(dot(tables[:, 2 * PAIR :], tables[:, :PAIR], (0, 0))).astype(BF16)
    shape = (32 * PAIR_HEADS, PAIR)
    spread = jnp.where(iota(shape, 0) // 32 == iota(shape, 1) // HEAD_DIM, 1.0, 0.0).astype(BF16)
    states = []
    for strand in range(2):
        placed = jnp.concatenate(
            [sums[32 * strand + code : 32 * strand + code + 1] * same for code in range(32)], 0
        )
        wide = dot(placed.astype(BF16), spread, (1, 0))
        states.append(dot(gram_b, wide.astype(BF16) * gram_values, (1, 0)))

    hots = [
        jnp.concatenate([hot(ref[tap, pl.ds(own_line, 1), :], 8) for tap in range(CONV)], 0)
        for ref in (fwd_ref, back_ref)
    ]
    hots = jnp.concatenate(hots, 1)
    mixed = dot(jnp.concatenate([hots, hots], 0).astype(BF16), conv_tab, (0, 0))
    gate = mixed[:, PAIR + 2 * STATE :]
    mixed = silu(mixed[:, : PAIR + 2 * STATE])
    head_of = iota((1, OWN), 1) // HEAD_DIM
    row, column = (iota((LINE, LINE), 0), iota((LINE, LINE), 1))
    squares = []
    for strand in range(2):
        own = slice(LINE * strand, LINE * (strand + 1))
        b_in = mixed[own, PAIR : PAIR + STATE].astype(BF16)
        c_out = mixed[own, PAIR + STATE :]
        causal = row >= column if strand == 0 else row <= column
        order = row <= column if strand == 0 else row >= column
        symbols = hots[24:32, own]
        seen = dot(symbols.astype(BF16), jnp.where(order, 1.0, 0.0).astype(BF16), (1, 0))
        cumul, step = ([], [])
        for head in range(PAIR_HEADS):
            total = jnp.zeros((1, LINE), F32)
            own_step = jnp.zeros((1, LINE), F32)
            for symbol in range(VOCAB):
                total = total - step_at[8 + symbol, head] * seen[symbol : symbol + 1]
                own_step = own_step + step_at[symbol, head] * symbols[symbol : symbol + 1]
            cumul.append(total)
            step.append(own_step)
        across = jnp.transpose(
            jnp.concatenate(cumul + [jnp.zeros((LINE - PAIR_HEADS, LINE), F32)], 0)
        )
        scores = dot(c_out.astype(BF16), b_in, (1, 1))
        squared = jnp.zeros((LINE, LINE), F32)
        for side in range(2):
            at = slice(OWN * side, OWN * (side + 1))
            values = mixed[own, at]
            left, right, tail_left, tail_right = ([], [], [], [])
            for near in range(OWN_HEADS):
                head = OWN_HEADS * side + near
                column_of = across[:, head : head + 1]
                decayed = jnp.exp(jnp.where(causal, column_of - cumul[head], -1e30))
                left.append((decayed * (scores * step[head])).astype(BF16))
                right.append(jnp.where(head_of == near, values, 0.0).astype(BF16))
                tail_left.append((c_out * jnp.exp(column_of)).astype(BF16))
                tail_right.append(jnp.where(head_of == near, states[strand][:, at], 0.0).astype(BF16))
            ssd = dot(
                jnp.concatenate(left + tail_left, 1), jnp.concatenate(right + tail_right, 0), (1, 0)
            )
            gated = (ssd + values * rows[5:6, at]) * gate[own, at]
            out[own, at] = gated * rows[4:5, at]
            squared = squared + gated[:, :LINE] * gated[:, :LINE] + gated[:, LINE:] * gated[:, LINE:]
        squares.append(jnp.sum(jnp.transpose(squared), axis=0, keepdims=True))
    mine = jnp.concatenate(squares, 0)
    for peer in range(GROUP):
        send[peer] = mine


def project_kernel(squares, gated, w_own, w_other, out):
    total = squares[0]
    for peer in range(1, GROUP):
        total = total + squares[peer]
    scale = lax.rsqrt(total / (HEADS * HEAD_DIM) + EPSILON)
    combined = jnp.zeros((LINE, PAIR), F32)
    for strand in range(2):
        down = jnp.transpose(jnp.broadcast_to(scale[strand : strand + 1], (LINE, LINE)))
        block = gated[LINE * strand : LINE * (strand + 1), :]
        normed = block * jnp.concatenate([down] * (PAIR // LINE), 1)
        combined = combined + normed.astype(BF16).astype(F32)
    combined = combined.astype(BF16)
    mixed = dot(combined[:, :OWN], w_own[...], (1, 0)) + dot(combined[:, OWN:], w_other[...], (1, 0))
    out[...] = mixed.astype(BF16).reshape(out.shape)


def sum_kernel(received, out):
    total = received[0].astype(F32)
    for peer in range(1, GROUP):
        total = total + received[peer].astype(F32)
    out[...] = total.astype(BF16)


def call(kernel, outs, kinds, work, limit, scratch=()):
    return pl.pallas_call(
        kernel,
        out_shape=outs,
        in_specs=[pl.BlockSpec(memory_space=kind) for kind in kinds],
        out_specs=jax.tree.map(lambda _: pl.BlockSpec(memory_space=VMEM), outs),
        scratch_shapes=scratch,
        compiler_params=pltpu.CompilerParams(vmem_limit_bytes=limit * 2**20),
        cost_estimate=pl.CostEstimate(flops=work * 10**9, bytes_accessed=work * 2**20, transcendentals=0),
    )


def make_send(*args):
    return call(send_kernel, jax.ShapeDtypeStruct((CHIPS, 16, 128), F32), [VMEM] * 4, 1, 16)(*args)


def make_tables(*args):
    return call(tables_kernel, jax.ShapeDtypeStruct((32, OWN), F32), [VMEM] * 5, 1, 16)(*args)


def make_prepare(mine, other, conv_bc, complement):
    grams = gram_table()
    return call(
        prepare_kernel,
        (
            jax.ShapeDtypeStruct((64, 2 * PAIR + 1024), BF16),
            jax.ShapeDtypeStruct((16, PAIR), F32),
            jax.ShapeDtypeStruct((16, LINE), F32),
        ),
        [VMEM] * 4 + [SMEM],
        1,
        16,
    )(mine, other, conv_bc, jnp.asarray(grams, BF16), complement)


def make_scan(received, prepared):
    return call(
        scan_kernel,
        (
            jax.ShapeDtypeStruct((2 * LINE, PAIR), F32),
            jax.ShapeDtypeStruct((GROUP, 2, LINE), F32),
        ),
        [VMEM] * 3 + [SMEM],
        7,
        24,
        [
            pltpu.VMEM((LINES, 128), F32),
            pltpu.VMEM((CONV, LINES, 128), F32),
            pltpu.VMEM((CONV, LINES, 128), F32),
        ],
    )(received, *prepared)


def make_project(squares, gated, w_own, w_other):
    return call(
        project_kernel, jax.ShapeDtypeStruct((GROUP, PIECE, w_own.shape[1]), BF16), [VMEM] * 4, 1, 16
    )(squares, gated, w_own, w_other)


def make_sum(received):
    return call(sum_kernel, jax.ShapeDtypeStruct(received.shape[1:], BF16), [VMEM], 1, 16)(received)


def device(seq, chan):
    return seq * CHAN + chan


def mixed_groups():
    side = range(SIDE)
    return [
        [
            device(2 * (SIDE * y + high) + core, (y + right) % SIDE * SIDE + (high + up) % SIDE)
            for y in side
            for high in side
        ]
        for core in range(2)
        for right in side
        for up in side
    ]


def row_groups():
    return [list(range(GROUP)), list(range(GROUP, CHAN))]


def with_partner(value):
    pairs = [(x * SIDE + z, (SIDE - 1 - x) * SIDE + z) for x in range(SIDE) for z in range(SIDE)]
    return lax.ppermute(value, "chan", pairs)


def exchange(value, axes, groups=None):
    return lax.all_to_all(value, axes, 0, 0, tiled=True, axis_index_groups=groups)


def per_device(
    tokens, complement, embed, w_x, w_z, w_bc, w_dt, dt_bias, decay_rate, d_skip, conv_x, conv_bc,
    norm_gain, w_out,
):
    own = tokens.reshape(2, 128)
    sibling = lax.ppermute(own, "seq", [(source, source ^ 1) for source in range(SEQ)])
    send = make_send(own, sibling, embed, w_bc)
    send, embed, conv_x, norm_gain, d_skip, dt_bias, decay_rate = lax.optimization_barrier(
        (send, embed, conv_x, norm_gain, d_skip, dt_bias, decay_rate)
    )
    received = exchange(send, ("seq", "chan"), mixed_groups())
    by_head = jnp.pad(jnp.stack([dt_bias, decay_rate]), ((0, 0), (0, OWN - OWN_HEADS)))
    by_channel = jnp.stack([norm_gain, jnp.repeat(d_skip, HEAD_DIM)])
    params = jnp.concatenate([conv_x.astype(F32), by_channel, by_head], 0)
    tables = make_tables(embed, w_x, w_z, w_dt.T, params)
    other, w_own = lax.optimization_barrier((with_partner(tables), w_out))
    w_other = with_partner(w_own)
    prepared = make_prepare(tables, other, conv_bc, complement)
    gated, squares = make_scan(received, prepared)
    partial = make_project(exchange(squares, "chan", row_groups()), gated, w_own, w_other)
    return make_sum(exchange(partial, "chan", row_groups()))


def solution(mesh):
    placed = (
        P("seq"),
        P(),
        P(),
        P(None, "chan"),
        P(None, "chan"),
        P("chan", None),
        P(None, "chan"),
        P("chan"),
        P("chan"),
        P("chan"),
        P(None, "chan"),
        P(),
        P("chan"),
        P("chan", None),
    )
    return jax.shard_map(
        per_device, mesh=mesh, in_specs=placed, out_specs=P(("seq", "chan"), None), check_vma=False
    )
```

time: 86.8 us -> 81 us (0.933)
  the two profiles are of different devices: /device:TPU:2 before, /device:TPU:8 now
where the time goes in v3:
time: 81 us; the launch traced here: 80.4 us
  blocking collectives  28.7 us (35%)
  starting transfers between devices  26.4 us (33%)
  waiting for transfers between devices  11.5 us (14%)
  Pallas kernels  9.97 us (12%)
  local copies, waits for them, and re-layouts  3.68 us (5%)
    all_to_all x2, blocking collectives, exchange(): lax.all_to_all(value, axes, 0, 0, tiled=True, axis_index_groups=groups)  28.7 us
    all_to_all x1, starting transfers between devices, exchange(): lax.all_to_all(value, axes, 0, 0, tiled=True, axis_index_groups=groups)  20.5 us
    ppermute x2, waiting for transfers between devices, with_partner(): return lax.ppermute(value, 'chan', pairs)  7.53 us
    pallas_call x1, Pallas kernels, make_scan(): call(scan_kernel, (jax.ShapeDtypeStruct((2 * LINE, PAIR), F32), jax.Shape...  6.91 us
    ppermute x2, starting transfers between devices, with_partner(): return lax.ppermute(value, 'chan', pairs)  3.84 us
    unnamed x32, local copies, waits for them, and re-layouts  3.53 us
    all_to_all x1, waiting for transfers between devices, exchange(): lax.all_to_all(value, axes, 0, 0, tiled=True, axis_index_groups=groups)  2.85 us
    ppermute x1, starting transfers between devices, per_device(): lax.ppermute(own, 'seq', [(source, source ^ 1) for source in range(SEQ)])  2.04 us
  transfers between devices with their start and end apart: 4, of which 4 were waited for; matrix products, arithmetic and copies ran while one was open for 0% of the time, Pallas kernels for 10%

profile of v3, /device:TPU:8, one launch (start us, length us, event | category | flops | bytes accessed | tf_op | source)
XLA Modules:
  0.0 80.4 jit_solution(642672831921522602)
XLA Ops:
  0.0 0.7 copy-done.8
  0.7 2.0 %collective-permute-start = (s32[2,128]{1,0:T(2,128)S(1)}, s32[2,128]{1,0:T(2,128)S(1)}, u32[]{:S(2)}, u32[]{:S(2)}) collective-permute-start(s32[2,128]{1,0:T(2,128)S(1)} %bitcast.6), channel_id=1, source_target_pairs={{0,16},{16,0},{32,48},{48,32},{64,80},{80,64},{96,112},{112,96},{1... | collective-permute-start | bytes 3080 | tf_op jit(solution)/shard_map/ppermute | solution.py:426
  2.7 1.1 %collective-permute-done.sibling = s32[2,128]{1,0:T(2,128)S(1)} collective-permute-done((s32[2,128]{1,0:T(2,128)S(1)}, s32[2,128]{1,0:T(2,128)S(1)}, u32[]{:S(2)}, u32[]{:S(2)}) %collective-permute-start) | collective-permute-done | bytes 1056 | tf_op jit(solution)/shard_map/ppermute | solution.py:426
  3.8 0.8 %copy-done.3 = bf16[128,256]{1,0:T(8,128)(2,1)S(1)} copy-done((bf16[128,256]{1,0:T(8,128)(2,1)S(1)}, bf16[128,256]{1,0:T(8,128)(2,1)}, u32[]{:S(2)}) %copy-start.3) | copy-done | bytes 65560
  4.7 0.8 copy-done.4
  5.4 0.8 shard_map.145
  6.2 0.1 broadcast_in_dim.3
  6.3 0.1 stack_reshape.3
  6.4 0.6 copy-done.11
  7.0 0.0 copy-start.5
  7.0 20.5 %all-to-all-start = ((f32[16,16,128]{2,1,0:T(8,128)}), f32[16,16,128]{2,1,0:T(8,128)S(1)}, u32[]{:S(2)}, u32[]{:S(2)}) async-start(f32[16,16,128]{2,1,0:T(8,128)} %shard_map.145), calls=%async_computation | async-start | bytes 262144 | tf_op jit(solution)/shard_map/all_to_all | solution.py:418
  27.6 0.6 copy-done.6
  28.2 0.4 shard_map.146.mine
  28.6 1.9 %collective-permute-start.1 = (f32[32,256]{1,0:T(8,128)S(1)}, f32[32,256]{1,0:T(8,128)S(1)}, u32[]{:S(2)}, u32[]{:S(2)}) collective-permute-start(f32[32,256]{1,0:T(8,128)S(1)} %shard_map.146.mine), channel_id=1, source_target_pairs={{0,12},{1,13},{2,14},{3,15},{4,8},{5,9},{6,10},{7,11},{8,4},{9,5},... | collective-permute-start | bytes 98312 | tf_op jit(solution)/shard_map/ppermute | solution.py:414
  30.6 5.1 %collective-permute-done.1.other = f32[32,256]{1,0:T(8,128)S(1)} collective-permute-done((f32[32,256]{1,0:T(8,128)S(1)}, f32[32,256]{1,0:T(8,128)S(1)}, u32[]{:S(2)}, u32[]{:S(2)}) %collective-permute-start.1) | collective-permute-done | bytes 32800 | tf_op jit(solution)/shard_map/ppermute | solution.py:414
  35.7 1.9 %collective-permute-start.2 = (bf16[256,2048]{1,0:T(8,128)(2,1)S(1)}, bf16[256,2048]{1,0:T(8,128)(2,1)S(1)}, u32[]{:S(2)}, u32[]{:S(2)}) collective-permute-start(bf16[256,2048]{1,0:T(8,128)(2,1)S(1)} %copy-done.2), channel_id=1, source_target_pairs={{0,12},{1,13},{2,14},{3,15},{4,8},{5,9},{6,10},{7,11},{8,4},{9,5},... | collective-permute-start | bytes 3145736 | tf_op jit(solution)/shard_map/ppermute | solution.py:414
  37.6 0.6 shard_map.147
  38.2 2.9 %all-to-all-done.received = f32[16,16,128]{2,1,0:T(8,128)S(1)} async-done(((f32[16,16,128]{2,1,0:T(8,128)}), f32[16,16,128]{2,1,0:T(8,128)S(1)}, u32[]{:S(2)}, u32[]{:S(2)}) %all-to-all-start) | async-done | bytes 131104 | tf_op jit(solution)/shard_map/all_to_all | solution.py:418
  41.1 6.9 %shard_map.148 = (f32[256,512]{1,0:T(8,128)S(1)}, f32[8,2,128]{2,1,0:T(2,128)S(1)}) custom-call(f32[16,16,128]{2,1,0:T(8,128)S(1)} %all-to-all-done.received, bf16[64,2048]{1,0:T(8,128)(2,1)S(1)} %get-tuple-element.27.tables, f32[16,512]{1,0:T(8,128)S(1)} %get-tuple-element.28.rows, f32[16,128]{1,0:T(8,128)S(1)} %get-tuple-element.29.step_at), custom_call_target="tpu_custom_call" | custom-call | flops 7000000000 | bytes 7340032 | tf_op jit(solution)/shard_map/pallas_call | solution.py:363
  48.0 12.2 %all_to_all.15.squares = f32[8,2,128]{2,1,0:T(2,128)S(1)} all-to-all(f32[8,2,128]{2,1,0:T(2,128)S(1)} %get-tuple-element.30), channel_id=1, replica_groups={{0,1,2,3,4,5,6,7},{8,9,10,11,12,13,14,15},{16,17,18,19,20,21,22,23},{24..., dimensions={0} | all-to-all | bytes 16384 | tf_op jit(solution)/shard_map/all_to_all | solution.py:418
  60.3 2.4 %collective-permute-done.2.w_other = bf16[256,2048]{1,0:T(8,128)(2,1)S(1)} collective-permute-done((bf16[256,2048]{1,0:T(8,128)(2,1)S(1)}, bf16[256,2048]{1,0:T(8,128)(2,1)S(1)}, u32[]{:S(2)}, u32[]{:S(2)}) %collective-permute-start.2) | collective-permute-done | bytes 1048608 | tf_op jit(solution)/shard_map/ppermute | solution.py:414
  62.7 0.5 shard_map.149
  63.2 16.5 %all_to_all.16.received = bf16[8,16,2048]{2,1,0:T(8,128)(2,1)S(1)} all-to-all(bf16[8,16,2048]{2,1,0:T(8,128)(2,1)S(1)} %shard_map.149), channel_id=1, replica_groups={{0,1,2,3,4,5,6,7},{8,9,10,11,12,13,14,15},{16,17,18,19,20,21,22,23},{24..., dimensions={0} | all-to-all | bytes 1048576 | tf_op jit(solution)/shard_map/all_to_all | solution.py:418
  79.7 0.7 shard_map.150
  (29 shorter events, 0.1 us)
Async XLA Ops:
  0.0 0.7 copy-start.8
  0.0 6.2 %copy-start.13 = (f32[4]{0:T(128)S(1)}, f32[4]{0:T(128)}, u32[]{:S(2)}) copy-start(f32[4]{0:T(128)} %param.24) | copy-start | bytes 52
  0.7 26.9 %copy-start = (bf16[2048,256]{1,0:T(8,128)(2,1)S(1)}, bf16[2048,256]{1,0:T(8,128)(2,1)}, u32[]{:S(2)}) copy-start(bf16[2048,256]{1,0:T(8,128)(2,1)} %w_x.1) | copy-start | bytes 3145732
  0.7 26.9 %copy-start.1 = (bf16[2048,256]{1,0:T(8,128)(2,1)S(1)}, bf16[2048,256]{1,0:T(8,128)(2,1)}, u32[]{:S(2)}) copy-start(bf16[2048,256]{1,0:T(8,128)(2,1)} %w_z.1) | copy-start | bytes 3145732
  0.7 3.2 %collective-permute-start = (s32[2,128]{1,0:T(2,128)S(1)}, s32[2,128]{1,0:T(2,128)S(1)}, u32[]{:S(2)}, u32[]{:S(2)}) collective-permute-start(s32[2,128]{1,0:T(2,128)S(1)} %bitcast.6), channel_id=1, source_target_pairs={{0,16},{16,0},{32,48},{48,32},{64,80},{80,64},{96,112},{112,96},{1... | collective-permute-start | bytes 3080 | tf_op jit(solution)/shard_map/ppermute | solution.py:426
  3.8 0.8 %copy-start.3 = (bf16[128,256]{1,0:T(8,128)(2,1)S(1)}, bf16[128,256]{1,0:T(8,128)(2,1)}, u32[]{:S(2)}) copy-start(bf16[128,256]{1,0:T(8,128)(2,1)} %w_bc.1) | copy-start | bytes 196612
  4.7 0.8 copy-start.4
  6.3 0.7 copy-start.11
  7.0 20.5 %copy-start.14 = (f32[4]{0:T(128)S(1)}, f32[4]{0:T(128)}, u32[]{:S(2)}) copy-start(f32[4]{0:T(128)} %param.23) | copy-start | bytes 52
  7.0 20.5 %copy-start.15 = (f32[4]{0:T(128)S(1)}, f32[4]{0:T(128)}, u32[]{:S(2)}) copy-start(f32[4]{0:T(128)} %param.22) | copy-start | bytes 52
  7.0 20.5 %copy-start.12 = (f32[256]{0:T(256)S(1)}, f32[256]{0:T(256)}, u32[]{:S(2)}) copy-start(f32[256]{0:T(256)} %param.27) | copy-start | bytes 3076
  7.0 20.6 %copy-start.5 = (bf16[5,2048]{1,0:T(8,128)(2,1)S(1)}, bf16[5,2048]{1,0:T(8,128)(2,1)}, u32[]{:S(2)}) copy-start(bf16[5,2048]{1,0:T(8,128)(2,1)} %embed.2) | copy-start | bytes 61444
  7.0 34.1 %all-to-all-start = ((f32[16,16,128]{2,1,0:T(8,128)}), f32[16,16,128]{2,1,0:T(8,128)S(1)}, u32[]{:S(2)}, u32[]{:S(2)}) async-start(f32[16,16,128]{2,1,0:T(8,128)} %shard_map.145), calls=%async_computation | async-start | bytes 262144 | tf_op jit(solution)/shard_map/all_to_all | solution.py:418
  27.5 0.7 copy-start.6
  28.2 7.5 %copy-start.2 = (bf16[256,2048]{1,0:T(8,128)(2,1)S(1)}, bf16[256,2048]{1,0:T(8,128)(2,1)}, u32[]{:S(2)}) copy-start(bf16[256,2048]{1,0:T(8,128)(2,1)} %w_own) | copy-start | bytes 3145732
  28.2 9.4 %copy-start.7 = (bf16[4,256]{1,0:T(4,128)(2,1)S(1)}, bf16[4,256]{1,0:T(4,128)(2,1)}, u32[]{:S(2)}) copy-start(bf16[4,256]{1,0:T(4,128)(2,1)} %conv_bc.1) | copy-start | bytes 6148
  28.2 9.4 %copy-start.9 = (s32[5]{0:T(128)S(1)}, s32[5]{0:T(128)}, u32[]{:S(2)}) copy-start(s32[5]{0:T(128)} %complement.1) | copy-start | bytes 64
  28.2 9.4 %copy-start.10 = (bf16[64,1024]{1,0:T(8,128)(2,1)S(1)}, bf16[64,1024]{1,0:T(8,128)(2,1)}, u32[]{:S(2)}) copy-start(bf16[64,1024]{1,0:T(8,128)(2,1)} %constant.5.clone.grams_in) | copy-start | bytes 393220
  28.6 7.0 %collective-permute-start.1 = (f32[32,256]{1,0:T(8,128)S(1)}, f32[32,256]{1,0:T(8,128)S(1)}, u32[]{:S(2)}, u32[]{:S(2)}) collective-permute-start(f32[32,256]{1,0:T(8,128)S(1)} %shard_map.146.mine), channel_id=1, source_target_pairs={{0,12},{1,13},{2,14},{3,15},{4,8},{5,9},{6,10},{7,11},{8,4},{9,5},... | collective-permute-start | bytes 98312 | tf_op jit(solution)/shard_map/ppermute | solution.py:414
  35.7 27.0 %collective-permute-start.2 = (bf16[256,2048]{1,0:T(8,128)(2,1)S(1)}, bf16[256,2048]{1,0:T(8,128)(2,1)S(1)}, u32[]{:S(2)}, u32[]{:S(2)}) collective-permute-start(bf16[256,2048]{1,0:T(8,128)(2,1)S(1)} %copy-done.2), channel_id=1, source_target_pairs={{0,12},{1,13},{2,14},{3,15},{4,8},{5,9},{6,10},{7,11},{8,4},{9,5},... | collective-permute-start | bytes 3145736 | tf_op jit(solution)/shard_map/ppermute | solution.py:414

commit v4 on v3

--- a/solution.py
+++ b/solution.py
@@ -217,18 +217,21 @@
             own_step = jnp.where(newest[symbol], step_at[symbol, head], own_step)
         weights.append(own_step * jnp.exp(-lost))
 
-    sums = jnp.zeros((64, 32 * PAIR_HEADS), F32)
+    older_down = jnp.transpose(jnp.concatenate([older, older], 0))
+    lanes = fiota((128, 64), 1)
+    sums = jnp.zeros((32 * PAIR_HEADS, 64), F32)
     for first in range(0, LINES, 2):
         left, right = ([], [])
         for at in (first, first + 1):
-            left.append(hot(older[at : at + 1], 64))
+            left.append(jnp.where(lanes == older_down[:, at : at + 1], 1.0, 0.0))
             hits = fiota((32, 128), 0) == newer[at : at + 1]
             right.append(
                 jnp.concatenate([jnp.where(hits, w[at : at + 1], 0.0) for w in weights], 0)
             )
         sums = sums + dot(
-            jnp.concatenate(left, 1).astype(BF16), jnp.concatenate(right, 1).astype(BF16), (1, 1)
+            jnp.concatenate(right, 1).astype(BF16), jnp.concatenate(left, 0).astype(BF16), (1, 0)
         )
+    sums = jnp.transpose(jnp.concatenate([sums, sums], 1))[0:64]
 
     gram_b = silu(dot(bc_taps[:, :STATE], tables[:, 2 * PAIR :], (0, 0))).astype(BF16)
     wide_code = (32, 32 * PAIR_HEADS)
@@ -301,7 +304,9 @@
         send[peer] = mine
 
 
-def project_kernel(squares, gated, w_own, w_other, out):
+def project_kernel(squares, gated, w_own, w_near, w_far, out):
+    seq, _ = place()
+    first = lax.rem(seq, 2) == 0
     total = squares[0]
     for peer in range(1, GROUP):
         total = total + squares[peer]
@@ -312,8 +317,11 @@
         block = gated[LINE * strand : LINE * (strand + 1), :]
         normed = block * jnp.concatenate([down] * (PAIR // LINE), 1)
         combined = combined + normed.astype(BF16).astype(F32)
-    combined = combined.astype(BF16)
-    mixed = dot(combined[:, :OWN], w_own[...], (1, 0)) + dot(combined[:, OWN:], w_other[...], (1, 0))
+    top, end = (combined[:, OWN : OWN + LINE], combined[:, OWN + LINE :])
+    near, far = (jnp.where(first, top, end), jnp.where(first, end, top))
+    mixed = dot(combined[:, :OWN].astype(BF16), w_own[...], (1, 0))
+    mixed = mixed + dot(near.astype(BF16), w_near[...], (1, 0))
+    mixed = mixed + dot(far.astype(BF16), w_far[...], (1, 0))
     out[...] = mixed.astype(BF16).reshape(out.shape)
 
 
@@ -377,10 +385,11 @@
     )(received, *prepared)
 
 
-def make_project(squares, gated, w_own, w_other):
-    return call(
-        project_kernel, jax.ShapeDtypeStruct((GROUP, PIECE, w_own.shape[1]), BF16), [VMEM] * 4, 1, 16
-    )(squares, gated, w_own, w_other)
+def make_project(squares, gated, *weights):
+    shape = (GROUP, PIECE, weights[0].shape[1])
+    return call(project_kernel, jax.ShapeDtypeStruct(shape, BF16), [VMEM] * 5, 1, 16)(
+        squares, gated, *weights
+    )
 
 
 def make_sum(received):
@@ -414,6 +423,10 @@
     return lax.ppermute(value, "chan", pairs)
 
 
+def with_sibling(value):
+    return lax.ppermute(value, "seq", [(source, source ^ 1) for source in range(SEQ)])
+
+
 def exchange(value, axes, groups=None):
     return lax.all_to_all(value, axes, 0, 0, tiled=True, axis_index_groups=groups)
 
@@ -423,8 +436,7 @@
     norm_gain, w_out,
 ):
     own = tokens.reshape(2, 128)
-    sibling = lax.ppermute(own, "seq", [(source, source ^ 1) for source in range(SEQ)])
-    send = make_send(own, sibling, embed, w_bc)
+    send = make_send(own, with_sibling(own), embed, w_bc)
     send, embed, conv_x, norm_gain, d_skip, dt_bias, decay_rate = lax.optimization_barrier(
         (send, embed, conv_x, norm_gain, d_skip, dt_bias, decay_rate)
     )
@@ -433,11 +445,13 @@
     by_channel = jnp.stack([norm_gain, jnp.repeat(d_skip, HEAD_DIM)])
     params = jnp.concatenate([conv_x.astype(F32), by_channel, by_head], 0)
     tables = make_tables(embed, w_x, w_z, w_dt.T, params)
-    other, w_own = lax.optimization_barrier((with_partner(tables), w_out))
-    w_other = with_partner(w_own)
+    half = lax.dynamic_slice_in_dim(w_out, lax.axis_index("seq") % 2 * LINE, LINE, 0)
+    w_near = with_partner(half)
+    other, w_near = lax.optimization_barrier((with_partner(tables), w_near))
+    w_far = with_sibling(w_near)
     prepared = make_prepare(tables, other, conv_bc, complement)
     gated, squares = make_scan(received, prepared)
-    partial = make_project(exchange(squares, "chan", row_groups()), gated, w_own, w_other)
+    partial = make_project(exchange(squares, "chan", row_groups()), gated, w_out, w_near, w_far)
     return make_sum(exchange(partial, "chan", row_groups()))
 
 

time: 81 us -> 78.8 us (0.973)
  the two profiles are of different devices: /device:TPU:8 before, /device:TPU:2 now
where the time goes in v4:
time: 78.8 us; the launch traced here: 78.4 us
  starting transfers between devices  29.1 us (37%)
  blocking collectives  27.1 us (34%)
  waiting for transfers between devices  9.87 us (13%)
  Pallas kernels  9.62 us (12%)
  local copies, waits for them, and re-layouts  2.55 us (3%)
    all_to_all x2, blocking collectives, exchange(): lax.all_to_all(value, axes, 0, 0, tiled=True, axis_index_groups=groups)  27.1 us
    all_to_all x1, starting transfers between devices, exchange(): lax.all_to_all(value, axes, 0, 0, tiled=True, axis_index_groups=groups)  18.1 us
    ppermute x2, starting transfers between devices, with_partner(): return lax.ppermute(value, 'chan', pairs)  6.95 us
    all_to_all x1, waiting for transfers between devices, exchange(): lax.all_to_all(value, axes, 0, 0, tiled=True, axis_index_groups=groups)  6.51 us
    pallas_call x1, Pallas kernels, make_scan(): call(scan_kernel, (jax.ShapeDtypeStruct((2 * LINE, PAIR), F32), jax.Shape...  6.43 us
    ppermute x2, starting transfers between devices, with_sibling(): lax.ppermute(value, 'seq', [(source, source ^ 1) for source in range(SEQ)])  3.96 us
    ppermute x2, waiting for transfers between devices, with_partner(): return lax.ppermute(value, 'chan', pairs)  2.25 us
  transfers between devices with their start and end apart: 5, of which 3 were waited for; matrix products, arithmetic and copies ran while one was open for 0% of the time, Pallas kernels for 11%

profile of v4, /device:TPU:2, one launch (start us, length us, event | category | flops | bytes accessed | tf_op | source)
XLA Modules:
  0.0 78.4 jit_solution(16652522798033162598)
XLA Ops:
  0.0 1.1 %constant_dynamic-slice_fusion = bf16[128,2048]{1,0:T(8,128)(2,1)S(1)} fusion(bf16[256,2048]{1,0:T(8,128)(2,1)} %w_own.1, s32[]{:T(128)S(6)} %select_n.11), kind=kLoop, calls=%fused_computation.2 | loop fusion | bytes 1048580 | tf_op jit(solution)/shard_map/dynamic_slice | solution.py:448
  1.1 0.0 copy-start.7
  1.1 3.4 %collective-permute-start.2 = (bf16[128,2048]{1,0:T(8,128)(2,1)S(1)}, bf16[128,2048]{1,0:T(8,128)(2,1)S(1)}, u32[]{:S(2)}, u32[]{:S(2)}) collective-permute-start(bf16[128,2048]{1,0:T(8,128)(2,1)S(1)} %constant_dynamic-slice_fusion), channel_id=1, source_target_pairs={{0,12},{1,13},{2,14},{3,15},{4,8},{5,9},{6,10},{7,11},{8,4},{9,5},... | collective-permute-start | bytes 1572872 | tf_op jit(solution)/shard_map/ppermute | solution.py:423
  4.5 0.0 copy-start.1
  4.6 0.0 copy-start.2
  4.6 2.1 %collective-permute-start = (s32[2,128]{1,0:T(2,128)S(1)}, s32[2,128]{1,0:T(2,128)S(1)}, u32[]{:S(2)}, u32[]{:S(2)}) collective-permute-start(s32[2,128]{1,0:T(2,128)S(1)} %bitcast.6), channel_id=1, source_target_pairs={{0,16},{16,0},{32,48},{48,32},{64,80},{80,64},{96,112},{112,96},{1... | collective-permute-start | bytes 3080 | tf_op jit(solution)/shard_map/ppermute | solution.py:427
  6.6 1.1 %collective-permute-done.sibling = s32[2,128]{1,0:T(2,128)S(1)} collective-permute-done((s32[2,128]{1,0:T(2,128)S(1)}, s32[2,128]{1,0:T(2,128)S(1)}, u32[]{:S(2)}, u32[]{:S(2)}) %collective-permute-start) | collective-permute-done | bytes 1056 | tf_op jit(solution)/shard_map/ppermute | solution.py:427
  7.7 0.8 %shard_map.145 = f32[16,16,128]{2,1,0:T(8,128)} custom-call(s32[2,128]{1,0:T(2,128)S(1)} %bitcast.7, s32[2,128]{1,0:T(2,128)S(1)} %collective-permute-done.sibling, bf16[5,2048]{1,0:T(8,128)(2,1)S(1)} %copy-done.4, bf16[128,256]{1,0:T(8,128)(2,1)S(1)} %copy-done.3), custom_call_target="tpu_custom_call" | custom-call | flops 1000000000 | bytes 1048576 | tf_op jit(solution)/shard_map/pallas_call | solution.py:348
  8.5 18.1 %all-to-all-start = ((f32[16,16,128]{2,1,0:T(8,128)}), f32[16,16,128]{2,1,0:T(8,128)S(1)}, u32[]{:S(2)}, u32[]{:S(2)}) async-start(f32[16,16,128]{2,1,0:T(8,128)} %shard_map.145), calls=%async_computation | async-start | bytes 262144 | tf_op jit(solution)/shard_map/all_to_all | solution.py:431
  26.7 0.1 broadcast_in_dim.3
  26.8 0.1 stack_reshape.3
  26.9 0.6 copy-done.10
  27.5 0.6 copy-done.5
  28.2 0.4 shard_map.146.mine
  28.6 3.6 %collective-permute-start.1 = (f32[32,256]{1,0:T(8,128)S(1)}, f32[32,256]{1,0:T(8,128)S(1)}, u32[]{:S(2)}, u32[]{:S(2)}) collective-permute-start(f32[32,256]{1,0:T(8,128)S(1)} %shard_map.146.mine), channel_id=1, source_target_pairs={{0,12},{1,13},{2,14},{3,15},{4,8},{5,9},{6,10},{7,11},{8,4},{9,5},... | collective-permute-start | bytes 98312 | tf_op jit(solution)/shard_map/ppermute | solution.py:423
  32.2 2.2 %collective-permute-done.1.other = f32[32,256]{1,0:T(8,128)S(1)} collective-permute-done((f32[32,256]{1,0:T(8,128)S(1)}, f32[32,256]{1,0:T(8,128)S(1)}, u32[]{:S(2)}, u32[]{:S(2)}) %collective-permute-start.1) | collective-permute-done | bytes 32800 | tf_op jit(solution)/shard_map/ppermute | solution.py:423
  34.4 1.9 %collective-permute-start.3 = (bf16[128,2048]{1,0:T(8,128)(2,1)S(1)}, bf16[128,2048]{1,0:T(8,128)(2,1)S(1)}, u32[]{:S(2)}, u32[]{:S(2)}) collective-permute-start(bf16[128,2048]{1,0:T(8,128)(2,1)S(1)} %collective-permute-done.2.w_near), channel_id=1, source_target_pairs={{0,16},{16,0},{32,48},{48,32},{64,80},{80,64},{96,112},{112,96},{1... | collective-permute-start | bytes 1572872 | tf_op jit(solution)/shard_map/ppermute | solution.py:427
  36.4 0.6 shard_map.147
  37.0 6.5 %all-to-all-done.received = f32[16,16,128]{2,1,0:T(8,128)S(1)} async-done(((f32[16,16,128]{2,1,0:T(8,128)}), f32[16,16,128]{2,1,0:T(8,128)S(1)}, u32[]{:S(2)}, u32[]{:S(2)}) %all-to-all-start) | async-done | bytes 131104 | tf_op jit(solution)/shard_map/all_to_all | solution.py:431
  43.5 6.4 %shard_map.148 = (f32[256,512]{1,0:T(8,128)S(1)}, f32[8,2,128]{2,1,0:T(2,128)S(1)}) custom-call(f32[16,16,128]{2,1,0:T(8,128)S(1)} %all-to-all-done.received, bf16[64,2048]{1,0:T(8,128)(2,1)S(1)} %get-tuple-element.27.tables, f32[16,512]{1,0:T(8,128)S(1)} %get-tuple-element.28.rows, f32[16,128]{1,0:T(8,128)S(1)} %get-tuple-element.29.step_at), custom_call_target="tpu_custom_call" | custom-call | flops 7000000000 | bytes 7340032 | tf_op jit(solution)/shard_map/pallas_call | solution.py:371
  49.9 11.0 %all_to_all.15.squares = f32[8,2,128]{2,1,0:T(2,128)S(1)} all-to-all(f32[8,2,128]{2,1,0:T(2,128)S(1)} %get-tuple-element.30), channel_id=1, replica_groups={{0,1,2,3,4,5,6,7},{8,9,10,11,12,13,14,15},{16,17,18,19,20,21,22,23},{24..., dimensions={0} | all-to-all | bytes 16384 | tf_op jit(solution)/shard_map/all_to_all | solution.py:431
  60.9 0.7 shard_map.149
  61.6 16.1 %all_to_all.16.received = bf16[8,16,2048]{2,1,0:T(8,128)(2,1)S(1)} all-to-all(bf16[8,16,2048]{2,1,0:T(8,128)(2,1)S(1)} %shard_map.149), channel_id=1, replica_groups={{0,1,2,3,4,5,6,7},{8,9,10,11,12,13,14,15},{16,17,18,19,20,21,22,23},{24..., dimensions={0} | all-to-all | bytes 1048576 | tf_op jit(solution)/shard_map/all_to_all | solution.py:431
  77.7 0.7 shard_map.150
  (30 shorter events, 0.1 us)
Async XLA Ops:
  0.0 7.7 %copy-start.3 = (bf16[128,256]{1,0:T(8,128)(2,1)S(1)}, bf16[128,256]{1,0:T(8,128)(2,1)}, u32[]{:S(2)}) copy-start(bf16[128,256]{1,0:T(8,128)(2,1)} %w_bc.1) | copy-start | bytes 196612
  0.0 7.7 %copy-start.4 = (bf16[5,2048]{1,0:T(8,128)(2,1)S(1)}, bf16[5,2048]{1,0:T(8,128)(2,1)}, u32[]{:S(2)}) copy-start(bf16[5,2048]{1,0:T(8,128)(2,1)} %embed.2) | copy-start | bytes 61444
  1.1 3.4 %copy-start.7 = (s32[256]{0:T(256)S(1)}, s32[256]{0:T(256)}, u32[]{:S(2)}) copy-start(s32[256]{0:T(256)} %param.15) | copy-start | bytes 3076
  1.1 33.3 %collective-permute-start.2 = (bf16[128,2048]{1,0:T(8,128)(2,1)S(1)}, bf16[128,2048]{1,0:T(8,128)(2,1)S(1)}, u32[]{:S(2)}, u32[]{:S(2)}) collective-permute-start(bf16[128,2048]{1,0:T(8,128)(2,1)S(1)} %constant_dynamic-slice_fusion), channel_id=1, source_target_pairs={{0,12},{1,13},{2,14},{3,15},{4,8},{5,9},{6,10},{7,11},{8,4},{9,5},... | collective-permute-start | bytes 1572872 | tf_op jit(solution)/shard_map/ppermute | solution.py:423
  4.5 23.0 %copy-start.1 = (bf16[2048,256]{1,0:T(8,128)(2,1)S(1)}, bf16[2048,256]{1,0:T(8,128)(2,1)}, u32[]{:S(2)}) copy-start(bf16[2048,256]{1,0:T(8,128)(2,1)} %w_x.1) | copy-start | bytes 3145732
  4.6 23.0 %copy-start.2 = (bf16[2048,256]{1,0:T(8,128)(2,1)S(1)}, bf16[2048,256]{1,0:T(8,128)(2,1)}, u32[]{:S(2)}) copy-start(bf16[2048,256]{1,0:T(8,128)(2,1)} %w_z.1) | copy-start | bytes 3145732
  4.6 3.2 %collective-permute-start = (s32[2,128]{1,0:T(2,128)S(1)}, s32[2,128]{1,0:T(2,128)S(1)}, u32[]{:S(2)}, u32[]{:S(2)}) collective-permute-start(s32[2,128]{1,0:T(2,128)S(1)} %bitcast.6), channel_id=1, source_target_pairs={{0,16},{16,0},{32,48},{48,32},{64,80},{80,64},{96,112},{112,96},{1... | collective-permute-start | bytes 3080 | tf_op jit(solution)/shard_map/ppermute | solution.py:427
  8.5 18.2 %copy-start.12 = (f32[4]{0:T(128)S(1)}, f32[4]{0:T(128)}, u32[]{:S(2)}) copy-start(f32[4]{0:T(128)} %param.24) | copy-start | bytes 52
  8.5 18.9 %copy-start.13 = (f32[4]{0:T(128)S(1)}, f32[4]{0:T(128)}, u32[]{:S(2)}) copy-start(f32[4]{0:T(128)} %param.23) | copy-start | bytes 52
  8.5 18.9 %copy-start.14 = (f32[4]{0:T(128)S(1)}, f32[4]{0:T(128)}, u32[]{:S(2)}) copy-start(f32[4]{0:T(128)} %param.22) | copy-start | bytes 52
  8.5 18.9 %copy-start.11 = (f32[256]{0:T(256)S(1)}, f32[256]{0:T(256)}, u32[]{:S(2)}) copy-start(f32[256]{0:T(256)} %param.27) | copy-start | bytes 3076
  8.5 34.9 %all-to-all-start = ((f32[16,16,128]{2,1,0:T(8,128)}), f32[16,16,128]{2,1,0:T(8,128)S(1)}, u32[]{:S(2)}, u32[]{:S(2)}) async-start(f32[16,16,128]{2,1,0:T(8,128)} %shard_map.145), calls=%async_computation | async-start | bytes 262144 | tf_op jit(solution)/shard_map/all_to_all | solution.py:431
  26.8 0.7 copy-start.10
  27.5 0.7 copy-start.5
  28.2 8.2 %copy-start.6 = (bf16[4,256]{1,0:T(4,128)(2,1)S(1)}, bf16[4,256]{1,0:T(4,128)(2,1)}, u32[]{:S(2)}) copy-start(bf16[4,256]{1,0:T(4,128)(2,1)} %conv_bc.1) | copy-start | bytes 6148
  28.2 8.2 %copy-start.8 = (s32[5]{0:T(128)S(1)}, s32[5]{0:T(128)}, u32[]{:S(2)}) copy-start(s32[5]{0:T(128)} %complement.1) | copy-start | bytes 64
  28.2 8.2 %copy-start.9 = (bf16[64,1024]{1,0:T(8,128)(2,1)S(1)}, bf16[64,1024]{1,0:T(8,128)(2,1)}, u32[]{:S(2)}) copy-start(bf16[64,1024]{1,0:T(8,128)(2,1)} %constant.28.clone.grams_in) | copy-start | bytes 393220
  28.6 5.8 %collective-permute-start.1 = (f32[32,256]{1,0:T(8,128)S(1)}, f32[32,256]{1,0:T(8,128)S(1)}, u32[]{:S(2)}, u32[]{:S(2)}) collective-permute-start(f32[32,256]{1,0:T(8,128)S(1)} %shard_map.146.mine), channel_id=1, source_target_pairs={{0,12},{1,13},{2,14},{3,15},{4,8},{5,9},{6,10},{7,11},{8,4},{9,5},... | collective-permute-start | bytes 98312 | tf_op jit(solution)/shard_map/ppermute | solution.py:423
  34.4 26.5 %collective-permute-start.3 = (bf16[128,2048]{1,0:T(8,128)(2,1)S(1)}, bf16[128,2048]{1,0:T(8,128)(2,1)S(1)}, u32[]{:S(2)}, u32[]{:S(2)}) collective-permute-start(bf16[128,2048]{1,0:T(8,128)(2,1)S(1)} %collective-permute-done.2.w_near), channel_id=1, source_target_pairs={{0,16},{16,0},{32,48},{48,32},{64,80},{80,64},{96,112},{112,96},{1... | collective-permute-start | bytes 1572872 | tf_op jit(solution)/shard_map/ppermute | solution.py:427
  43.5 17.4 %copy-start = (bf16[256,2048]{1,0:T(8,128)(2,1)S(1)}, bf16[256,2048]{1,0:T(8,128)(2,1)}, u32[]{:S(2)}) copy-start(bf16[256,2048]{1,0:T(8,128)(2,1)} %w_own.1) | copy-start | bytes 3145732

commit v5 on v4

--- a/solution.py
+++ b/solution.py
@@ -40,8 +40,8 @@
             pair = lambda code: (5, 5) if code == 30 else (code // 5, code % 5)
             for tap, symbol in enumerate(pair(older) + pair(newer)):
                 if symbol < VOCAB:
-                    table[tap * 8 + symbol, older * 32 + newer] = 1
-                    table[32 + tap * 8 + symbol, older * 32 + newer] = 1
+                    table[tap * 8 + symbol, newer * 32 + older] = 1
+                    table[32 + tap * 8 + symbol, newer * 32 + older] = 1
     return table
 
 
@@ -153,7 +153,7 @@
 
 def scan_kernel(
     received, tables, rows, step_at, out, send,
-    tok_ref, fwd_ref, back_ref,
+    tok_ref, fwd_ref, back_ref, sums_ref,
 ):
     seq, chan = place()
     own_line = 2 * seq + chan // GROUP
@@ -231,21 +231,28 @@
         sums = sums + dot(
             jnp.concatenate(right, 1).astype(BF16), jnp.concatenate(left, 0).astype(BF16), (1, 0)
         )
-    sums = jnp.transpose(jnp.concatenate([sums, sums], 1))[0:64]
-
+    sums_ref[...] = jnp.concatenate([sums, sums], 1)
+
+    gram_values = silu(dot(tables[:, :PAIR], tables[:, 2 * PAIR :], (0, 0))).astype(BF16)
     gram_b = silu(dot(bc_taps[:, :STATE], tables[:, 2 * PAIR :], (0, 0))).astype(BF16)
-    wide_code = (32, 32 * PAIR_HEADS)
-    same = jnp.where(lax.rem(iota(wide_code, 1), 32) == iota(wide_code, 0), 1.0, 0.0)
-    gram_values = silu(dot(tables[:, 2 * PAIR :], tables[:, :PAIR], (0, 0))).astype(BF16)
-    shape = (32 * PAIR_HEADS, PAIR)
-    spread = jnp.where(iota(shape, 0) // 32 == iota(shape, 1) // HEAD_DIM, 1.0, 0.0).astype(BF16)
+    by_newer = [sums_ref[pl.ds(newer, PAIR_HEADS, stride=32), :] for newer in range(32)]
+    lane = iota((PAIR_HEADS, 128), 1)
     states = []
     for strand in range(2):
-        placed = jnp.concatenate(
-            [sums[32 * strand + code : 32 * strand + code + 1] * same for code in range(32)], 0
-        )
-        wide = dot(placed.astype(BF16), spread, (1, 0))
-        states.append(dot(gram_b, wide.astype(BF16) * gram_values, (1, 0)))
+        lines = []
+        for first in range(0, 32, 4):
+            whole = jnp.zeros((PAIR_HEADS, 128), F32)
+            for k in range(4):
+                turned = pltpu.roll(by_newer[first + k], (32 * (k - strand)) % 128, 1)
+                whole = jnp.where(lane // 32 == k, turned, whole)
+            lines.append(whole)
+        weight_of = jnp.concatenate(lines, 1)
+        weighted = [
+            gram_values[HEAD_DIM * head : HEAD_DIM * (head + 1)]
+            * jnp.broadcast_to(weight_of[head : head + 1], (HEAD_DIM, 1024)).astype(BF16)
+            for head in range(PAIR_HEADS)
+        ]
+        states.append(jnp.transpose(dot(jnp.concatenate(weighted, 0), gram_b, (1, 1))))
 
     hots = [
         jnp.concatenate([hot(ref[tap, pl.ds(own_line, 1), :], 8) for tap in range(CONV)], 0)
@@ -304,9 +311,7 @@
         send[peer] = mine
 
 
-def project_kernel(squares, gated, w_own, w_near, w_far, out):
-    seq, _ = place()
-    first = lax.rem(seq, 2) == 0
+def project_kernel(squares, gated, w_own, w_other, out):
     total = squares[0]
     for peer in range(1, GROUP):
         total = total + squares[peer]
@@ -317,11 +322,8 @@
         block = gated[LINE * strand : LINE * (strand + 1), :]
         normed = block * jnp.concatenate([down] * (PAIR // LINE), 1)
         combined = combined + normed.astype(BF16).astype(F32)
-    top, end = (combined[:, OWN : OWN + LINE], combined[:, OWN + LINE :])
-    near, far = (jnp.where(first, top, end), jnp.where(first, end, top))
-    mixed = dot(combined[:, :OWN].astype(BF16), w_own[...], (1, 0))
-    mixed = mixed + dot(near.astype(BF16), w_near[...], (1, 0))
-    mixed = mixed + dot(far.astype(BF16), w_far[...], (1, 0))
+    combined = combined.astype(BF16)
+    mixed = dot(combined[:, :OWN], w_own[...], (1, 0)) + dot(combined[:, OWN:], w_other[...], (1, 0))
     out[...] = mixed.astype(BF16).reshape(out.shape)
 
 
@@ -381,13 +383,14 @@
             pltpu.VMEM((LINES, 128), F32),
             pltpu.VMEM((CONV, LINES, 128), F32),
             pltpu.VMEM((CONV, LINES, 128), F32),
+            pltpu.VMEM((32 * PAIR_HEADS, 128), F32),
         ],
     )(received, *prepared)
 
 
 def make_project(squares, gated, *weights):
     shape = (GROUP, PIECE, weights[0].shape[1])
-    return call(project_kernel, jax.ShapeDtypeStruct(shape, BF16), [VMEM] * 5, 1, 16)(
+    return call(project_kernel, jax.ShapeDtypeStruct(shape, BF16), [VMEM] * 4, 1, 16)(
         squares, gated, *weights
     )
 
@@ -445,13 +448,11 @@
     by_channel = jnp.stack([norm_gain, jnp.repeat(d_skip, HEAD_DIM)])
     params = jnp.concatenate([conv_x.astype(F32), by_channel, by_head], 0)
     tables = make_tables(embed, w_x, w_z, w_dt.T, params)
-    half = lax.dynamic_slice_in_dim(w_out, lax.axis_index("seq") % 2 * LINE, LINE, 0)
-    w_near = with_partner(half)
-    other, w_near = lax.optimization_barrier((with_partner(tables), w_near))
-    w_far = with_sibling(w_near)
+    w_other = with_partner(w_out)
+    other, w_other = lax.optimization_barrier((with_partner(tables), w_other))
     prepared = make_prepare(tables, other, conv_bc, complement)
     gated, squares = make_scan(received, prepared)
-    partial = make_project(exchange(squares, "chan", row_groups()), gated, w_out, w_near, w_far)
+    partial = make_project(exchange(squares, "chan", row_groups()), gated, w_out, w_other)
     return make_sum(exchange(partial, "chan", row_groups()))
 
 

time: 78.8 us -> 78.4 us (level)
  waiting for transfers between devices: 9.87 us -> 12.5 us
  starting transfers between devices: 29.1 us -> 27.3 us
  Pallas kernels: 9.62 us -> 8.47 us
    all_to_all x1, waiting for transfers between devices: 6.51 us -> 9.15 us  [exchange(): lax.all_to_all(value, axes, 0, 0, tiled=True, axis_index_groups=groups)]
    ppermute x2 -> x1, starting transfers between devices: 3.96 us -> 2.05 us  [with_sibling(): lax.ppermute(value, 'seq', [(source, source ^ 1) for source in range(SEQ)])]
    dynamic_slice x1 -> x0, local copies, waits for them, and re-layouts: 1.11 us -> none  [per_device(): lax.dynamic_slice_in_dim(w_out, lax.axis_index('seq') % 2 * LINE, LINE, 0)]
    pallas_call x1, Pallas kernels: 6.43 us -> 5.42 us  [make_scan(): call(scan_kernel, (jax.ShapeDtypeStruct((2 * LINE, PAIR), F32), jax.Shape...]
    unnamed x30 -> x32, local copies, waits for them, and re-layouts: 1.29 us -> 2.16 us
  transfers between devices with their start and end apart: 5 -> 4, of which waited for: 3 -> 3; matrix products, arithmetic and copies ran while one was open for 0% -> 0% of each run, Pallas kernels for 11% -> 2%
where the time goes in v5:
time: 78.4 us; the launch traced here: 77.8 us
  starting transfers between devices  27.3 us (35%)
  blocking collectives  27.1 us (35%)
  waiting for transfers between devices  12.5 us (16%)
  Pallas kernels  8.47 us (11%)
  local copies, waits for them, and re-layouts  2.31 us (3%)
    all_to_all x2, blocking collectives, exchange(): lax.all_to_all(value, axes, 0, 0, tiled=True, axis_index_groups=groups)  27.1 us
    all_to_all x1, starting transfers between devices, exchange(): lax.all_to_all(value, axes, 0, 0, tiled=True, axis_index_groups=groups)  18.1 us
    all_to_all x1, waiting for transfers between devices, exchange(): lax.all_to_all(value, axes, 0, 0, tiled=True, axis_index_groups=groups)  9.15 us
    ppermute x2, starting transfers between devices, with_partner(): return lax.ppermute(value, 'chan', pairs)  7.07 us
    pallas_call x1, Pallas kernels, make_scan(): call(scan_kernel, (jax.ShapeDtypeStruct((2 * LINE, PAIR), F32), jax.Shape...  5.42 us
    ppermute x2, waiting for transfers between devices, with_partner(): return lax.ppermute(value, 'chan', pairs)  2.25 us
    unnamed x32, local copies, waits for them, and re-layouts  2.16 us
    ppermute x1, starting transfers between devices, with_sibling(): lax.ppermute(value, 'seq', [(source, source ^ 1) for source in range(SEQ)])  2.05 us
  transfers between devices with their start and end apart: 4, of which 3 were waited for; matrix products, arithmetic and copies ran while one was open for 0% of the time, Pallas kernels for 2%

profile of v5, /device:TPU:2, one launch (start us, length us, event | category | flops | bytes accessed | tf_op | source)
XLA Modules:
  0.0 77.8 jit_solution(4194953265746129572)
XLA Ops:
  0.0 3.5 %collective-permute-start.2 = (bf16[256,2048]{1,0:T(8,128)(2,1)}, bf16[256,2048]{1,0:T(8,128)(2,1)S(1)}, u32[]{:S(2)}, u32[]{:S(2)}) collective-permute-start(bf16[256,2048]{1,0:T(8,128)(2,1)} %w_own.1), channel_id=1, source_target_pairs={{0,12},{1,13},{2,14},{3,15},{4,8},{5,9},{6,10},{7,11},{8,4},{9,5},... | collective-permute-start | bytes 3145736 | tf_op jit(solution)/shard_map/ppermute | solution.py:426
  3.6 2.1 %collective-permute-start = (s32[2,128]{1,0:T(2,128)S(1)}, s32[2,128]{1,0:T(2,128)S(1)}, u32[]{:S(2)}, u32[]{:S(2)}) collective-permute-start(s32[2,128]{1,0:T(2,128)S(1)} %bitcast.6), channel_id=1, source_target_pairs={{0,16},{16,0},{32,48},{48,32},{64,80},{80,64},{96,112},{112,96},{1... | collective-permute-start | bytes 3080 | tf_op jit(solution)/shard_map/ppermute | solution.py:430
  5.6 1.1 %collective-permute-done.sibling = s32[2,128]{1,0:T(2,128)S(1)} collective-permute-done((s32[2,128]{1,0:T(2,128)S(1)}, s32[2,128]{1,0:T(2,128)S(1)}, u32[]{:S(2)}, u32[]{:S(2)}) %collective-permute-start) | collective-permute-done | bytes 1056 | tf_op jit(solution)/shard_map/ppermute | solution.py:430
  6.7 0.8 %copy-done.3 = bf16[128,256]{1,0:T(8,128)(2,1)S(1)} copy-done((bf16[128,256]{1,0:T(8,128)(2,1)S(1)}, bf16[128,256]{1,0:T(8,128)(2,1)}, u32[]{:S(2)}) %copy-start.3) | copy-done | bytes 65560
  7.6 0.8 copy-done.4
  8.3 0.8 %shard_map.145 = f32[16,16,128]{2,1,0:T(8,128)} custom-call(s32[2,128]{1,0:T(2,128)S(1)} %bitcast.7, s32[2,128]{1,0:T(2,128)S(1)} %collective-permute-done.sibling, bf16[5,2048]{1,0:T(8,128)(2,1)S(1)} %copy-done.4, bf16[128,256]{1,0:T(8,128)(2,1)S(1)} %copy-done.3), custom_call_target="tpu_custom_call" | custom-call | flops 1000000000 | bytes 1048576 | tf_op jit(solution)/shard_map/pallas_call | solution.py:350
  9.1 0.0 copy-start.12
  9.1 0.0 copy-start.6
  9.2 18.1 %all-to-all-start = ((f32[16,16,128]{2,1,0:T(8,128)}), f32[16,16,128]{2,1,0:T(8,128)S(1)}, u32[]{:S(2)}, u32[]{:S(2)}) async-start(f32[16,16,128]{2,1,0:T(8,128)} %shard_map.145), calls=%async_computation | async-start | bytes 262144 | tf_op jit(solution)/shard_map/all_to_all | solution.py:434
  27.3 0.0 copy-start.5
  27.3 0.1 broadcast_in_dim.3
  27.4 0.1 stack_reshape.3
  27.6 0.5 copy-done.5
  28.1 0.4 shard_map.146.mine
  28.5 3.6 %collective-permute-start.1 = (f32[32,256]{1,0:T(8,128)S(1)}, f32[32,256]{1,0:T(8,128)S(1)}, u32[]{:S(2)}, u32[]{:S(2)}) collective-permute-start(f32[32,256]{1,0:T(8,128)S(1)} %shard_map.146.mine), channel_id=1, source_target_pairs={{0,12},{1,13},{2,14},{3,15},{4,8},{5,9},{6,10},{7,11},{8,4},{9,5},... | collective-permute-start | bytes 98312 | tf_op jit(solution)/shard_map/ppermute | solution.py:426
  32.1 2.2 %collective-permute-done.1.other = f32[32,256]{1,0:T(8,128)S(1)} collective-permute-done((f32[32,256]{1,0:T(8,128)S(1)}, f32[32,256]{1,0:T(8,128)S(1)}, u32[]{:S(2)}, u32[]{:S(2)}) %collective-permute-start.1) | collective-permute-done | bytes 32800 | tf_op jit(solution)/shard_map/ppermute | solution.py:426
  34.3 0.0 collective-permute-done.2.w_other
  34.3 0.6 shard_map.147
  35.0 9.2 %all-to-all-done.received = f32[16,16,128]{2,1,0:T(8,128)S(1)} async-done(((f32[16,16,128]{2,1,0:T(8,128)}), f32[16,16,128]{2,1,0:T(8,128)S(1)}, u32[]{:S(2)}, u32[]{:S(2)}) %all-to-all-start) | async-done | bytes 131104 | tf_op jit(solution)/shard_map/all_to_all | solution.py:434
  44.1 5.4 %shard_map.148 = (f32[256,512]{1,0:T(8,128)S(1)}, f32[8,2,128]{2,1,0:T(2,128)S(1)}) custom-call(f32[16,16,128]{2,1,0:T(8,128)S(1)} %all-to-all-done.received, bf16[64,2048]{1,0:T(8,128)(2,1)S(1)} %get-tuple-element.27.tables, f32[16,512]{1,0:T(8,128)S(1)} %get-tuple-element.28.rows, f32[16,128]{1,0:T(8,128)S(1)} %get-tuple-element.29.step_at), custom_call_target="tpu_custom_call" | custom-call | flops 7000000000 | bytes 7340032 | tf_op jit(solution)/shard_map/pallas_call | solution.py:373
  49.5 11.0 %all_to_all.15.squares = f32[8,2,128]{2,1,0:T(2,128)S(1)} all-to-all(f32[8,2,128]{2,1,0:T(2,128)S(1)} %get-tuple-element.30), channel_id=1, replica_groups={{0,1,2,3,4,5,6,7},{8,9,10,11,12,13,14,15},{16,17,18,19,20,21,22,23},{24..., dimensions={0} | all-to-all | bytes 16384 | tf_op jit(solution)/shard_map/all_to_all | solution.py:434
  60.5 0.5 shard_map.149
  61.0 16.1 %all_to_all.16.received = bf16[8,16,2048]{2,1,0:T(8,128)(2,1)S(1)} all-to-all(bf16[8,16,2048]{2,1,0:T(8,128)(2,1)S(1)} %shard_map.149), channel_id=1, replica_groups={{0,1,2,3,4,5,6,7},{8,9,10,11,12,13,14,15},{16,17,18,19,20,21,22,23},{24..., dimensions={0} | all-to-all | bytes 1048576 | tf_op jit(solution)/shard_map/all_to_all | solution.py:434
  77.1 0.7 shard_map.150
  (29 shorter events, 0.1 us)
Async XLA Ops:
  0.0 3.5 %copy-start.8 = (s32[256]{0:T(256)S(1)}, s32[256]{0:T(256)}, u32[]{:S(2)}) copy-start(s32[256]{0:T(256)} %param.15) | copy-start | bytes 3076
  0.0 34.3 %collective-permute-start.2 = (bf16[256,2048]{1,0:T(8,128)(2,1)}, bf16[256,2048]{1,0:T(8,128)(2,1)S(1)}, u32[]{:S(2)}, u32[]{:S(2)}) collective-permute-start(bf16[256,2048]{1,0:T(8,128)(2,1)} %w_own.1), channel_id=1, source_target_pairs={{0,12},{1,13},{2,14},{3,15},{4,8},{5,9},{6,10},{7,11},{8,4},{9,5},... | collective-permute-start | bytes 3145736 | tf_op jit(solution)/shard_map/ppermute | solution.py:426
  3.5 24.0 %copy-start = (bf16[2048,256]{1,0:T(8,128)(2,1)S(1)}, bf16[2048,256]{1,0:T(8,128)(2,1)}, u32[]{:S(2)}) copy-start(bf16[2048,256]{1,0:T(8,128)(2,1)} %w_x.1) | copy-start | bytes 3145732
  3.6 24.0 %copy-start.1 = (bf16[2048,256]{1,0:T(8,128)(2,1)S(1)}, bf16[2048,256]{1,0:T(8,128)(2,1)}, u32[]{:S(2)}) copy-start(bf16[2048,256]{1,0:T(8,128)(2,1)} %w_z.1) | copy-start | bytes 3145732
  3.6 3.2 %collective-permute-start = (s32[2,128]{1,0:T(2,128)S(1)}, s32[2,128]{1,0:T(2,128)S(1)}, u32[]{:S(2)}, u32[]{:S(2)}) collective-permute-start(s32[2,128]{1,0:T(2,128)S(1)} %bitcast.6), channel_id=1, source_target_pairs={{0,16},{16,0},{32,48},{48,32},{64,80},{80,64},{96,112},{112,96},{1... | collective-permute-start | bytes 3080 | tf_op jit(solution)/shard_map/ppermute | solution.py:430
  6.7 0.8 %copy-start.3 = (bf16[128,256]{1,0:T(8,128)(2,1)S(1)}, bf16[128,256]{1,0:T(8,128)(2,1)}, u32[]{:S(2)}) copy-start(bf16[128,256]{1,0:T(8,128)(2,1)} %w_bc.1) | copy-start | bytes 196612
  7.6 0.8 copy-start.4
  9.1 18.2 %copy-start.13 = (f32[4]{0:T(128)S(1)}, f32[4]{0:T(128)}, u32[]{:S(2)}) copy-start(f32[4]{0:T(128)} %param.24) | copy-start | bytes 52
  9.1 18.4 %copy-start.11 = (bf16[4,256]{1,0:T(4,128)(2,1)S(1)}, bf16[4,256]{1,0:T(4,128)(2,1)}, u32[]{:S(2)}) copy-start(bf16[4,256]{1,0:T(4,128)(2,1)} %param.25) | copy-start | bytes 6148
  9.1 18.4 %copy-start.14 = (f32[4]{0:T(128)S(1)}, f32[4]{0:T(128)}, u32[]{:S(2)}) copy-start(f32[4]{0:T(128)} %param.23) | copy-start | bytes 52
  9.1 18.4 %copy-start.15 = (f32[4]{0:T(128)S(1)}, f32[4]{0:T(128)}, u32[]{:S(2)}) copy-start(f32[4]{0:T(128)} %param.22) | copy-start | bytes 52
  9.1 18.4 %copy-start.12 = (f32[256]{0:T(256)S(1)}, f32[256]{0:T(256)}, u32[]{:S(2)}) copy-start(f32[256]{0:T(256)} %param.27) | copy-start | bytes 3076
  9.1 18.4 %copy-start.6 = (bf16[2048,4]{0,1:T(4,128)(2,1)S(1)}, bf16[2048,4]{0,1:T(4,128)(2,1)}, u32[]{:S(2)}) copy-start(bf16[2048,4]{0,1:T(4,128)(2,1)} %param.21) | copy-start | bytes 49156
  9.2 34.9 %all-to-all-start = ((f32[16,16,128]{2,1,0:T(8,128)}), f32[16,16,128]{2,1,0:T(8,128)S(1)}, u32[]{:S(2)}, u32[]{:S(2)}) async-start(f32[16,16,128]{2,1,0:T(8,128)} %shard_map.145), calls=%async_computation | async-start | bytes 262144 | tf_op jit(solution)/shard_map/all_to_all | solution.py:434
  27.3 0.8 copy-start.5
  28.1 6.2 %copy-start.7 = (bf16[4,256]{1,0:T(4,128)(2,1)S(1)}, bf16[4,256]{1,0:T(4,128)(2,1)}, u32[]{:S(2)}) copy-start(bf16[4,256]{1,0:T(4,128)(2,1)} %conv_bc.1) | copy-start | bytes 6148
  28.1 6.2 %copy-start.9 = (s32[5]{0:T(128)S(1)}, s32[5]{0:T(128)}, u32[]{:S(2)}) copy-start(s32[5]{0:T(128)} %complement.1) | copy-start | bytes 64
  28.1 6.3 %copy-start.10 = (bf16[64,1024]{1,0:T(8,128)(2,1)S(1)}, bf16[64,1024]{1,0:T(8,128)(2,1)}, u32[]{:S(2)}) copy-start(bf16[64,1024]{1,0:T(8,128)(2,1)} %constant.5.clone.grams_in) | copy-start | bytes 393220
  28.5 5.8 %collective-permute-start.1 = (f32[32,256]{1,0:T(8,128)S(1)}, f32[32,256]{1,0:T(8,128)S(1)}, u32[]{:S(2)}, u32[]{:S(2)}) collective-permute-start(f32[32,256]{1,0:T(8,128)S(1)} %shard_map.146.mine), channel_id=1, source_target_pairs={{0,12},{1,13},{2,14},{3,15},{4,8},{5,9},{6,10},{7,11},{8,4},{9,5},... | collective-permute-start | bytes 98312 | tf_op jit(solution)/shard_map/ppermute | solution.py:426
  44.1 16.4 %copy-start.2 = (bf16[256,2048]{1,0:T(8,128)(2,1)S(1)}, bf16[256,2048]{1,0:T(8,128)(2,1)}, u32[]{:S(2)}) copy-start(bf16[256,2048]{1,0:T(8,128)(2,1)} %w_own.1) | copy-start | bytes 3145732

commit v6 on v5

--- a/solution.py
+++ b/solution.py
@@ -65,10 +65,9 @@
     return x / (1.0 + jnp.exp(-x))
 
 
-def send_kernel(tokens, sibling, embed, w_bc, send):
-    seq, chan = place()
-    part = embed[:, pl.ds(pl.multiple_of(chan * 128, 128), 128)]
-    bc = dot(part, w_bc[...], (1, 0))
+def send_kernel(tokens, sibling, state_map, send):
+    seq, _ = place()
+    bc = state_map[...]
     mine = tokens[...].astype(F32)
     other = sibling[...].astype(F32)
     first = lax.rem(seq, 2) == 0
@@ -347,7 +346,7 @@
 
 
 def make_send(*args):
-    return call(send_kernel, jax.ShapeDtypeStruct((CHIPS, 16, 128), F32), [VMEM] * 4, 1, 16)(*args)
+    return call(send_kernel, jax.ShapeDtypeStruct((CHIPS, 16, 128), F32), [VMEM] * 3, 1, 16)(*args)
 
 
 def make_tables(*args):
@@ -439,7 +438,9 @@
     norm_gain, w_out,
 ):
     own = tokens.reshape(2, 128)
-    send = make_send(own, with_sibling(own), embed, w_bc)
+    depth = w_bc.shape[0]
+    part = lax.dynamic_slice_in_dim(embed, lax.axis_index("chan") * depth, depth, 1)
+    send = make_send(own, with_sibling(own), dot(part, w_bc, (1, 0)))
     send, embed, conv_x, norm_gain, d_skip, dt_bias, decay_rate = lax.optimization_barrier(
         (send, embed, conv_x, norm_gain, d_skip, dt_bias, decay_rate)
     )

time: 78.4 us -> 76.5 us (0.976)
  local copies, waits for them, and re-layouts: 2.31 us -> 0.72 us
  matrix products: 0 us -> 0.81 us
  waiting for transfers between devices: 12.5 us -> 11.7 us
    unnamed x32 -> x30, local copies, waits for them, and re-layouts: 2.16 us -> 0.56 us
    ppermute x1, waiting for transfers between devices: 1.1 us -> 0.28 us  [with_sibling(): lax.ppermute(value, 'seq', [(source, source ^ 1) for source in range(SEQ)])]
    dot_general x0 -> x1, matrix products: none -> 0.81 us  [dot(): lax.dot_general(a, b, ((contract[:1], contract[1:]), ((), ())), preferred...]
  transfers between devices with their start and end apart: 4 -> 4, of which waited for: 3 -> 3; matrix products, arithmetic and copies ran while one was open for 0% -> 1% of each run, Pallas kernels for 2% -> 2%
where the time goes in v6:
time: 76.5 us; the launch traced here: 76 us
  starting transfers between devices  27.1 us (35%)
  blocking collectives  27.1 us (35%)
  waiting for transfers between devices  11.7 us (15%)
  Pallas kernels  8.34 us (11%)
  matrix products  0.81 us (1%)
    all_to_all x2, blocking collectives, exchange(): lax.all_to_all(value, axes, 0, 0, tiled=True, axis_index_groups=groups)  27.1 us
    all_to_all x1, starting transfers between devices, exchange(): lax.all_to_all(value, axes, 0, 0, tiled=True, axis_index_groups=groups)  18.1 us
    all_to_all x1, waiting for transfers between devices, exchange(): lax.all_to_all(value, axes, 0, 0, tiled=True, axis_index_groups=groups)  9.2 us
    ppermute x2, starting transfers between devices, with_partner(): return lax.ppermute(value, 'chan', pairs)  7.07 us
    pallas_call x1, Pallas kernels, make_scan(): call(scan_kernel, (jax.ShapeDtypeStruct((2 * LINE, PAIR), F32), jax.Shape...  5.41 us
    ppermute x2, waiting for transfers between devices, with_partner(): return lax.ppermute(value, 'chan', pairs)  2.25 us
    ppermute x1, starting transfers between devices, with_sibling(): lax.ppermute(value, 'seq', [(source, source ^ 1) for source in range(SEQ)])  1.92 us
  transfers between devices with their start and end apart: 4, of which 3 were waited for; matrix products, arithmetic and copies ran while one was open for 1% of the time, Pallas kernels for 2%

profile of v6, /device:TPU:2, one launch (start us, length us, event | category | flops | bytes accessed | tf_op | source)
XLA Modules:
  0.0 76.0 jit_solution(66853655322972966)
XLA Ops:
  0.0 3.5 %collective-permute-start.2 = (bf16[256,2048]{1,0:T(8,128)(2,1)}, bf16[256,2048]{1,0:T(8,128)(2,1)S(1)}, u32[]{:S(2)}, u32[]{:S(2)}) collective-permute-start(bf16[256,2048]{1,0:T(8,128)(2,1)} %w_own.1), channel_id=1, source_target_pairs={{0,12},{1,13},{2,14},{3,15},{4,8},{5,9},{6,10},{7,11},{8,4},{9,5},... | collective-permute-start | bytes 3145736 | tf_op jit(solution)/shard_map/ppermute | solution.py:425
  3.5 1.9 %collective-permute-start = (s32[2,128]{1,0:T(2,128)S(1)}, s32[2,128]{1,0:T(2,128)S(1)}, u32[]{:S(2)}, u32[]{:S(2)}) collective-permute-start(s32[2,128]{1,0:T(2,128)S(1)} %bitcast.7), channel_id=1, source_target_pairs={{0,16},{16,0},{32,48},{48,32},{64,80},{80,64},{96,112},{112,96},{1... | collective-permute-start | bytes 3080 | tf_op jit(solution)/shard_map/ppermute | solution.py:429
  5.5 0.8 %fusion.state_map = f32[5,256]{1,0:T(8,128)S(1)} fusion(bf16[128,256]{1,0:T(8,128)(2,1)S(1)} %copy-done, bf16[5,2048]{1,0:T(8,128)(2,1)} %embed, s32[]{:T(128)S(6)} %select_n.3), kind=kOutput, calls=%fused_computation.2 | convolution fusion | flops 327680 | bytes 72708 | tf_op jit(solution)/shard_map/dot_general | solution.py:61
  6.3 0.3 collective-permute-done.sibling
  6.6 0.7 shard_map.145
  7.3 0.0 copy-start.11
  7.3 0.0 copy-start.5
  7.3 18.1 %all-to-all-start = ((f32[16,16,128]{2,1,0:T(8,128)}), f32[16,16,128]{2,1,0:T(8,128)S(1)}, u32[]{:S(2)}, u32[]{:S(2)}) async-start(f32[16,16,128]{2,1,0:T(8,128)} %shard_map.145), calls=%async_computation | async-start | bytes 262144 | tf_op jit(solution)/shard_map/all_to_all | solution.py:433
  25.4 0.0 copy-start.1
  25.4 0.1 broadcast_in_dim.3
  25.5 0.1 stack_reshape.3
  25.7 0.5 copy-done.1
  26.2 0.4 shard_map.146.mine
  26.6 3.6 %collective-permute-start.1 = (f32[32,256]{1,0:T(8,128)S(1)}, f32[32,256]{1,0:T(8,128)S(1)}, u32[]{:S(2)}, u32[]{:S(2)}) collective-permute-start(f32[32,256]{1,0:T(8,128)S(1)} %shard_map.146.mine), channel_id=1, source_target_pairs={{0,12},{1,13},{2,14},{3,15},{4,8},{5,9},{6,10},{7,11},{8,4},{9,5},... | collective-permute-start | bytes 98312 | tf_op jit(solution)/shard_map/ppermute | solution.py:425
  30.2 2.2 %collective-permute-done.1.other = f32[32,256]{1,0:T(8,128)S(1)} collective-permute-done((f32[32,256]{1,0:T(8,128)S(1)}, f32[32,256]{1,0:T(8,128)S(1)}, u32[]{:S(2)}, u32[]{:S(2)}) %collective-permute-start.1) | collective-permute-done | bytes 32800 | tf_op jit(solution)/shard_map/ppermute | solution.py:425
  32.4 0.0 collective-permute-done.2.w_other
  32.4 0.0 copy-done.6
  32.5 0.6 shard_map.147
  33.1 9.2 %all-to-all-done.received = f32[16,16,128]{2,1,0:T(8,128)S(1)} async-done(((f32[16,16,128]{2,1,0:T(8,128)}), f32[16,16,128]{2,1,0:T(8,128)S(1)}, u32[]{:S(2)}, u32[]{:S(2)}) %all-to-all-start) | async-done | bytes 131104 | tf_op jit(solution)/shard_map/all_to_all | solution.py:433
  42.3 5.4 %shard_map.148 = (f32[256,512]{1,0:T(8,128)S(1)}, f32[8,2,128]{2,1,0:T(2,128)S(1)}) custom-call(f32[16,16,128]{2,1,0:T(8,128)S(1)} %all-to-all-done.received, bf16[64,2048]{1,0:T(8,128)(2,1)S(1)} %get-tuple-element.27.tables, f32[16,512]{1,0:T(8,128)S(1)} %get-tuple-element.28.rows, f32[16,128]{1,0:T(8,128)S(1)} %get-tuple-element.29.step_at), custom_call_target="tpu_custom_call" | custom-call | flops 7000000000 | bytes 7340032 | tf_op jit(solution)/shard_map/pallas_call | solution.py:372
  47.7 11.0 %all_to_all.15.squares = f32[8,2,128]{2,1,0:T(2,128)S(1)} all-to-all(f32[8,2,128]{2,1,0:T(2,128)S(1)} %get-tuple-element.30), channel_id=1, replica_groups={{0,1,2,3,4,5,6,7},{8,9,10,11,12,13,14,15},{16,17,18,19,20,21,22,23},{24..., dimensions={0} | all-to-all | bytes 16384 | tf_op jit(solution)/shard_map/all_to_all | solution.py:433
  58.7 0.5 shard_map.149
  59.2 16.1 %all_to_all.16.received = bf16[8,16,2048]{2,1,0:T(8,128)(2,1)S(1)} all-to-all(bf16[8,16,2048]{2,1,0:T(8,128)(2,1)S(1)} %shard_map.149), channel_id=1, replica_groups={{0,1,2,3,4,5,6,7},{8,9,10,11,12,13,14,15},{16,17,18,19,20,21,22,23},{24..., dimensions={0} | all-to-all | bytes 1048576 | tf_op jit(solution)/shard_map/all_to_all | solution.py:433
  75.3 0.7 shard_map.150
  (28 shorter events, 0.1 us)
Async XLA Ops:
  0.0 5.5 %copy-start = (bf16[128,256]{1,0:T(8,128)(2,1)S(1)}, bf16[128,256]{1,0:T(8,128)(2,1)}, u32[]{:S(2)}) copy-start(bf16[128,256]{1,0:T(8,128)(2,1)} %param.20) | copy-start | bytes 196612
  0.0 3.5 %copy-start.7 = (s32[256]{0:T(256)S(1)}, s32[256]{0:T(256)}, u32[]{:S(2)}) copy-start(s32[256]{0:T(256)} %param.15) | copy-start | bytes 3076
  0.0 32.4 %collective-permute-start.2 = (bf16[256,2048]{1,0:T(8,128)(2,1)}, bf16[256,2048]{1,0:T(8,128)(2,1)S(1)}, u32[]{:S(2)}, u32[]{:S(2)}) collective-permute-start(bf16[256,2048]{1,0:T(8,128)(2,1)} %w_own.1), channel_id=1, source_target_pairs={{0,12},{1,13},{2,14},{3,15},{4,8},{5,9},{6,10},{7,11},{8,4},{9,5},... | collective-permute-start | bytes 3145736 | tf_op jit(solution)/shard_map/ppermute | solution.py:425
  3.5 3.0 %collective-permute-start = (s32[2,128]{1,0:T(2,128)S(1)}, s32[2,128]{1,0:T(2,128)S(1)}, u32[]{:S(2)}, u32[]{:S(2)}) collective-permute-start(s32[2,128]{1,0:T(2,128)S(1)} %bitcast.7), channel_id=1, source_target_pairs={{0,16},{16,0},{32,48},{48,32},{64,80},{80,64},{96,112},{112,96},{1... | collective-permute-start | bytes 3080 | tf_op jit(solution)/shard_map/ppermute | solution.py:429
  6.3 19.4 %copy-start.2 = (bf16[2048,256]{1,0:T(8,128)(2,1)S(1)}, bf16[2048,256]{1,0:T(8,128)(2,1)}, u32[]{:S(2)}) copy-start(bf16[2048,256]{1,0:T(8,128)(2,1)} %w_x.1) | copy-start | bytes 3145732
  6.3 19.4 %copy-start.3 = (bf16[2048,256]{1,0:T(8,128)(2,1)S(1)}, bf16[2048,256]{1,0:T(8,128)(2,1)}, u32[]{:S(2)}) copy-start(bf16[2048,256]{1,0:T(8,128)(2,1)} %w_z.1) | copy-start | bytes 3145732
  7.2 18.2 %copy-start.12 = (f32[4]{0:T(128)S(1)}, f32[4]{0:T(128)}, u32[]{:S(2)}) copy-start(f32[4]{0:T(128)} %param.24) | copy-start | bytes 52
  7.2 18.4 %copy-start.10 = (bf16[4,256]{1,0:T(4,128)(2,1)S(1)}, bf16[4,256]{1,0:T(4,128)(2,1)}, u32[]{:S(2)}) copy-start(bf16[4,256]{1,0:T(4,128)(2,1)} %param.25) | copy-start | bytes 6148
  7.2 18.4 %copy-start.13 = (f32[4]{0:T(128)S(1)}, f32[4]{0:T(128)}, u32[]{:S(2)}) copy-start(f32[4]{0:T(128)} %param.23) | copy-start | bytes 52
  7.2 18.4 %copy-start.14 = (f32[4]{0:T(128)S(1)}, f32[4]{0:T(128)}, u32[]{:S(2)}) copy-start(f32[4]{0:T(128)} %param.22) | copy-start | bytes 52
  7.3 18.4 %copy-start.11 = (f32[256]{0:T(256)S(1)}, f32[256]{0:T(256)}, u32[]{:S(2)}) copy-start(f32[256]{0:T(256)} %param.27) | copy-start | bytes 3076
  7.3 18.4 %copy-start.5 = (bf16[2048,4]{0,1:T(4,128)(2,1)S(1)}, bf16[2048,4]{0,1:T(4,128)(2,1)}, u32[]{:S(2)}) copy-start(bf16[2048,4]{0,1:T(4,128)(2,1)} %param.21) | copy-start | bytes 49156
  7.3 35.0 %all-to-all-start = ((f32[16,16,128]{2,1,0:T(8,128)}), f32[16,16,128]{2,1,0:T(8,128)S(1)}, u32[]{:S(2)}, u32[]{:S(2)}) async-start(f32[16,16,128]{2,1,0:T(8,128)} %shard_map.145), calls=%async_computation | async-start | bytes 262144 | tf_op jit(solution)/shard_map/all_to_all | solution.py:433
  25.4 0.8 %copy-start.1 = (bf16[5,2048]{1,0:T(8,128)(2,1)S(1)}, bf16[5,2048]{1,0:T(8,128)(2,1)}, u32[]{:S(2)}) copy-start(bf16[5,2048]{1,0:T(8,128)(2,1)} %embed) | copy-start | bytes 61444
  26.2 6.2 %copy-start.6 = (bf16[4,256]{1,0:T(4,128)(2,1)S(1)}, bf16[4,256]{1,0:T(4,128)(2,1)}, u32[]{:S(2)}) copy-start(bf16[4,256]{1,0:T(4,128)(2,1)} %conv_bc.1) | copy-start | bytes 6148
  26.2 6.2 %copy-start.8 = (s32[5]{0:T(128)S(1)}, s32[5]{0:T(128)}, u32[]{:S(2)}) copy-start(s32[5]{0:T(128)} %complement.1) | copy-start | bytes 64
  26.2 6.3 %copy-start.9 = (bf16[64,1024]{1,0:T(8,128)(2,1)S(1)}, bf16[64,1024]{1,0:T(8,128)(2,1)}, u32[]{:S(2)}) copy-start(bf16[64,1024]{1,0:T(8,128)(2,1)} %constant.14.clone.grams_in) | copy-start | bytes 393220
  26.6 5.8 %collective-permute-start.1 = (f32[32,256]{1,0:T(8,128)S(1)}, f32[32,256]{1,0:T(8,128)S(1)}, u32[]{:S(2)}, u32[]{:S(2)}) collective-permute-start(f32[32,256]{1,0:T(8,128)S(1)} %shard_map.146.mine), channel_id=1, source_target_pairs={{0,12},{1,13},{2,14},{3,15},{4,8},{5,9},{6,10},{7,11},{8,4},{9,5},... | collective-permute-start | bytes 98312 | tf_op jit(solution)/shard_map/ppermute | solution.py:425
  42.3 16.4 %copy-start.4 = (bf16[256,2048]{1,0:T(8,128)(2,1)S(1)}, bf16[256,2048]{1,0:T(8,128)(2,1)}, u32[]{:S(2)}) copy-start(bf16[256,2048]{1,0:T(8,128)(2,1)} %w_own.1) | copy-start | bytes 3145732

commit v7 on v6

--- a/solution.py
+++ b/solution.py
@@ -216,6 +216,66 @@
             own_step = jnp.where(newest[symbol], step_at[symbol, head], own_step)
         weights.append(own_step * jnp.exp(-lost))
 
+    head_of = iota((1, OWN), 1) // HEAD_DIM
+    row, column = (iota((LINE, LINE), 0), iota((LINE, LINE), 1))
+    done = {}
+
+    def own_steps():
+        hots = [
+            jnp.concatenate([hot(ref[tap, pl.ds(own_line, 1), :], 8) for tap in range(CONV)], 0)
+            for ref in (fwd_ref, back_ref)
+        ]
+        hots = jnp.concatenate(hots, 1)
+        mixed = dot(jnp.concatenate([hots, hots], 0).astype(BF16), conv_tab, (0, 0))
+        done["gate"] = mixed[:, PAIR + 2 * STATE :]
+        yield
+        first = silu(mixed[:, PAIR : PAIR + 2 * STATE])
+        yield
+        done["values"] = silu(mixed[:, :PAIR])
+        yield
+        grams = tables[:, 2 * PAIR :]
+        done["gram_b"] = silu(dot(bc_taps[:, :STATE], grams, (0, 0))).astype(BF16)
+        yield
+        for head in range(PAIR_HEADS):
+            x_taps = tables[:, LINE * (head // 2) : LINE * (head // 2 + 1)]
+            if head % 2 == 0:
+                both = silu(dot(x_taps, grams, (0, 0))).astype(BF16)
+            done[head] = both[HEAD_DIM * (head % 2) : HEAD_DIM * (head % 2 + 1)]
+            yield
+        for strand in range(2):
+            own = slice(LINE * strand, LINE * (strand + 1))
+            b_in = first[own, :STATE].astype(BF16)
+            c_out = first[own, STATE:]
+            causal = row >= column if strand == 0 else row <= column
+            order = row <= column if strand == 0 else row >= column
+            symbols = hots[24:32, own]
+            seen = dot(symbols.astype(BF16), jnp.where(order, 1.0, 0.0).astype(BF16), (1, 0))
+            cumul, step = ([], [])
+            for head in range(PAIR_HEADS):
+                total = jnp.zeros((1, LINE), F32)
+                own_step = jnp.zeros((1, LINE), F32)
+                for symbol in range(VOCAB):
+                    total = total - step_at[8 + symbol, head] * seen[symbol : symbol + 1]
+                    own_step = own_step + step_at[symbol, head] * symbols[symbol : symbol + 1]
+                cumul.append(total)
+                step.append(own_step)
+            yield
+            across = jnp.transpose(
+                jnp.concatenate(cumul + [jnp.zeros((LINE - PAIR_HEADS, LINE), F32)], 0)
+            )
+            scores = dot(c_out.astype(BF16), b_in, (1, 1))
+            yield
+            for head in range(PAIR_HEADS):
+                at = slice(OWN * (head // OWN_HEADS), OWN * (head // OWN_HEADS + 1))
+                column_of = across[:, head : head + 1]
+                decayed = jnp.exp(jnp.where(causal, column_of - cumul[head], -1e30))
+                left = (decayed * (scores * step[head])).astype(BF16)
+                right = jnp.where(head_of == head % OWN_HEADS, done["values"][own, at], 0.0).astype(BF16)
+                done[strand, head] = (left, right, (c_out * jnp.exp(column_of)).astype(BF16))
+                yield
+
+    steps = own_steps()
+
     older_down = jnp.transpose(jnp.concatenate([older, older], 0))
     lanes = fiota((128, 64), 1)
     sums = jnp.zeros((32 * PAIR_HEADS, 64), F32)
@@ -230,10 +290,11 @@
         sums = sums + dot(
             jnp.concatenate(right, 1).astype(BF16), jnp.concatenate(left, 0).astype(BF16), (1, 0)
         )
+        next(steps, None)
+    for _ in steps:
+        pass
     sums_ref[...] = jnp.concatenate([sums, sums], 1)
 
-    gram_values = silu(dot(tables[:, :PAIR], tables[:, 2 * PAIR :], (0, 0))).astype(BF16)
-    gram_b = silu(dot(bc_taps[:, :STATE], tables[:, 2 * PAIR :], (0, 0))).astype(BF16)
     by_newer = [sums_ref[pl.ds(newer, PAIR_HEADS, stride=32), :] for newer in range(32)]
     lane = iota((PAIR_HEADS, 128), 1)
     states = []
@@ -247,61 +308,30 @@
             lines.append(whole)
         weight_of = jnp.concatenate(lines, 1)
         weighted = [
-            gram_values[HEAD_DIM * head : HEAD_DIM * (head + 1)]
+            done[head]
             * jnp.broadcast_to(weight_of[head : head + 1], (HEAD_DIM, 1024)).astype(BF16)
             for head in range(PAIR_HEADS)
         ]
-        states.append(jnp.transpose(dot(jnp.concatenate(weighted, 0), gram_b, (1, 1))))
-
-    hots = [
-        jnp.concatenate([hot(ref[tap, pl.ds(own_line, 1), :], 8) for tap in range(CONV)], 0)
-        for ref in (fwd_ref, back_ref)
-    ]
-    hots = jnp.concatenate(hots, 1)
-    mixed = dot(jnp.concatenate([hots, hots], 0).astype(BF16), conv_tab, (0, 0))
-    gate = mixed[:, PAIR + 2 * STATE :]
-    mixed = silu(mixed[:, : PAIR + 2 * STATE])
-    head_of = iota((1, OWN), 1) // HEAD_DIM
-    row, column = (iota((LINE, LINE), 0), iota((LINE, LINE), 1))
+        states.append(jnp.transpose(dot(jnp.concatenate(weighted, 0), done["gram_b"], (1, 1))))
+
     squares = []
     for strand in range(2):
         own = slice(LINE * strand, LINE * (strand + 1))
-        b_in = mixed[own, PAIR : PAIR + STATE].astype(BF16)
-        c_out = mixed[own, PAIR + STATE :]
-        causal = row >= column if strand == 0 else row <= column
-        order = row <= column if strand == 0 else row >= column
-        symbols = hots[24:32, own]
-        seen = dot(symbols.astype(BF16), jnp.where(order, 1.0, 0.0).astype(BF16), (1, 0))
-        cumul, step = ([], [])
-        for head in range(PAIR_HEADS):
-            total = jnp.zeros((1, LINE), F32)
-            own_step = jnp.zeros((1, LINE), F32)
-            for symbol in range(VOCAB):
-                total = total - step_at[8 + symbol, head] * seen[symbol : symbol + 1]
-                own_step = own_step + step_at[symbol, head] * symbols[symbol : symbol + 1]
-            cumul.append(total)
-            step.append(own_step)
-        across = jnp.transpose(
-            jnp.concatenate(cumul + [jnp.zeros((LINE - PAIR_HEADS, LINE), F32)], 0)
-        )
-        scores = dot(c_out.astype(BF16), b_in, (1, 1))
         squared = jnp.zeros((LINE, LINE), F32)
         for side in range(2):
             at = slice(OWN * side, OWN * (side + 1))
-            values = mixed[own, at]
-            left, right, tail_left, tail_right = ([], [], [], [])
-            for near in range(OWN_HEADS):
-                head = OWN_HEADS * side + near
-                column_of = across[:, head : head + 1]
-                decayed = jnp.exp(jnp.where(causal, column_of - cumul[head], -1e30))
-                left.append((decayed * (scores * step[head])).astype(BF16))
-                right.append(jnp.where(head_of == near, values, 0.0).astype(BF16))
-                tail_left.append((c_out * jnp.exp(column_of)).astype(BF16))
-                tail_right.append(jnp.where(head_of == near, states[strand][:, at], 0.0).astype(BF16))
+            values = done["values"][own, at]
+            heads = [done[strand, OWN_HEADS * side + near] for near in range(OWN_HEADS)]
+            tail = [
+                jnp.where(head_of == near, states[strand][:, at], 0.0).astype(BF16)
+                for near in range(OWN_HEADS)
+            ]
             ssd = dot(
-                jnp.concatenate(left + tail_left, 1), jnp.concatenate(right + tail_right, 0), (1, 0)
+                jnp.concatenate([head[0] for head in heads] + [head[2] for head in heads], 1),
+                jnp.concatenate([head[1] for head in heads] + tail, 0),
+                (1, 0),
             )
-            gated = (ssd + values * rows[5:6, at]) * gate[own, at]
+            gated = (ssd + values * rows[5:6, at]) * done["gate"][own, at]
             out[own, at] = gated * rows[4:5, at]
             squared = squared + gated[:, :LINE] * gated[:, :LINE] + gated[:, LINE:] * gated[:, LINE:]
         squares.append(jnp.sum(jnp.transpose(squared), axis=0, keepdims=True))

time: 76.5 us -> 76 us (level)
  no operation moved by 1% of the time
where the time goes in v7:
time: 76 us; the launch traced here: 75.5 us
  starting transfers between devices  27.1 us (36%)
  blocking collectives  27.1 us (36%)
  waiting for transfers between devices  11.7 us (15%)
  Pallas kernels  7.87 us (10%)
  matrix products  0.81 us (1%)
    all_to_all x2, blocking collectives, exchange(): lax.all_to_all(value, axes, 0, 0, tiled=True, axis_index_groups=groups)  27.1 us
    all_to_all x1, starting transfers between devices, exchange(): lax.all_to_all(value, axes, 0, 0, tiled=True, axis_index_groups=groups)  18.1 us
    all_to_all x1, waiting for transfers between devices, exchange(): lax.all_to_all(value, axes, 0, 0, tiled=True, axis_index_groups=groups)  9.2 us
    ppermute x2, starting transfers between devices, with_partner(): return lax.ppermute(value, 'chan', pairs)  7.07 us
    pallas_call x1, Pallas kernels, make_scan(): call(scan_kernel, (jax.ShapeDtypeStruct((2 * LINE, PAIR), F32), jax.Shape...  4.95 us
    ppermute x2, waiting for transfers between devices, with_partner(): return lax.ppermute(value, 'chan', pairs)  2.25 us
    ppermute x1, starting transfers between devices, with_sibling(): lax.ppermute(value, 'seq', [(source, source ^ 1) for source in range(SEQ)])  1.92 us
  transfers between devices with their start and end apart: 4, of which 3 were waited for; matrix products, arithmetic and copies ran while one was open for 1% of the time, Pallas kernels for 2%

profile of v7, /device:TPU:2, one launch (start us, length us, event | category | flops | bytes accessed | tf_op | source)
XLA Modules:
  0.0 75.5 jit_solution(3422335950632456627)
XLA Ops:
  0.0 3.5 %collective-permute-start.2 = (bf16[256,2048]{1,0:T(8,128)(2,1)}, bf16[256,2048]{1,0:T(8,128)(2,1)S(1)}, u32[]{:S(2)}, u32[]{:S(2)}) collective-permute-start(bf16[256,2048]{1,0:T(8,128)(2,1)} %w_own.1), channel_id=1, source_target_pairs={{0,12},{1,13},{2,14},{3,15},{4,8},{5,9},{6,10},{7,11},{8,4},{9,5},... | collective-permute-start | bytes 3145736 | tf_op jit(solution)/shard_map/ppermute | solution.py:455
  3.5 1.9 %collective-permute-start = (s32[2,128]{1,0:T(2,128)S(1)}, s32[2,128]{1,0:T(2,128)S(1)}, u32[]{:S(2)}, u32[]{:S(2)}) collective-permute-start(s32[2,128]{1,0:T(2,128)S(1)} %bitcast.7), channel_id=1, source_target_pairs={{0,16},{16,0},{32,48},{48,32},{64,80},{80,64},{96,112},{112,96},{1... | collective-permute-start | bytes 3080 | tf_op jit(solution)/shard_map/ppermute | solution.py:459
  5.5 0.8 %fusion.state_map = f32[5,256]{1,0:T(8,128)S(1)} fusion(bf16[128,256]{1,0:T(8,128)(2,1)S(1)} %copy-done, bf16[5,2048]{1,0:T(8,128)(2,1)} %embed, s32[]{:T(128)S(6)} %select_n.3), kind=kOutput, calls=%fused_computation.2 | convolution fusion | flops 327680 | bytes 72708 | tf_op jit(solution)/shard_map/dot_general | solution.py:61
  6.3 0.3 collective-permute-done.sibling
  6.6 0.7 shard_map.145
  7.3 0.0 copy-start.11
  7.3 0.0 copy-start.5
  7.3 18.1 %all-to-all-start = ((f32[16,16,128]{2,1,0:T(8,128)}), f32[16,16,128]{2,1,0:T(8,128)S(1)}, u32[]{:S(2)}, u32[]{:S(2)}) async-start(f32[16,16,128]{2,1,0:T(8,128)} %shard_map.145), calls=%async_computation | async-start | bytes 262144 | tf_op jit(solution)/shard_map/all_to_all | solution.py:463
  25.4 0.0 copy-start.1
  25.4 0.1 broadcast_in_dim.3
  25.5 0.1 stack_reshape.3
  25.7 0.5 copy-done.1
  26.2 0.4 shard_map.146.mine
  26.6 3.6 %collective-permute-start.1 = (f32[32,256]{1,0:T(8,128)S(1)}, f32[32,256]{1,0:T(8,128)S(1)}, u32[]{:S(2)}, u32[]{:S(2)}) collective-permute-start(f32[32,256]{1,0:T(8,128)S(1)} %shard_map.146.mine), channel_id=1, source_target_pairs={{0,12},{1,13},{2,14},{3,15},{4,8},{5,9},{6,10},{7,11},{8,4},{9,5},... | collective-permute-start | bytes 98312 | tf_op jit(solution)/shard_map/ppermute | solution.py:455
  30.2 2.2 %collective-permute-done.1.other = f32[32,256]{1,0:T(8,128)S(1)} collective-permute-done((f32[32,256]{1,0:T(8,128)S(1)}, f32[32,256]{1,0:T(8,128)S(1)}, u32[]{:S(2)}, u32[]{:S(2)}) %collective-permute-start.1) | collective-permute-done | bytes 32800 | tf_op jit(solution)/shard_map/ppermute | solution.py:455
  32.4 0.0 collective-permute-done.2.w_other
  32.4 0.0 copy-done.6
  32.5 0.6 shard_map.147
  33.1 9.2 %all-to-all-done.received = f32[16,16,128]{2,1,0:T(8,128)S(1)} async-done(((f32[16,16,128]{2,1,0:T(8,128)}), f32[16,16,128]{2,1,0:T(8,128)S(1)}, u32[]{:S(2)}, u32[]{:S(2)}) %all-to-all-start) | async-done | bytes 131104 | tf_op jit(solution)/shard_map/all_to_all | solution.py:463
  42.3 4.9 %shard_map.148 = (f32[256,512]{1,0:T(8,128)S(1)}, f32[8,2,128]{2,1,0:T(2,128)S(1)}) custom-call(f32[16,16,128]{2,1,0:T(8,128)S(1)} %all-to-all-done.received, bf16[64,2048]{1,0:T(8,128)(2,1)S(1)} %get-tuple-element.27.tables, f32[16,512]{1,0:T(8,128)S(1)} %get-tuple-element.28.rows, f32[16,128]{1,0:T(8,128)S(1)} %get-tuple-element.29.step_at), custom_call_target="tpu_custom_call" | custom-call | flops 7000000000 | bytes 7340032 | tf_op jit(solution)/shard_map/pallas_call | solution.py:402
  47.2 11.0 %all_to_all.15.squares = f32[8,2,128]{2,1,0:T(2,128)S(1)} all-to-all(f32[8,2,128]{2,1,0:T(2,128)S(1)} %get-tuple-element.30), channel_id=1, replica_groups={{0,1,2,3,4,5,6,7},{8,9,10,11,12,13,14,15},{16,17,18,19,20,21,22,23},{24..., dimensions={0} | all-to-all | bytes 16384 | tf_op jit(solution)/shard_map/all_to_all | solution.py:463
  58.2 0.5 shard_map.149
  58.7 16.1 %all_to_all.16.received = bf16[8,16,2048]{2,1,0:T(8,128)(2,1)S(1)} all-to-all(bf16[8,16,2048]{2,1,0:T(8,128)(2,1)S(1)} %shard_map.149), channel_id=1, replica_groups={{0,1,2,3,4,5,6,7},{8,9,10,11,12,13,14,15},{16,17,18,19,20,21,22,23},{24..., dimensions={0} | all-to-all | bytes 1048576 | tf_op jit(solution)/shard_map/all_to_all | solution.py:463
  74.8 0.7 shard_map.150
  (28 shorter events, 0.1 us)
Async XLA Ops:
  0.0 5.5 %copy-start = (bf16[128,256]{1,0:T(8,128)(2,1)S(1)}, bf16[128,256]{1,0:T(8,128)(2,1)}, u32[]{:S(2)}) copy-start(bf16[128,256]{1,0:T(8,128)(2,1)} %param.20) | copy-start | bytes 196612
  0.0 3.5 %copy-start.7 = (s32[256]{0:T(256)S(1)}, s32[256]{0:T(256)}, u32[]{:S(2)}) copy-start(s32[256]{0:T(256)} %param.15) | copy-start | bytes 3076
  0.0 32.4 %collective-permute-start.2 = (bf16[256,2048]{1,0:T(8,128)(2,1)}, bf16[256,2048]{1,0:T(8,128)(2,1)S(1)}, u32[]{:S(2)}, u32[]{:S(2)}) collective-permute-start(bf16[256,2048]{1,0:T(8,128)(2,1)} %w_own.1), channel_id=1, source_target_pairs={{0,12},{1,13},{2,14},{3,15},{4,8},{5,9},{6,10},{7,11},{8,4},{9,5},... | collective-permute-start | bytes 3145736 | tf_op jit(solution)/shard_map/ppermute | solution.py:455
  3.5 3.0 %collective-permute-start = (s32[2,128]{1,0:T(2,128)S(1)}, s32[2,128]{1,0:T(2,128)S(1)}, u32[]{:S(2)}, u32[]{:S(2)}) collective-permute-start(s32[2,128]{1,0:T(2,128)S(1)} %bitcast.7), channel_id=1, source_target_pairs={{0,16},{16,0},{32,48},{48,32},{64,80},{80,64},{96,112},{112,96},{1... | collective-permute-start | bytes 3080 | tf_op jit(solution)/shard_map/ppermute | solution.py:459
  6.3 19.4 %copy-start.2 = (bf16[2048,256]{1,0:T(8,128)(2,1)S(1)}, bf16[2048,256]{1,0:T(8,128)(2,1)}, u32[]{:S(2)}) copy-start(bf16[2048,256]{1,0:T(8,128)(2,1)} %w_x.1) | copy-start | bytes 3145732
  6.3 19.4 %copy-start.3 = (bf16[2048,256]{1,0:T(8,128)(2,1)S(1)}, bf16[2048,256]{1,0:T(8,128)(2,1)}, u32[]{:S(2)}) copy-start(bf16[2048,256]{1,0:T(8,128)(2,1)} %w_z.1) | copy-start | bytes 3145732
  7.2 18.2 %copy-start.12 = (f32[4]{0:T(128)S(1)}, f32[4]{0:T(128)}, u32[]{:S(2)}) copy-start(f32[4]{0:T(128)} %param.24) | copy-start | bytes 52
  7.2 18.4 %copy-start.10 = (bf16[4,256]{1,0:T(4,128)(2,1)S(1)}, bf16[4,256]{1,0:T(4,128)(2,1)}, u32[]{:S(2)}) copy-start(bf16[4,256]{1,0:T(4,128)(2,1)} %param.25) | copy-start | bytes 6148
  7.2 18.4 %copy-start.13 = (f32[4]{0:T(128)S(1)}, f32[4]{0:T(128)}, u32[]{:S(2)}) copy-start(f32[4]{0:T(128)} %param.23) | copy-start | bytes 52
  7.2 18.4 %copy-start.14 = (f32[4]{0:T(128)S(1)}, f32[4]{0:T(128)}, u32[]{:S(2)}) copy-start(f32[4]{0:T(128)} %param.22) | copy-start | bytes 52
  7.3 18.4 %copy-start.11 = (f32[256]{0:T(256)S(1)}, f32[256]{0:T(256)}, u32[]{:S(2)}) copy-start(f32[256]{0:T(256)} %param.27) | copy-start | bytes 3076
  7.3 18.4 %copy-start.5 = (bf16[2048,4]{0,1:T(4,128)(2,1)S(1)}, bf16[2048,4]{0,1:T(4,128)(2,1)}, u32[]{:S(2)}) copy-start(bf16[2048,4]{0,1:T(4,128)(2,1)} %param.21) | copy-start | bytes 49156
  7.3 35.0 %all-to-all-start = ((f32[16,16,128]{2,1,0:T(8,128)}), f32[16,16,128]{2,1,0:T(8,128)S(1)}, u32[]{:S(2)}, u32[]{:S(2)}) async-start(f32[16,16,128]{2,1,0:T(8,128)} %shard_map.145), calls=%async_computation | async-start | bytes 262144 | tf_op jit(solution)/shard_map/all_to_all | solution.py:463
  25.4 0.8 %copy-start.1 = (bf16[5,2048]{1,0:T(8,128)(2,1)S(1)}, bf16[5,2048]{1,0:T(8,128)(2,1)}, u32[]{:S(2)}) copy-start(bf16[5,2048]{1,0:T(8,128)(2,1)} %embed) | copy-start | bytes 61444
  26.2 6.2 %copy-start.6 = (bf16[4,256]{1,0:T(4,128)(2,1)S(1)}, bf16[4,256]{1,0:T(4,128)(2,1)}, u32[]{:S(2)}) copy-start(bf16[4,256]{1,0:T(4,128)(2,1)} %conv_bc.1) | copy-start | bytes 6148
  26.2 6.2 %copy-start.8 = (s32[5]{0:T(128)S(1)}, s32[5]{0:T(128)}, u32[]{:S(2)}) copy-start(s32[5]{0:T(128)} %complement.1) | copy-start | bytes 64
  26.2 6.3 %copy-start.9 = (bf16[64,1024]{1,0:T(8,128)(2,1)S(1)}, bf16[64,1024]{1,0:T(8,128)(2,1)}, u32[]{:S(2)}) copy-start(bf16[64,1024]{1,0:T(8,128)(2,1)} %constant.14.clone.grams_in) | copy-start | bytes 393220
  26.6 5.8 %collective-permute-start.1 = (f32[32,256]{1,0:T(8,128)S(1)}, f32[32,256]{1,0:T(8,128)S(1)}, u32[]{:S(2)}, u32[]{:S(2)}) collective-permute-start(f32[32,256]{1,0:T(8,128)S(1)} %shard_map.146.mine), channel_id=1, source_target_pairs={{0,12},{1,13},{2,14},{3,15},{4,8},{5,9},{6,10},{7,11},{8,4},{9,5},... | collective-permute-start | bytes 98312 | tf_op jit(solution)/shard_map/ppermute | solution.py:455
  42.3 15.9 %copy-start.4 = (bf16[256,2048]{1,0:T(8,128)(2,1)S(1)}, bf16[256,2048]{1,0:T(8,128)(2,1)}, u32[]{:S(2)}) copy-start(bf16[256,2048]{1,0:T(8,128)(2,1)} %w_own.1) | copy-start | bytes 3145732

commit v8 on v7

--- a/solution.py
+++ b/solution.py
@@ -71,14 +71,10 @@
     mine = tokens[...].astype(F32)
     other = sibling[...].astype(F32)
     first = lax.rem(seq, 2) == 0
-    send[0, 0:VOCAB, :] = bc[:, :STATE]
-    send[0, 5:7, :] = jnp.where(first, mine, other)
-    send[0, 7:8, :] = jnp.zeros((1, 128), F32)
-    send[0, 8 : 8 + VOCAB, :] = bc[:, STATE:]
-    send[0, 13:15, :] = jnp.where(first, other, mine)
-    send[0, 15:16, :] = jnp.zeros((1, 128), F32)
-    block = send[0]
-    for peer in range(1, CHIPS):
+    own, other = (jnp.where(first, mine, other), jnp.where(first, other, mine))
+    rest = jnp.zeros((1, 128), F32)
+    block = jnp.concatenate([bc[:, :STATE], own, rest, bc[:, STATE:], other, rest], 0).astype(BF16)
+    for peer in range(CHIPS):
         send[peer] = block
 
 
@@ -156,12 +152,12 @@
 ):
     seq, chan = place()
     own_line = 2 * seq + chan // GROUP
+    bc_sum = jnp.zeros((16, 128), F32)
     for chip in range(CHIPS):
-        tok_ref[4 * chip : 4 * chip + 2, :] = received[chip, 5:7, :]
-        tok_ref[4 * chip + 2 : 4 * chip + 4, :] = received[chip, 13:15, :]
-    bc_sum = received[0]
-    for chip in range(1, CHIPS):
-        bc_sum = bc_sum + received[chip]
+        block = received[chip].astype(F32)
+        tok_ref[4 * chip : 4 * chip + 2, :] = block[5:7]
+        tok_ref[4 * chip + 2 : 4 * chip + 4, :] = block[13:15]
+        bc_sum = bc_sum + block
     bc_sum = jnp.where(lax.rem(iota((16, 128), 0), 8) < VOCAB, bc_sum, 0.0)
     bc_sum = bc_sum.astype(BF16).astype(F32)
     bc_tab = jnp.concatenate([bc_sum[0:8], bc_sum[8:16]], 1)
@@ -376,7 +372,7 @@
 
 
 def make_send(*args):
-    return call(send_kernel, jax.ShapeDtypeStruct((CHIPS, 16, 128), F32), [VMEM] * 3, 1, 16)(*args)
+    return call(send_kernel, jax.ShapeDtypeStruct((CHIPS, 16, 128), BF16), [VMEM] * 3, 1, 16)(*args)
 
 
 def make_tables(*args):
@@ -471,8 +467,8 @@
     depth = w_bc.shape[0]
     part = lax.dynamic_slice_in_dim(embed, lax.axis_index("chan") * depth, depth, 1)
     send = make_send(own, with_sibling(own), dot(part, w_bc, (1, 0)))
-    send, embed, conv_x, norm_gain, d_skip, dt_bias, decay_rate = lax.optimization_barrier(
-        (send, embed, conv_x, norm_gain, d_skip, dt_bias, decay_rate)
+    send, embed, norm_gain, d_skip, dt_bias, decay_rate = lax.optimization_barrier(
+        (send, embed, norm_gain, d_skip, dt_bias, decay_rate)
     )
     received = exchange(send, ("seq", "chan"), mixed_groups())
     by_head = jnp.pad(jnp.stack([dt_bias, decay_rate]), ((0, 0), (0, OWN - OWN_HEADS)))

time: 76 us -> 73.3 us (0.964)
  the two profiles are of different devices: /device:TPU:2 before, /device:TPU:4 now
where the time goes in v8:
time: 73.3 us; the launch traced here: 72.8 us
  starting transfers between devices  26 us (35%)
  blocking collectives  25.2 us (34%)
  waiting for transfers between devices  11.8 us (16%)
  Pallas kernels  7.89 us (11%)
  local copies, waits for them, and re-layouts  0.83 us (1%)
  matrix products  0.81 us (1%)
    all_to_all x2, blocking collectives, exchange(): lax.all_to_all(value, axes, 0, 0, tiled=True, axis_index_groups=groups)  25.2 us
    all_to_all x1, starting transfers between devices, exchange(): lax.all_to_all(value, axes, 0, 0, tiled=True, axis_index_groups=groups)  19.2 us
    all_to_all x1, waiting for transfers between devices, exchange(): lax.all_to_all(value, axes, 0, 0, tiled=True, axis_index_groups=groups)  8.08 us
    pallas_call x1, Pallas kernels, make_scan(): call(scan_kernel, (jax.ShapeDtypeStruct((2 * LINE, PAIR), F32), jax.Shape...  4.99 us
    ppermute x2, starting transfers between devices, with_partner(): return lax.ppermute(value, 'chan', pairs)  4.86 us
    ppermute x2, waiting for transfers between devices, with_partner(): return lax.ppermute(value, 'chan', pairs)  3.51 us
    ppermute x1, starting transfers between devices, with_sibling(): lax.ppermute(value, 'seq', [(source, source ^ 1) for source in range(SEQ)])  1.92 us
  transfers between devices with their start and end apart: 4, of which 3 were waited for; matrix products, arithmetic and copies ran while one was open for 1% of the time, Pallas kernels for 2%

profile of v8, /device:TPU:4, one launch (start us, length us, event | category | flops | bytes accessed | tf_op | source)
XLA Modules:
  0.0 72.8 jit_solution(17168651902807067618)
XLA Ops:
  0.0 2.6 %collective-permute-start.2 = (bf16[256,2048]{1,0:T(8,128)(2,1)}, bf16[256,2048]{1,0:T(8,128)(2,1)S(1)}, u32[]{:S(2)}, u32[]{:S(2)}) collective-permute-start(bf16[256,2048]{1,0:T(8,128)(2,1)} %w_own.1), channel_id=1, source_target_pairs={{0,12},{1,13},{2,14},{3,15},{4,8},{5,9},{6,10},{7,11},{8,4},{9,5},... | collective-permute-start | bytes 3145736 | tf_op jit(solution)/shard_map/ppermute | solution.py:451
  2.6 1.9 %collective-permute-start = (s32[2,128]{1,0:T(2,128)S(1)}, s32[2,128]{1,0:T(2,128)S(1)}, u32[]{:S(2)}, u32[]{:S(2)}) collective-permute-start(s32[2,128]{1,0:T(2,128)S(1)} %bitcast.7), channel_id=1, source_target_pairs={{0,16},{16,0},{32,48},{48,32},{64,80},{80,64},{96,112},{112,96},{1... | collective-permute-start | bytes 3080 | tf_op jit(solution)/shard_map/ppermute | solution.py:455
  4.5 0.8 %fusion.state_map = f32[5,256]{1,0:T(8,128)S(1)} fusion(bf16[128,256]{1,0:T(8,128)(2,1)S(1)} %copy-done, bf16[5,2048]{1,0:T(8,128)(2,1)} %embed, s32[]{:T(128)S(6)} %select_n.3), kind=kOutput, calls=%fused_computation.2 | convolution fusion | flops 327680 | bytes 72708 | tf_op jit(solution)/shard_map/dot_general | solution.py:61
  5.4 0.0 copy-start.12
  5.4 0.0 copy-start.2
  5.4 0.0 copy-start.3
  5.4 0.2 collective-permute-done.sibling
  5.6 0.6 shard_map.145
  6.3 0.1 broadcast_in_dim.3
  6.3 0.1 stack_reshape.3
  6.4 19.2 %all-to-all-start = ((bf16[16,16,128]{2,1,0:T(8,128)(2,1)}), bf16[16,16,128]{2,1,0:T(8,128)(2,1)S(1)}, u32[]{:S(2)}, u32[]{:S(2)}) async-start(bf16[16,16,128]{2,1,0:T(8,128)(2,1)} %shard_map.145), calls=%async_computation | async-start | bytes 131072 | tf_op jit(solution)/shard_map/all_to_all | solution.py:459
  25.7 0.0 copy-start.5
  25.8 0.6 copy-done.5
  26.4 0.4 shard_map.146.mine
  26.8 2.3 %collective-permute-start.1 = (f32[32,256]{1,0:T(8,128)S(1)}, f32[32,256]{1,0:T(8,128)S(1)}, u32[]{:S(2)}, u32[]{:S(2)}) collective-permute-start(f32[32,256]{1,0:T(8,128)S(1)} %shard_map.146.mine), channel_id=1, source_target_pairs={{0,12},{1,13},{2,14},{3,15},{4,8},{5,9},{6,10},{7,11},{8,4},{9,5},... | collective-permute-start | bytes 98312 | tf_op jit(solution)/shard_map/ppermute | solution.py:451
  29.1 3.5 %collective-permute-done.1.other = f32[32,256]{1,0:T(8,128)S(1)} collective-permute-done((f32[32,256]{1,0:T(8,128)S(1)}, f32[32,256]{1,0:T(8,128)S(1)}, u32[]{:S(2)}, u32[]{:S(2)}) %collective-permute-start.1) | collective-permute-done | bytes 32800 | tf_op jit(solution)/shard_map/ppermute | solution.py:451
  32.6 0.0 collective-permute-done.2.w_other
  32.7 0.6 shard_map.147
  33.3 8.1 %all-to-all-done.received = bf16[16,16,128]{2,1,0:T(8,128)(2,1)S(1)} async-done(((bf16[16,16,128]{2,1,0:T(8,128)(2,1)}), bf16[16,16,128]{2,1,0:T(8,128)(2,1)S(1)}, u32[]{:S(2)}, u32[]{:S(2)}) %all-to-all-start) | async-done | bytes 65568 | tf_op jit(solution)/shard_map/all_to_all | solution.py:459
  41.4 5.0 %shard_map.148 = (f32[256,512]{1,0:T(8,128)S(1)}, f32[8,2,128]{2,1,0:T(2,128)S(1)}) custom-call(bf16[16,16,128]{2,1,0:T(8,128)(2,1)S(1)} %all-to-all-done.received, bf16[64,2048]{1,0:T(8,128)(2,1)S(1)} %get-tuple-element.25.tables, f32[16,512]{1,0:T(8,128)S(1)} %get-tuple-element.26.rows, f32[16,128]{1,0:T(8,128)S(1)} %get-tuple-element.27.step_at), custom_call_target="tpu_custom_call" | custom-call | flops 7000000000 | bytes 7340032 | tf_op jit(solution)/shard_map/pallas_call | solution.py:398
  46.4 9.8 %all_to_all.15.squares = f32[8,2,128]{2,1,0:T(2,128)S(1)} all-to-all(f32[8,2,128]{2,1,0:T(2,128)S(1)} %get-tuple-element.28), channel_id=1, replica_groups={{0,1,2,3,4,5,6,7},{8,9,10,11,12,13,14,15},{16,17,18,19,20,21,22,23},{24..., dimensions={0} | all-to-all | bytes 16384 | tf_op jit(solution)/shard_map/all_to_all | solution.py:459
  56.2 0.5 shard_map.149
  56.7 15.4 %all_to_all.16.received = bf16[8,16,2048]{2,1,0:T(8,128)(2,1)S(1)} all-to-all(bf16[8,16,2048]{2,1,0:T(8,128)(2,1)S(1)} %shard_map.149), channel_id=1, replica_groups={{0,1,2,3,4,5,6,7},{8,9,10,11,12,13,14,15},{16,17,18,19,20,21,22,23},{24..., dimensions={0} | all-to-all | bytes 1048576 | tf_op jit(solution)/shard_map/all_to_all | solution.py:459
  72.1 0.7 shard_map.150
  (28 shorter events, 0.1 us)
Async XLA Ops:
  0.0 4.5 %copy-start = (bf16[128,256]{1,0:T(8,128)(2,1)S(1)}, bf16[128,256]{1,0:T(8,128)(2,1)}, u32[]{:S(2)}) copy-start(bf16[128,256]{1,0:T(8,128)(2,1)} %param.20) | copy-start | bytes 196612
  0.0 2.6 %copy-start.7 = (s32[256]{0:T(256)S(1)}, s32[256]{0:T(256)}, u32[]{:S(2)}) copy-start(s32[256]{0:T(256)} %param.15) | copy-start | bytes 3076
  0.0 32.6 %collective-permute-start.2 = (bf16[256,2048]{1,0:T(8,128)(2,1)}, bf16[256,2048]{1,0:T(8,128)(2,1)S(1)}, u32[]{:S(2)}, u32[]{:S(2)}) collective-permute-start(bf16[256,2048]{1,0:T(8,128)(2,1)} %w_own.1), channel_id=1, source_target_pairs={{0,12},{1,13},{2,14},{3,15},{4,8},{5,9},{6,10},{7,11},{8,4},{9,5},... | collective-permute-start | bytes 3145736 | tf_op jit(solution)/shard_map/ppermute | solution.py:451
  2.6 3.0 %collective-permute-start = (s32[2,128]{1,0:T(2,128)S(1)}, s32[2,128]{1,0:T(2,128)S(1)}, u32[]{:S(2)}, u32[]{:S(2)}) collective-permute-start(s32[2,128]{1,0:T(2,128)S(1)} %bitcast.7), channel_id=1, source_target_pairs={{0,16},{16,0},{32,48},{48,32},{64,80},{80,64},{96,112},{112,96},{1... | collective-permute-start | bytes 3080 | tf_op jit(solution)/shard_map/ppermute | solution.py:455
  4.5 0.8 %copy-start.10 = (bf16[4,256]{1,0:T(4,128)(2,1)S(1)}, bf16[4,256]{1,0:T(4,128)(2,1)}, u32[]{:S(2)}) copy-start(bf16[4,256]{1,0:T(4,128)(2,1)} %param.25) | copy-start | bytes 6148
  5.4 0.9 %copy-start.12 = (f32[4]{0:T(128)S(1)}, f32[4]{0:T(128)}, u32[]{:S(2)}) copy-start(f32[4]{0:T(128)} %param.24) | copy-start | bytes 52
  5.4 20.4 %copy-start.2 = (bf16[2048,256]{1,0:T(8,128)(2,1)S(1)}, bf16[2048,256]{1,0:T(8,128)(2,1)}, u32[]{:S(2)}) copy-start(bf16[2048,256]{1,0:T(8,128)(2,1)} %w_x.1) | copy-start | bytes 3145732
  5.4 20.4 %copy-start.3 = (bf16[2048,256]{1,0:T(8,128)(2,1)S(1)}, bf16[2048,256]{1,0:T(8,128)(2,1)}, u32[]{:S(2)}) copy-start(bf16[2048,256]{1,0:T(8,128)(2,1)} %w_z.1) | copy-start | bytes 3145732
  6.4 19.3 %copy-start.13 = (f32[4]{0:T(128)S(1)}, f32[4]{0:T(128)}, u32[]{:S(2)}) copy-start(f32[4]{0:T(128)} %param.23) | copy-start | bytes 52
  6.4 19.3 %copy-start.14 = (f32[4]{0:T(128)S(1)}, f32[4]{0:T(128)}, u32[]{:S(2)}) copy-start(f32[4]{0:T(128)} %param.22) | copy-start | bytes 52
  6.4 19.3 %copy-start.11 = (f32[256]{0:T(256)S(1)}, f32[256]{0:T(256)}, u32[]{:S(2)}) copy-start(f32[256]{0:T(256)} %param.27) | copy-start | bytes 3076
  6.4 19.4 %copy-start.1 = (bf16[5,2048]{1,0:T(8,128)(2,1)S(1)}, bf16[5,2048]{1,0:T(8,128)(2,1)}, u32[]{:S(2)}) copy-start(bf16[5,2048]{1,0:T(8,128)(2,1)} %embed) | copy-start | bytes 61444
  6.4 34.9 %all-to-all-start = ((bf16[16,16,128]{2,1,0:T(8,128)(2,1)}), bf16[16,16,128]{2,1,0:T(8,128)(2,1)S(1)}, u32[]{:S(2)}, u32[]{:S(2)}) async-start(bf16[16,16,128]{2,1,0:T(8,128)(2,1)} %shard_map.145), calls=%async_computation | async-start | bytes 131072 | tf_op jit(solution)/shard_map/all_to_all | solution.py:459
  25.7 0.7 copy-start.5
  26.4 6.2 %copy-start.6 = (bf16[4,256]{1,0:T(4,128)(2,1)S(1)}, bf16[4,256]{1,0:T(4,128)(2,1)}, u32[]{:S(2)}) copy-start(bf16[4,256]{1,0:T(4,128)(2,1)} %conv_bc.1) | copy-start | bytes 6148
  26.4 6.2 %copy-start.8 = (s32[5]{0:T(128)S(1)}, s32[5]{0:T(128)}, u32[]{:S(2)}) copy-start(s32[5]{0:T(128)} %complement.1) | copy-start | bytes 64
  26.4 6.3 %copy-start.9 = (bf16[64,1024]{1,0:T(8,128)(2,1)S(1)}, bf16[64,1024]{1,0:T(8,128)(2,1)}, u32[]{:S(2)}) copy-start(bf16[64,1024]{1,0:T(8,128)(2,1)} %constant.14.clone.grams_in) | copy-start | bytes 393220
  26.8 5.8 %collective-permute-start.1 = (f32[32,256]{1,0:T(8,128)S(1)}, f32[32,256]{1,0:T(8,128)S(1)}, u32[]{:S(2)}, u32[]{:S(2)}) collective-permute-start(f32[32,256]{1,0:T(8,128)S(1)} %shard_map.146.mine), channel_id=1, source_target_pairs={{0,12},{1,13},{2,14},{3,15},{4,8},{5,9},{6,10},{7,11},{8,4},{9,5},... | collective-permute-start | bytes 98312 | tf_op jit(solution)/shard_map/ppermute | solution.py:451
  41.4 14.8 %copy-start.4 = (bf16[256,2048]{1,0:T(8,128)(2,1)S(1)}, bf16[256,2048]{1,0:T(8,128)(2,1)}, u32[]{:S(2)}) copy-start(bf16[256,2048]{1,0:T(8,128)(2,1)} %w_own.1) | copy-start | bytes 3145732

commit v9 on v8

--- a/solution.py
+++ b/solution.py
@@ -260,6 +260,7 @@
                 jnp.concatenate(cumul + [jnp.zeros((LINE - PAIR_HEADS, LINE), F32)], 0)
             )
             scores = dot(c_out.astype(BF16), b_in, (1, 1))
+            done["c_out", strand] = c_out.astype(BF16)
             yield
             for head in range(PAIR_HEADS):
                 at = slice(OWN * (head // OWN_HEADS), OWN * (head // OWN_HEADS + 1))
@@ -267,7 +268,7 @@
                 decayed = jnp.exp(jnp.where(causal, column_of - cumul[head], -1e30))
                 left = (decayed * (scores * step[head])).astype(BF16)
                 right = jnp.where(head_of == head % OWN_HEADS, done["values"][own, at], 0.0).astype(BF16)
-                done[strand, head] = (left, right, (c_out * jnp.exp(column_of)).astype(BF16))
+                done[strand, head] = (left, right, jnp.exp(column_of))
                 yield
 
     steps = own_steps()
@@ -308,25 +309,26 @@
             * jnp.broadcast_to(weight_of[head : head + 1], (HEAD_DIM, 1024)).astype(BF16)
             for head in range(PAIR_HEADS)
         ]
-        states.append(jnp.transpose(dot(jnp.concatenate(weighted, 0), done["gram_b"], (1, 1))))
+        states.append(dot(jnp.concatenate(weighted, 0), done["gram_b"], (1, 1)).astype(BF16))
 
     squares = []
     for strand in range(2):
         own = slice(LINE * strand, LINE * (strand + 1))
         squared = jnp.zeros((LINE, LINE), F32)
+        carried = dot(done["c_out", strand], states[strand], (1, 1))
         for side in range(2):
             at = slice(OWN * side, OWN * (side + 1))
             values = done["values"][own, at]
             heads = [done[strand, OWN_HEADS * side + near] for near in range(OWN_HEADS)]
-            tail = [
-                jnp.where(head_of == near, states[strand][:, at], 0.0).astype(BF16)
-                for near in range(OWN_HEADS)
-            ]
+            growth = jnp.zeros((LINE, OWN), F32)
+            for near in range(OWN_HEADS):
+                growth = jnp.where(head_of == near, heads[near][2], growth)
             ssd = dot(
-                jnp.concatenate([head[0] for head in heads] + [head[2] for head in heads], 1),
-                jnp.concatenate([head[1] for head in heads] + tail, 0),
+                jnp.concatenate([head[0] for head in heads], 1),
+                jnp.concatenate([head[1] for head in heads], 0),
                 (1, 0),
             )
+            ssd = ssd + growth * carried[:, at]
             gated = (ssd + values * rows[5:6, at]) * done["gate"][own, at]
             out[own, at] = gated * rows[4:5, at]
             squared = squared + gated[:, :LINE] * gated[:, :LINE] + gated[:, LINE:] * gated[:, LINE:]

time: 73.3 us -> 73 us (level)
  no operation moved by 1% of the time
where the time goes in v9:
time: 73 us; the launch traced here: 72.5 us
  starting transfers between devices  26 us (36%)
  blocking collectives  25.2 us (35%)
  waiting for transfers between devices  11.8 us (16%)
  Pallas kernels  7.63 us (10%)
  local copies, waits for them, and re-layouts  0.83 us (1%)
  matrix products  0.81 us (1%)
    all_to_all x2, blocking collectives, exchange(): lax.all_to_all(value, axes, 0, 0, tiled=True, axis_index_groups=groups)  25.2 us
    all_to_all x1, starting transfers between devices, exchange(): lax.all_to_all(value, axes, 0, 0, tiled=True, axis_index_groups=groups)  19.2 us
    all_to_all x1, waiting for transfers between devices, exchange(): lax.all_to_all(value, axes, 0, 0, tiled=True, axis_index_groups=groups)  8.08 us
    ppermute x2, starting transfers between devices, with_partner(): return lax.ppermute(value, 'chan', pairs)  4.86 us
    pallas_call x1, Pallas kernels, make_scan(): call(scan_kernel, (jax.ShapeDtypeStruct((2 * LINE, PAIR), F32), jax.Shape...  4.73 us
    ppermute x2, waiting for transfers between devices, with_partner(): return lax.ppermute(value, 'chan', pairs)  3.51 us
    ppermute x1, starting transfers between devices, with_sibling(): lax.ppermute(value, 'seq', [(source, source ^ 1) for source in range(SEQ)])  1.92 us
  transfers between devices with their start and end apart: 4, of which 3 were waited for; matrix products, arithmetic and copies ran while one was open for 1% of the time, Pallas kernels for 2%

profile of v9, /device:TPU:4, one launch (start us, length us, event | category | flops | bytes accessed | tf_op | source)
XLA Modules:
  0.0 72.5 jit_solution(17461997209907411251)
XLA Ops:
  0.0 2.6 %collective-permute-start.2 = (bf16[256,2048]{1,0:T(8,128)(2,1)}, bf16[256,2048]{1,0:T(8,128)(2,1)S(1)}, u32[]{:S(2)}, u32[]{:S(2)}) collective-permute-start(bf16[256,2048]{1,0:T(8,128)(2,1)} %w_own.1), channel_id=1, source_target_pairs={{0,12},{1,13},{2,14},{3,15},{4,8},{5,9},{6,10},{7,11},{8,4},{9,5},... | collective-permute-start | bytes 3145736 | tf_op jit(solution)/shard_map/ppermute | solution.py:453
  2.6 1.9 %collective-permute-start = (s32[2,128]{1,0:T(2,128)S(1)}, s32[2,128]{1,0:T(2,128)S(1)}, u32[]{:S(2)}, u32[]{:S(2)}) collective-permute-start(s32[2,128]{1,0:T(2,128)S(1)} %bitcast.7), channel_id=1, source_target_pairs={{0,16},{16,0},{32,48},{48,32},{64,80},{80,64},{96,112},{112,96},{1... | collective-permute-start | bytes 3080 | tf_op jit(solution)/shard_map/ppermute | solution.py:457
  4.5 0.8 %fusion.state_map = f32[5,256]{1,0:T(8,128)S(1)} fusion(bf16[128,256]{1,0:T(8,128)(2,1)S(1)} %copy-done, bf16[5,2048]{1,0:T(8,128)(2,1)} %embed, s32[]{:T(128)S(6)} %select_n.3), kind=kOutput, calls=%fused_computation.2 | convolution fusion | flops 327680 | bytes 72708 | tf_op jit(solution)/shard_map/dot_general | solution.py:61
  5.4 0.0 copy-start.12
  5.4 0.0 copy-start.2
  5.4 0.0 copy-start.3
  5.4 0.2 collective-permute-done.sibling
  5.6 0.6 shard_map.145
  6.3 0.1 broadcast_in_dim.3
  6.3 0.1 stack_reshape.3
  6.4 19.2 %all-to-all-start = ((bf16[16,16,128]{2,1,0:T(8,128)(2,1)}), bf16[16,16,128]{2,1,0:T(8,128)(2,1)S(1)}, u32[]{:S(2)}, u32[]{:S(2)}) async-start(bf16[16,16,128]{2,1,0:T(8,128)(2,1)} %shard_map.145), calls=%async_computation | async-start | bytes 131072 | tf_op jit(solution)/shard_map/all_to_all | solution.py:461
  25.7 0.0 copy-start.5
  25.8 0.6 copy-done.5
  26.4 0.4 shard_map.146.mine
  26.8 2.3 %collective-permute-start.1 = (f32[32,256]{1,0:T(8,128)S(1)}, f32[32,256]{1,0:T(8,128)S(1)}, u32[]{:S(2)}, u32[]{:S(2)}) collective-permute-start(f32[32,256]{1,0:T(8,128)S(1)} %shard_map.146.mine), channel_id=1, source_target_pairs={{0,12},{1,13},{2,14},{3,15},{4,8},{5,9},{6,10},{7,11},{8,4},{9,5},... | collective-permute-start | bytes 98312 | tf_op jit(solution)/shard_map/ppermute | solution.py:453
  29.1 3.5 %collective-permute-done.1.other = f32[32,256]{1,0:T(8,128)S(1)} collective-permute-done((f32[32,256]{1,0:T(8,128)S(1)}, f32[32,256]{1,0:T(8,128)S(1)}, u32[]{:S(2)}, u32[]{:S(2)}) %collective-permute-start.1) | collective-permute-done | bytes 32800 | tf_op jit(solution)/shard_map/ppermute | solution.py:453
  32.6 0.0 collective-permute-done.2.w_other
  32.7 0.6 shard_map.147
  33.3 8.1 %all-to-all-done.received = bf16[16,16,128]{2,1,0:T(8,128)(2,1)S(1)} async-done(((bf16[16,16,128]{2,1,0:T(8,128)(2,1)}), bf16[16,16,128]{2,1,0:T(8,128)(2,1)S(1)}, u32[]{:S(2)}, u32[]{:S(2)}) %all-to-all-start) | async-done | bytes 65568 | tf_op jit(solution)/shard_map/all_to_all | solution.py:461
  41.4 4.7 %shard_map.148 = (f32[256,512]{1,0:T(8,128)S(1)}, f32[8,2,128]{2,1,0:T(2,128)S(1)}) custom-call(bf16[16,16,128]{2,1,0:T(8,128)(2,1)S(1)} %all-to-all-done.received, bf16[64,2048]{1,0:T(8,128)(2,1)S(1)} %get-tuple-element.25.tables, f32[16,512]{1,0:T(8,128)S(1)} %get-tuple-element.26.rows, f32[16,128]{1,0:T(8,128)S(1)} %get-tuple-element.27.step_at), custom_call_target="tpu_custom_call" | custom-call | flops 7000000000 | bytes 7340032 | tf_op jit(solution)/shard_map/pallas_call | solution.py:400
  46.1 9.8 %all_to_all.15.squares = f32[8,2,128]{2,1,0:T(2,128)S(1)} all-to-all(f32[8,2,128]{2,1,0:T(2,128)S(1)} %get-tuple-element.28), channel_id=1, replica_groups={{0,1,2,3,4,5,6,7},{8,9,10,11,12,13,14,15},{16,17,18,19,20,21,22,23},{24..., dimensions={0} | all-to-all | bytes 16384 | tf_op jit(solution)/shard_map/all_to_all | solution.py:461
  55.9 0.5 shard_map.149
  56.5 15.4 %all_to_all.16.received = bf16[8,16,2048]{2,1,0:T(8,128)(2,1)S(1)} all-to-all(bf16[8,16,2048]{2,1,0:T(8,128)(2,1)S(1)} %shard_map.149), channel_id=1, replica_groups={{0,1,2,3,4,5,6,7},{8,9,10,11,12,13,14,15},{16,17,18,19,20,21,22,23},{24..., dimensions={0} | all-to-all | bytes 1048576 | tf_op jit(solution)/shard_map/all_to_all | solution.py:461
  71.8 0.7 shard_map.150
  (28 shorter events, 0.1 us)
Async XLA Ops:
  0.0 4.5 %copy-start = (bf16[128,256]{1,0:T(8,128)(2,1)S(1)}, bf16[128,256]{1,0:T(8,128)(2,1)}, u32[]{:S(2)}) copy-start(bf16[128,256]{1,0:T(8,128)(2,1)} %param.20) | copy-start | bytes 196612
  0.0 2.6 %copy-start.7 = (s32[256]{0:T(256)S(1)}, s32[256]{0:T(256)}, u32[]{:S(2)}) copy-start(s32[256]{0:T(256)} %param.15) | copy-start | bytes 3076
  0.0 32.6 %collective-permute-start.2 = (bf16[256,2048]{1,0:T(8,128)(2,1)}, bf16[256,2048]{1,0:T(8,128)(2,1)S(1)}, u32[]{:S(2)}, u32[]{:S(2)}) collective-permute-start(bf16[256,2048]{1,0:T(8,128)(2,1)} %w_own.1), channel_id=1, source_target_pairs={{0,12},{1,13},{2,14},{3,15},{4,8},{5,9},{6,10},{7,11},{8,4},{9,5},... | collective-permute-start | bytes 3145736 | tf_op jit(solution)/shard_map/ppermute | solution.py:453
  2.6 3.0 %collective-permute-start = (s32[2,128]{1,0:T(2,128)S(1)}, s32[2,128]{1,0:T(2,128)S(1)}, u32[]{:S(2)}, u32[]{:S(2)}) collective-permute-start(s32[2,128]{1,0:T(2,128)S(1)} %bitcast.7), channel_id=1, source_target_pairs={{0,16},{16,0},{32,48},{48,32},{64,80},{80,64},{96,112},{112,96},{1... | collective-permute-start | bytes 3080 | tf_op jit(solution)/shard_map/ppermute | solution.py:457
  4.5 0.8 %copy-start.10 = (bf16[4,256]{1,0:T(4,128)(2,1)S(1)}, bf16[4,256]{1,0:T(4,128)(2,1)}, u32[]{:S(2)}) copy-start(bf16[4,256]{1,0:T(4,128)(2,1)} %param.25) | copy-start | bytes 6148
  5.4 0.9 %copy-start.12 = (f32[4]{0:T(128)S(1)}, f32[4]{0:T(128)}, u32[]{:S(2)}) copy-start(f32[4]{0:T(128)} %param.24) | copy-start | bytes 52
  5.4 20.4 %copy-start.2 = (bf16[2048,256]{1,0:T(8,128)(2,1)S(1)}, bf16[2048,256]{1,0:T(8,128)(2,1)}, u32[]{:S(2)}) copy-start(bf16[2048,256]{1,0:T(8,128)(2,1)} %w_x.1) | copy-start | bytes 3145732
  5.4 20.4 %copy-start.3 = (bf16[2048,256]{1,0:T(8,128)(2,1)S(1)}, bf16[2048,256]{1,0:T(8,128)(2,1)}, u32[]{:S(2)}) copy-start(bf16[2048,256]{1,0:T(8,128)(2,1)} %w_z.1) | copy-start | bytes 3145732
  6.4 19.3 %copy-start.13 = (f32[4]{0:T(128)S(1)}, f32[4]{0:T(128)}, u32[]{:S(2)}) copy-start(f32[4]{0:T(128)} %param.23) | copy-start | bytes 52
  6.4 19.3 %copy-start.14 = (f32[4]{0:T(128)S(1)}, f32[4]{0:T(128)}, u32[]{:S(2)}) copy-start(f32[4]{0:T(128)} %param.22) | copy-start | bytes 52
  6.4 19.3 %copy-start.11 = (f32[256]{0:T(256)S(1)}, f32[256]{0:T(256)}, u32[]{:S(2)}) copy-start(f32[256]{0:T(256)} %param.27) | copy-start | bytes 3076
  6.4 19.4 %copy-start.1 = (bf16[5,2048]{1,0:T(8,128)(2,1)S(1)}, bf16[5,2048]{1,0:T(8,128)(2,1)}, u32[]{:S(2)}) copy-start(bf16[5,2048]{1,0:T(8,128)(2,1)} %embed) | copy-start | bytes 61444
  6.4 34.9 %all-to-all-start = ((bf16[16,16,128]{2,1,0:T(8,128)(2,1)}), bf16[16,16,128]{2,1,0:T(8,128)(2,1)S(1)}, u32[]{:S(2)}, u32[]{:S(2)}) async-start(bf16[16,16,128]{2,1,0:T(8,128)(2,1)} %shard_map.145), calls=%async_computation | async-start | bytes 131072 | tf_op jit(solution)/shard_map/all_to_all | solution.py:461
  25.7 0.7 copy-start.5
  26.4 6.2 %copy-start.6 = (bf16[4,256]{1,0:T(4,128)(2,1)S(1)}, bf16[4,256]{1,0:T(4,128)(2,1)}, u32[]{:S(2)}) copy-start(bf16[4,256]{1,0:T(4,128)(2,1)} %conv_bc.1) | copy-start | bytes 6148
  26.4 6.2 %copy-start.8 = (s32[5]{0:T(128)S(1)}, s32[5]{0:T(128)}, u32[]{:S(2)}) copy-start(s32[5]{0:T(128)} %complement.1) | copy-start | bytes 64
  26.4 6.3 %copy-start.9 = (bf16[64,1024]{1,0:T(8,128)(2,1)S(1)}, bf16[64,1024]{1,0:T(8,128)(2,1)}, u32[]{:S(2)}) copy-start(bf16[64,1024]{1,0:T(8,128)(2,1)} %constant.14.clone.grams_in) | copy-start | bytes 393220
  26.8 5.8 %collective-permute-start.1 = (f32[32,256]{1,0:T(8,128)S(1)}, f32[32,256]{1,0:T(8,128)S(1)}, u32[]{:S(2)}, u32[]{:S(2)}) collective-permute-start(f32[32,256]{1,0:T(8,128)S(1)} %shard_map.146.mine), channel_id=1, source_target_pairs={{0,12},{1,13},{2,14},{3,15},{4,8},{5,9},{6,10},{7,11},{8,4},{9,5},... | collective-permute-start | bytes 98312 | tf_op jit(solution)/shard_map/ppermute | solution.py:453
  41.4 14.6 %copy-start.4 = (bf16[256,2048]{1,0:T(8,128)(2,1)S(1)}, bf16[256,2048]{1,0:T(8,128)(2,1)}, u32[]{:S(2)}) copy-start(bf16[256,2048]{1,0:T(8,128)(2,1)} %w_own.1) | copy-start | bytes 3145732

commit v10 on v9

--- a/solution.py
+++ b/solution.py
@@ -434,7 +434,7 @@
     side = range(SIDE)
     return [
         [
-            device(2 * (SIDE * y + high) + core, (y + right) % SIDE * SIDE + (high + up) % SIDE)
+            device(2 * (SIDE * y + high) + core, (y ^ right) * SIDE + (high ^ up))
             for y in side
             for high in side
         ]

time: 73 us -> 73.2 us (level)
  no operation moved by 1% of the time
where the time goes in v10:
time: 73.2 us; the launch traced here: 72.7 us
  starting transfers between devices  25.7 us (35%)
  blocking collectives  25.4 us (35%)
  waiting for transfers between devices  12.2 us (17%)
  Pallas kernels  7.62 us (10%)
  local copies, waits for them, and re-layouts  0.83 us (1%)
  matrix products  0.81 us (1%)
    all_to_all x2, blocking collectives, exchange(): lax.all_to_all(value, axes, 0, 0, tiled=True, axis_index_groups=groups)  25.4 us
    all_to_all x1, starting transfers between devices, exchange(): lax.all_to_all(value, axes, 0, 0, tiled=True, axis_index_groups=groups)  19.2 us
    all_to_all x1, waiting for transfers between devices, exchange(): lax.all_to_all(value, axes, 0, 0, tiled=True, axis_index_groups=groups)  8.08 us
    pallas_call x1, Pallas kernels, make_scan(): call(scan_kernel, (jax.ShapeDtypeStruct((2 * LINE, PAIR), F32), jax.Shape...  4.73 us
    ppermute x2, starting transfers between devices, with_partner(): return lax.ppermute(value, 'chan', pairs)  4.49 us
    ppermute x2, waiting for transfers between devices, with_partner(): return lax.ppermute(value, 'chan', pairs)  3.88 us
    ppermute x1, starting transfers between devices, with_sibling(): lax.ppermute(value, 'seq', [(source, source ^ 1) for source in range(SEQ)])  1.92 us
  transfers between devices with their start and end apart: 4, of which 3 were waited for; matrix products, arithmetic and copies ran while one was open for 1% of the time, Pallas kernels for 2%

profile of v10, /device:TPU:4, one launch (start us, length us, event | category | flops | bytes accessed | tf_op | source)
XLA Modules:
  0.0 72.7 jit_solution(13262959838964902325)
XLA Ops:
  0.0 2.6 %collective-permute-start.2 = (bf16[256,2048]{1,0:T(8,128)(2,1)}, bf16[256,2048]{1,0:T(8,128)(2,1)S(1)}, u32[]{:S(2)}, u32[]{:S(2)}) collective-permute-start(bf16[256,2048]{1,0:T(8,128)(2,1)} %w_own.1), channel_id=1, source_target_pairs={{0,12},{1,13},{2,14},{3,15},{4,8},{5,9},{6,10},{7,11},{8,4},{9,5},... | collective-permute-start | bytes 3145736 | tf_op jit(solution)/shard_map/ppermute | solution.py:453
  2.6 1.9 %collective-permute-start = (s32[2,128]{1,0:T(2,128)S(1)}, s32[2,128]{1,0:T(2,128)S(1)}, u32[]{:S(2)}, u32[]{:S(2)}) collective-permute-start(s32[2,128]{1,0:T(2,128)S(1)} %bitcast.7), channel_id=1, source_target_pairs={{0,16},{16,0},{32,48},{48,32},{64,80},{80,64},{96,112},{112,96},{1... | collective-permute-start | bytes 3080 | tf_op jit(solution)/shard_map/ppermute | solution.py:457
  4.5 0.8 %fusion.state_map = f32[5,256]{1,0:T(8,128)S(1)} fusion(bf16[128,256]{1,0:T(8,128)(2,1)S(1)} %copy-done, bf16[5,2048]{1,0:T(8,128)(2,1)} %embed, s32[]{:T(128)S(6)} %select_n.3), kind=kOutput, calls=%fused_computation.2 | convolution fusion | flops 327680 | bytes 72708 | tf_op jit(solution)/shard_map/dot_general | solution.py:61
  5.4 0.0 copy-start.12
  5.4 0.0 copy-start.2
  5.4 0.0 copy-start.3
  5.4 0.2 collective-permute-done.sibling
  5.6 0.6 shard_map.145
  6.3 0.1 broadcast_in_dim.3
  6.3 0.1 stack_reshape.3
  6.4 19.2 %all-to-all-start = ((bf16[16,16,128]{2,1,0:T(8,128)(2,1)}), bf16[16,16,128]{2,1,0:T(8,128)(2,1)S(1)}, u32[]{:S(2)}, u32[]{:S(2)}) async-start(bf16[16,16,128]{2,1,0:T(8,128)(2,1)} %shard_map.145), calls=%async_computation | async-start | bytes 131072 | tf_op jit(solution)/shard_map/all_to_all | solution.py:461
  25.7 0.0 copy-start.5
  25.8 0.6 copy-done.5
  26.4 0.4 shard_map.146.mine
  26.8 1.9 %collective-permute-start.1 = (f32[32,256]{1,0:T(8,128)S(1)}, f32[32,256]{1,0:T(8,128)S(1)}, u32[]{:S(2)}, u32[]{:S(2)}) collective-permute-start(f32[32,256]{1,0:T(8,128)S(1)} %shard_map.146.mine), channel_id=1, source_target_pairs={{0,12},{1,13},{2,14},{3,15},{4,8},{5,9},{6,10},{7,11},{8,4},{9,5},... | collective-permute-start | bytes 98312 | tf_op jit(solution)/shard_map/ppermute | solution.py:453
  28.8 3.9 %collective-permute-done.1.other = f32[32,256]{1,0:T(8,128)S(1)} collective-permute-done((f32[32,256]{1,0:T(8,128)S(1)}, f32[32,256]{1,0:T(8,128)S(1)}, u32[]{:S(2)}, u32[]{:S(2)}) %collective-permute-start.1) | collective-permute-done | bytes 32800 | tf_op jit(solution)/shard_map/ppermute | solution.py:453
  32.6 0.0 collective-permute-done.2.w_other
  32.7 0.6 shard_map.147
  33.3 8.1 %all-to-all-done.received = bf16[16,16,128]{2,1,0:T(8,128)(2,1)S(1)} async-done(((bf16[16,16,128]{2,1,0:T(8,128)(2,1)}), bf16[16,16,128]{2,1,0:T(8,128)(2,1)S(1)}, u32[]{:S(2)}, u32[]{:S(2)}) %all-to-all-start) | async-done | bytes 65568 | tf_op jit(solution)/shard_map/all_to_all | solution.py:461
  41.4 4.7 %shard_map.148 = (f32[256,512]{1,0:T(8,128)S(1)}, f32[8,2,128]{2,1,0:T(2,128)S(1)}) custom-call(bf16[16,16,128]{2,1,0:T(8,128)(2,1)S(1)} %all-to-all-done.received, bf16[64,2048]{1,0:T(8,128)(2,1)S(1)} %get-tuple-element.25.tables, f32[16,512]{1,0:T(8,128)S(1)} %get-tuple-element.26.rows, f32[16,128]{1,0:T(8,128)S(1)} %get-tuple-element.27.step_at), custom_call_target="tpu_custom_call" | custom-call | flops 7000000000 | bytes 7340032 | tf_op jit(solution)/shard_map/pallas_call | solution.py:400
  46.1 10.0 %all_to_all.15.squares = f32[8,2,128]{2,1,0:T(2,128)S(1)} all-to-all(f32[8,2,128]{2,1,0:T(2,128)S(1)} %get-tuple-element.28), channel_id=1, replica_groups={{0,1,2,3,4,5,6,7},{8,9,10,11,12,13,14,15},{16,17,18,19,20,21,22,23},{24..., dimensions={0} | all-to-all | bytes 16384 | tf_op jit(solution)/shard_map/all_to_all | solution.py:461
  56.1 0.5 shard_map.149
  56.7 15.4 %all_to_all.16.received = bf16[8,16,2048]{2,1,0:T(8,128)(2,1)S(1)} all-to-all(bf16[8,16,2048]{2,1,0:T(8,128)(2,1)S(1)} %shard_map.149), channel_id=1, replica_groups={{0,1,2,3,4,5,6,7},{8,9,10,11,12,13,14,15},{16,17,18,19,20,21,22,23},{24..., dimensions={0} | all-to-all | bytes 1048576 | tf_op jit(solution)/shard_map/all_to_all | solution.py:461
  72.0 0.7 shard_map.150
  (28 shorter events, 0.1 us)
Async XLA Ops:
  0.0 4.5 %copy-start = (bf16[128,256]{1,0:T(8,128)(2,1)S(1)}, bf16[128,256]{1,0:T(8,128)(2,1)}, u32[]{:S(2)}) copy-start(bf16[128,256]{1,0:T(8,128)(2,1)} %param.20) | copy-start | bytes 196612
  0.0 2.6 %copy-start.7 = (s32[256]{0:T(256)S(1)}, s32[256]{0:T(256)}, u32[]{:S(2)}) copy-start(s32[256]{0:T(256)} %param.15) | copy-start | bytes 3076
  0.0 32.6 %collective-permute-start.2 = (bf16[256,2048]{1,0:T(8,128)(2,1)}, bf16[256,2048]{1,0:T(8,128)(2,1)S(1)}, u32[]{:S(2)}, u32[]{:S(2)}) collective-permute-start(bf16[256,2048]{1,0:T(8,128)(2,1)} %w_own.1), channel_id=1, source_target_pairs={{0,12},{1,13},{2,14},{3,15},{4,8},{5,9},{6,10},{7,11},{8,4},{9,5},... | collective-permute-start | bytes 3145736 | tf_op jit(solution)/shard_map/ppermute | solution.py:453
  2.6 3.0 %collective-permute-start = (s32[2,128]{1,0:T(2,128)S(1)}, s32[2,128]{1,0:T(2,128)S(1)}, u32[]{:S(2)}, u32[]{:S(2)}) collective-permute-start(s32[2,128]{1,0:T(2,128)S(1)} %bitcast.7), channel_id=1, source_target_pairs={{0,16},{16,0},{32,48},{48,32},{64,80},{80,64},{96,112},{112,96},{1... | collective-permute-start | bytes 3080 | tf_op jit(solution)/shard_map/ppermute | solution.py:457
  4.5 0.8 %copy-start.10 = (bf16[4,256]{1,0:T(4,128)(2,1)S(1)}, bf16[4,256]{1,0:T(4,128)(2,1)}, u32[]{:S(2)}) copy-start(bf16[4,256]{1,0:T(4,128)(2,1)} %param.25) | copy-start | bytes 6148
  5.4 0.9 %copy-start.12 = (f32[4]{0:T(128)S(1)}, f32[4]{0:T(128)}, u32[]{:S(2)}) copy-start(f32[4]{0:T(128)} %param.24) | copy-start | bytes 52
  5.4 20.4 %copy-start.2 = (bf16[2048,256]{1,0:T(8,128)(2,1)S(1)}, bf16[2048,256]{1,0:T(8,128)(2,1)}, u32[]{:S(2)}) copy-start(bf16[2048,256]{1,0:T(8,128)(2,1)} %w_x.1) | copy-start | bytes 3145732
  5.4 20.4 %copy-start.3 = (bf16[2048,256]{1,0:T(8,128)(2,1)S(1)}, bf16[2048,256]{1,0:T(8,128)(2,1)}, u32[]{:S(2)}) copy-start(bf16[2048,256]{1,0:T(8,128)(2,1)} %w_z.1) | copy-start | bytes 3145732
  6.4 19.3 %copy-start.13 = (f32[4]{0:T(128)S(1)}, f32[4]{0:T(128)}, u32[]{:S(2)}) copy-start(f32[4]{0:T(128)} %param.23) | copy-start | bytes 52
  6.4 19.3 %copy-start.14 = (f32[4]{0:T(128)S(1)}, f32[4]{0:T(128)}, u32[]{:S(2)}) copy-start(f32[4]{0:T(128)} %param.22) | copy-start | bytes 52
  6.4 19.3 %copy-start.11 = (f32[256]{0:T(256)S(1)}, f32[256]{0:T(256)}, u32[]{:S(2)}) copy-start(f32[256]{0:T(256)} %param.27) | copy-start | bytes 3076
  6.4 19.4 %copy-start.1 = (bf16[5,2048]{1,0:T(8,128)(2,1)S(1)}, bf16[5,2048]{1,0:T(8,128)(2,1)}, u32[]{:S(2)}) copy-start(bf16[5,2048]{1,0:T(8,128)(2,1)} %embed) | copy-start | bytes 61444
  6.4 34.9 %all-to-all-start = ((bf16[16,16,128]{2,1,0:T(8,128)(2,1)}), bf16[16,16,128]{2,1,0:T(8,128)(2,1)S(1)}, u32[]{:S(2)}, u32[]{:S(2)}) async-start(bf16[16,16,128]{2,1,0:T(8,128)(2,1)} %shard_map.145), calls=%async_computation | async-start | bytes 131072 | tf_op jit(solution)/shard_map/all_to_all | solution.py:461
  25.7 0.7 copy-start.5
  26.4 6.2 %copy-start.6 = (bf16[4,256]{1,0:T(4,128)(2,1)S(1)}, bf16[4,256]{1,0:T(4,128)(2,1)}, u32[]{:S(2)}) copy-start(bf16[4,256]{1,0:T(4,128)(2,1)} %conv_bc.1) | copy-start | bytes 6148
  26.4 6.2 %copy-start.8 = (s32[5]{0:T(128)S(1)}, s32[5]{0:T(128)}, u32[]{:S(2)}) copy-start(s32[5]{0:T(128)} %complement.1) | copy-start | bytes 64
  26.4 6.3 %copy-start.9 = (bf16[64,1024]{1,0:T(8,128)(2,1)S(1)}, bf16[64,1024]{1,0:T(8,128)(2,1)}, u32[]{:S(2)}) copy-start(bf16[64,1024]{1,0:T(8,128)(2,1)} %constant.14.clone.grams_in) | copy-start | bytes 393220
  26.8 5.8 %collective-permute-start.1 = (f32[32,256]{1,0:T(8,128)S(1)}, f32[32,256]{1,0:T(8,128)S(1)}, u32[]{:S(2)}, u32[]{:S(2)}) collective-permute-start(f32[32,256]{1,0:T(8,128)S(1)} %shard_map.146.mine), channel_id=1, source_target_pairs={{0,12},{1,13},{2,14},{3,15},{4,8},{5,9},{6,10},{7,11},{8,4},{9,5},... | collective-permute-start | bytes 98312 | tf_op jit(solution)/shard_map/ppermute | solution.py:453
  41.4 14.8 %copy-start.4 = (bf16[256,2048]{1,0:T(8,128)(2,1)S(1)}, bf16[256,2048]{1,0:T(8,128)(2,1)}, u32[]{:S(2)}) copy-start(bf16[256,2048]{1,0:T(8,128)(2,1)} %w_own.1) | copy-start | bytes 3145732
